TPU v7x, 32 devices: a whole 2x2x4 slice. The times are simulated.
32 devices in a mesh: dp: 16 (over z, x, core), tensor: 2 (over y).
Axes of the slice: x: 2, y: 2, z: 4, core: 2. Of those that a mesh axis runs over, the one named last changes fastest.
Arguments:
- inputs: bfloat16 [8192, 2560], P(('dp', 'tensor')), may hold values from -1.5 to 1.5
- cotangent: bfloat16 [8192, 2560], P(('dp', 'tensor')), may hold values from -6 to 6
- segment_ids: int32 [8192], P('dp'), may hold values from 0 to 510, as said below
- gains: float32 [6144], P(('dp', 'tensor')), may hold values from 0.5 to 1.5
- gains_first: float32 [6144], P(('dp', 'tensor'))
- gains_second: float32 [6144], P(('dp', 'tensor')), as said below
- query_down: float32 [2560, 768], P(('dp', 'tensor')), may hold values from -0.125 to 0.125
- query_down_first: float32 [2560, 768], P(('dp', 'tensor'))
- query_down_second: float32 [2560, 768], P(('dp', 'tensor')), as said below
- latent_down: float32 [2560, 288], P(('dp', 'tensor')), may hold values from -0.125 to 0.125
- latent_down_first: float32 [2560, 288], P(('dp', 'tensor'))
- latent_down_second: float32 [2560, 288], P(('dp', 'tensor')), as said below
- query_up: float32 [768, 3840], P('dp', 'tensor'), may hold values from -0.21875 to 0.21875
- query_up_first: float32 [768, 3840], P('dp', 'tensor')
- query_up_second: float32 [768, 3840], P('dp', 'tensor'), as said below
- latent_up: float32 [256, 5120], P('dp', 'tensor'), may hold values from -0.375 to 0.375
- latent_up_first: float32 [256, 5120], P('dp', 'tensor')
- latent_up_second: float32 [256, 5120], P('dp', 'tensor'), as said below
- output_proj: float32 [2560, 2560], P(('tensor', 'dp')), may hold values from -1 to 1
- output_proj_first: float32 [2560, 2560], P(('tensor', 'dp'))
- output_proj_second: float32 [2560, 2560], P(('tensor', 'dp')), as said below
- gate_proj: float32 [2560, 6400], P('dp', 'tensor'), may hold values from -0.125 to 0.125
- gate_proj_first: float32 [2560, 6400], P('dp', 'tensor')
- gate_proj_second: float32 [2560, 6400], P('dp', 'tensor'), as said below
- up_proj: float32 [2560, 6400], P('dp', 'tensor'), may hold values from -0.125 to 0.125
- up_proj_first: float32 [2560, 6400], P('dp', 'tensor')
- up_proj_second: float32 [2560, 6400], P('dp', 'tensor'), as said below
- down_proj: float32 [6400, 2560], P(('tensor', 'dp')), may hold values from -0.21875 to 0.21875
- down_proj_first: float32 [6400, 2560], P(('tensor', 'dp'))
- down_proj_second: float32 [6400, 2560], P(('tensor', 'dp')), as said below
Outputs:
- block_output: bfloat16 [8192, 2560], P(('dp', 'tensor'))
- input_grad: bfloat16 [8192, 2560], P(('dp', 'tensor'))
- gains_new: float32 [6144], P(('dp', 'tensor'))
- gains_first_new: float32 [6144], P(('dp', 'tensor'))
- gains_second_new: float32 [6144], P(('dp', 'tensor'))
- query_down_new: float32 [2560, 768], P(('dp', 'tensor'))
- query_down_first_new: float32 [2560, 768], P(('dp', 'tensor'))
- query_down_second_new: float32 [2560, 768], P(('dp', 'tensor'))
- latent_down_new: float32 [2560, 288], P(('dp', 'tensor'))
- latent_down_first_new: float32 [2560, 288], P(('dp', 'tensor'))
- latent_down_second_new: float32 [2560, 288], P(('dp', 'tensor'))
- query_up_new: float32 [768, 3840], P('dp', 'tensor')
- query_up_first_new: float32 [768, 3840], P('dp', 'tensor')
- query_up_second_new: float32 [768, 3840], P('dp', 'tensor')
- latent_up_new: float32 [256, 5120], P('dp', 'tensor')
- latent_up_first_new: float32 [256, 5120], P('dp', 'tensor')
- latent_up_second_new: float32 [256, 5120], P('dp', 'tensor')
- output_proj_new: float32 [2560, 2560], P(('tensor', 'dp'))
- output_proj_first_new: float32 [2560, 2560], P(('tensor', 'dp'))
- output_proj_second_new: float32 [2560, 2560], P(('tensor', 'dp'))
- gate_proj_new: float32 [2560, 6400], P('dp', 'tensor')
- gate_proj_first_new: float32 [2560, 6400], P('dp', 'tensor')
- gate_proj_second_new: float32 [2560, 6400], P('dp', 'tensor')
- up_proj_new: float32 [2560, 6400], P('dp', 'tensor')
- up_proj_first_new: float32 [2560, 6400], P('dp', 'tensor')
- up_proj_second_new: float32 [2560, 6400], P('dp', 'tensor')
- down_proj_new: float32 [6400, 2560], P(('tensor', 'dp'))
- down_proj_first_new: float32 [6400, 2560], P(('tensor', 'dp'))
- down_proj_second_new: float32 [6400, 2560], P(('tensor', 'dp'))
Inputs may be any that keep to these rules, and one draw needn't show every extreme that they name: `segment_ids`: within each pack of 512 consecutive tokens the ids count documents from 0 upward, start at 0 and never fall; the tokens at indices 512 // 2 - 1 and 256 of a pack have the same id; some pack reaches the largest id. `gains_second`: positive. `query_down_second`: positive. `latent_down_second`: positive. `query_up_second`: positive. `latent_up_second`: positive. `output_proj_second`: positive. `gate_proj_second`: positive. `up_proj_second`: positive. `down_proj_second`: positive.
All inputs are finite; a program needn't handle non-finite values.
Results may differ from a plain program's by a relative error of at most 0.02.
Values may be sent and summed in bfloat16 or wider, within the bound.
A program may use at most 248 MiB of HBM per device.

v0:
```python
import math

import jax
import jax.numpy as jnp
from jax import lax
from jax.sharding import PartitionSpec as P

D = 2560
H = 40
DN = 64
DR = 32
DV = 64
QR = 768
KVR = 256
FF = 6400
STEP = 10
QH = 96
KH = 128


RESIDUAL = 1.4 / math.sqrt(62.0)
NORM_EPSILON = 1e-05
MOMENT_DECAY = 0.9
SQUARE_DECAY = 0.95
ADAM_EPSILON = 1e-08
WEIGHT_DECAY = 0.1
GAIN_RATE = 0.3
ROPE_BASE = 10000.0
MASKED = -1e30


def right_transposed(left_side, right_side):
    return lax.dot_general(
        left_side, right_side, (((1,), (1,)), ((), ())), preferred_element_type=jnp.float32
    )


def left_transposed(left_side, right_side):
    return lax.dot_general(
        left_side, right_side, (((0,), (0,)), ((), ())), preferred_element_type=jnp.float32
    )


def gather_tokens(local_rows):
    return lax.all_gather(local_rows, "tensor", axis=0, tiled=True)


def sum_tokens(term, local_count):
    return lax.psum_scatter(
        term(jnp.int32(0), lax.axis_size("tensor") * local_count).astype(jnp.bfloat16),
        "tensor",
        scatter_dimension=0,
        tiled=True,
    ).astype(jnp.float32)


def norm_forward(values, gain_values):
    inverse = lax.rsqrt(jnp.mean(values * values, axis=-1, keepdims=True) + NORM_EPSILON)
    return (values * inverse * gain_values, inverse)


def norm_backward(values, inverse, gain_values, grad_out):
    unit_values = values * inverse
    weighted = grad_out * gain_values
    grad_values = inverse * (
        weighted - unit_values * jnp.mean(weighted * unit_values, axis=-1, keepdims=True)
    )
    return (grad_values, jnp.sum(grad_out * unit_values, axis=0))


def rotate(values, rope_cosine, rope_sine):
    half_width = values.shape[-1] // 2
    first_half = values[..., :half_width]
    second_half = values[..., half_width:]
    return jnp.concatenate(
        [
            first_half * rope_cosine - second_half * rope_sine,
            second_half * rope_cosine + first_half * rope_sine,
        ],
        axis=-1,
    )


def unrotate(grads_in, rope_cosine, rope_sine):
    half_width = grads_in.shape[-1] // 2
    first_half = grads_in[..., :half_width]
    second_half = grads_in[..., half_width:]
    return jnp.concatenate(
        [
            first_half * rope_cosine + second_half * rope_sine,
            second_half * rope_cosine - first_half * rope_sine,
        ],
        axis=-1,
    )


def rope_tables(segment_ids):
    token_index = jnp.arange(segment_ids.shape[0], dtype=jnp.int32)
    doc_start = jnp.concatenate(
        [jnp.ones((1,), dtype=jnp.bool_), segment_ids[1:] != segment_ids[:-1]]
    )
    starts = lax.cummax(jnp.where(doc_start, token_index, 0), axis=0)
    position = (token_index - starts).astype(jnp.float32)
    exponent = jnp.arange(DR // 2, dtype=jnp.float32) * (2.0 / DR)
    rope_angle = position[:, None] * (ROPE_BASE ** (-exponent))[None, :]
    return (jnp.cos(rope_angle), jnp.sin(rope_angle))


def block_scores(rows_query, key_heads, segment_ids, row_start, score_scale):
    block_rows = rows_query.shape[0]
    row_index = row_start + jnp.arange(block_rows, dtype=jnp.int32)
    column_index = jnp.arange(segment_ids.shape[0], dtype=jnp.int32)
    allowed = (segment_ids[:, None] == segment_ids[None, :]) & (
        column_index[None, :] <= row_index[:, None]
    )
    scores = (
        jnp.einsum("ihd,jhd->hij", rows_query, key_heads, preferred_element_type=jnp.float32)
        * score_scale
    )
    return jnp.where(allowed[None], scores, MASKED)


def adamw_update(weight, first_moment, second_moment, gradient, step_rate):
    new_first = MOMENT_DECAY * first_moment + (1.0 - MOMENT_DECAY) * gradient
    new_second = SQUARE_DECAY * second_moment + (1.0 - SQUARE_DECAY) * gradient * gradient
    first_hat = new_first / (1.0 - MOMENT_DECAY**STEP)
    second_hat = new_second / (1.0 - SQUARE_DECAY**STEP)
    new_weight = weight - step_rate * (
        first_hat / (jnp.sqrt(second_hat) + ADAM_EPSILON) + WEIGHT_DECAY * weight
    )
    return (new_weight, new_first, new_second)


def matrix_rate(fan_in):
    return 2.0 / math.sqrt(fan_in)


def local(
    inputs,
    cotangent,
    segment_ids,
    gains,
    gains_first,
    gains_second,
    query_down,
    query_down_first,
    query_down_second,
    latent_down,
    latent_down_first,
    latent_down_second,
    query_up,
    query_up_first,
    query_up_second,
    latent_up,
    latent_up_first,
    latent_up_second,
    output_proj,
    output_proj_first,
    output_proj_second,
    gate_proj,
    gate_proj_first,
    gate_proj_second,
    up_proj,
    up_proj_first,
    up_proj_second,
    down_proj,
    down_proj_first,
    down_proj_second,
):
    half_rows = inputs.shape[0]
    pack_rows = segment_ids.shape[0]
    local_heads = query_up.shape[1] // QH
    block_rows = min(pack_rows, 512)
    score_scale = QH ** (-0.5)
    query_down_all, latent_down_all, gains_all = (
        lax.all_gather(query_down.astype(jnp.bfloat16), ("dp", "tensor"), axis=0, tiled=True),
        lax.all_gather(latent_down.astype(jnp.bfloat16), ("dp", "tensor"), axis=0, tiled=True),
        lax.all_gather(gains.astype(jnp.bfloat16), ("dp", "tensor"), axis=0, tiled=True),
    )
    gain_values = gains_all.astype(jnp.float32)
    gain_attention = gain_values[:D]
    gain_query = gain_values[D : D + QR]
    gain_latent = gain_values[D + QR : D + QR + KVR]
    gain_ffn = gain_values[D + QR + KVR :]
    query_up_all, latent_up_all, output_all = (
        lax.all_gather(query_up.astype(jnp.bfloat16), "dp", axis=0, tiled=True),
        lax.all_gather(latent_up.astype(jnp.bfloat16), "dp", axis=0, tiled=True),
        lax.all_gather(output_proj.astype(jnp.bfloat16), "dp", axis=0, tiled=True),
    )
    incoming = inputs.astype(jnp.float32)
    attn_unit, inverse_attention = norm_forward(incoming, gain_attention)
    normed_attn = gather_tokens(attn_unit.astype(jnp.bfloat16))
    query_latent = jnp.dot(normed_attn, query_down_all, preferred_element_type=jnp.float32)
    query_unit, inverse_query = norm_forward(query_latent, gain_query)
    query_normed = query_unit.astype(jnp.bfloat16)
    latent = jnp.dot(normed_attn, latent_down_all, preferred_element_type=jnp.float32)
    latent_unit, inverse_latent = norm_forward(latent[:, :KVR], gain_latent)
    latent_normed = latent_unit.astype(jnp.bfloat16)
    rope_cosine, rope_sine = rope_tables(segment_ids)
    head_cosine = rope_cosine[:, None, :]
    head_sine = rope_sine[:, None, :]
    query_heads = jnp.dot(query_normed, query_up_all, preferred_element_type=jnp.float32).reshape(
        pack_rows, local_heads, QH
    )
    queries = jnp.concatenate(
        [query_heads[..., :DN], rotate(query_heads[..., DN:], head_cosine, head_sine)], axis=-1
    ).astype(jnp.bfloat16)
    latent_heads = (
        jnp.dot(latent_normed, latent_up_all, preferred_element_type=jnp.float32)
        .reshape(pack_rows, local_heads, KH)
        .astype(jnp.bfloat16)
    )
    head_values = latent_heads[..., DN:]
    rope_key = rotate(latent[:, KVR:], rope_cosine, rope_sine).astype(jnp.bfloat16)
    key_heads = jnp.concatenate(
        [
            latent_heads[..., :DN],
            jnp.broadcast_to(rope_key[:, None, :], (pack_rows, local_heads, DR)),
        ],
        axis=-1,
    )
    starts = jnp.arange(pack_rows // block_rows, dtype=jnp.int32) * block_rows

    def forward_block(row_start):
        scores = block_scores(queries, key_heads, segment_ids, row_start, score_scale)
        row_top = jnp.max(scores, axis=-1, keepdims=True)
        exponent_rows = jnp.exp(scores - row_top)
        row_total = jnp.sum(exponent_rows, axis=-1, keepdims=True)
        prob_low = (exponent_rows / row_total).astype(jnp.bfloat16)
        mixed_rows = jnp.einsum(
            "hij,jhd->ihd", prob_low, head_values, preferred_element_type=jnp.float32
        )
        return (mixed_rows.astype(jnp.bfloat16), (row_top + jnp.log(row_total))[..., 0])

    mixed_blocks, log_totals = lax.map(forward_block, starts)
    mixed_heads = mixed_blocks.reshape(pack_rows, local_heads * DV)

    def attention_term(row_start, row_count):
        return jnp.dot(mixed_heads, output_all, preferred_element_type=jnp.float32)

    residual = incoming + RESIDUAL * sum_tokens(attention_term, half_rows)
    ffn_unit, inverse_ffn = norm_forward(residual, gain_ffn)
    normed_ffn = gather_tokens(ffn_unit.astype(jnp.bfloat16))
    gate_all, up_all, down_all = (
        lax.all_gather(gate_proj.astype(jnp.bfloat16), "dp", axis=0, tiled=True),
        lax.all_gather(up_proj.astype(jnp.bfloat16), "dp", axis=0, tiled=True),
        lax.all_gather(down_proj.astype(jnp.bfloat16), "dp", axis=0, tiled=True),
    )
    gate_value = jnp.dot(normed_ffn, gate_all, preferred_element_type=jnp.float32)
    up_value = jnp.dot(normed_ffn, up_all, preferred_element_type=jnp.float32)
    gate_sigmoid = lax.logistic(gate_value)
    silu_gate = gate_value * gate_sigmoid
    hidden = (silu_gate * up_value).astype(jnp.bfloat16)

    def ffn_term(row_start, row_count):
        return jnp.dot(hidden, down_all, preferred_element_type=jnp.float32)

    block_output = (residual + RESIDUAL * sum_tokens(ffn_term, half_rows)).astype(jnp.bfloat16)
    outer_grad = cotangent.astype(jnp.float32)
    gate_back, up_back, down_back = (
        lax.all_gather(gate_proj.astype(jnp.bfloat16), "dp", axis=0, tiled=True),
        lax.all_gather(up_proj.astype(jnp.bfloat16), "dp", axis=0, tiled=True),
        lax.all_gather(down_proj.astype(jnp.bfloat16), "dp", axis=0, tiled=True),
    )
    grad_ffn = gather_tokens((RESIDUAL * outer_grad).astype(jnp.bfloat16))
    grad_hidden = right_transposed(grad_ffn, down_back)
    grad_gate = (
        grad_hidden * up_value * gate_sigmoid * (1.0 + gate_value * (1.0 - gate_sigmoid))
    ).astype(jnp.bfloat16)
    grad_up = (grad_hidden * silu_gate).astype(jnp.bfloat16)

    def ffn_back_term(row_start, row_count):
        return right_transposed(grad_gate, gate_back) + right_transposed(grad_up, up_back)

    grad_normed_ffn = sum_tokens(ffn_back_term, half_rows)
    grad_incoming_ffn, gain_ffn_grad = norm_backward(
        residual, inverse_ffn, gain_ffn, grad_normed_ffn
    )
    grad_residual = outer_grad + grad_incoming_ffn
    down_grad = left_transposed(hidden, grad_ffn)
    gate_grad = left_transposed(normed_ffn, grad_gate)
    up_grad = left_transposed(normed_ffn, grad_up)
    gate_shard, up_shard, down_shard = (
        lax.psum_scatter(gate_grad, "dp", scatter_dimension=0, tiled=True),
        lax.psum_scatter(up_grad, "dp", scatter_dimension=0, tiled=True),
        lax.psum_scatter(down_grad, "dp", scatter_dimension=0, tiled=True),
    )
    query_up_back, latent_up_back, output_back = (
        lax.all_gather(query_up.astype(jnp.bfloat16), "dp", axis=0, tiled=True),
        lax.all_gather(latent_up.astype(jnp.bfloat16), "dp", axis=0, tiled=True),
        lax.all_gather(output_proj.astype(jnp.bfloat16), "dp", axis=0, tiled=True),
    )
    grad_branch = gather_tokens((RESIDUAL * grad_residual).astype(jnp.bfloat16))
    output_grad = left_transposed(mixed_heads, grad_branch)
    grad_mixed = right_transposed(grad_branch, output_back).astype(jnp.bfloat16)
    grad_mixed_blocks = grad_mixed.reshape(pack_rows // block_rows, block_rows, local_heads, DV)

    def backward_block(totals_carry, block_item):
        row_start, rows_total, rows_grad = block_item
        grad_key_heads, grad_values = totals_carry
        scores = block_scores(queries, key_heads, segment_ids, row_start, score_scale)
        probs = jnp.exp(scores - rows_total[..., None])
        grad_values = grad_values + jnp.einsum(
            "hij,ihd->jhd",
            probs.astype(jnp.bfloat16),
            rows_grad,
            preferred_element_type=jnp.float32,
        )
        grad_probs = jnp.einsum(
            "ihd,jhd->hij", rows_grad, head_values, preferred_element_type=jnp.float32
        )
        row_inner = jnp.sum(probs * grad_probs, axis=-1, keepdims=True)
        grad_scores = (probs * (grad_probs - row_inner)).astype(jnp.bfloat16)
        grad_rows = (
            jnp.einsum("hij,jhd->ihd", grad_scores, key_heads, preferred_element_type=jnp.float32)
            * score_scale
        )
        grad_key_heads = (
            grad_key_heads
            + jnp.einsum("hij,ihd->jhd", grad_scores, queries, preferred_element_type=jnp.float32)
            * score_scale
        )
        return ((grad_key_heads, grad_values), grad_rows)

    empty_keys = jnp.zeros((pack_rows, local_heads, QH), jnp.float32)
    empty_values = jnp.zeros((pack_rows, local_heads, DV), jnp.float32)
    (grad_key_heads, grad_values), grad_query_blocks = lax.scan(
        backward_block, (empty_keys, empty_values), (starts, log_totals, grad_mixed_blocks)
    )
    grad_queries = grad_query_blocks.reshape(pack_rows, local_heads, QH)
    grad_query_heads = (
        jnp.concatenate(
            [grad_queries[..., :DN], unrotate(grad_queries[..., DN:], head_cosine, head_sine)],
            axis=-1,
        )
        .astype(jnp.bfloat16)
        .reshape(pack_rows, local_heads * QH)
    )
    grad_latent_heads = (
        jnp.concatenate([grad_key_heads[..., :DN], grad_values], axis=-1)
        .astype(jnp.bfloat16)
        .reshape(pack_rows, local_heads * KH)
    )
    grad_rope = unrotate(jnp.sum(grad_key_heads[..., DN:], axis=1), rope_cosine, rope_sine)
    query_up_grad = left_transposed(query_normed, grad_query_heads)
    latent_up_grad = left_transposed(latent_normed, grad_latent_heads)
    grad_query_unit = right_transposed(grad_query_heads, query_up_back)
    grad_latent_unit = right_transposed(grad_latent_heads, latent_up_back)
    grad_query_wide, gain_query_grad = norm_backward(
        query_latent, inverse_query, gain_query, grad_query_unit
    )
    grad_latent_part, gain_latent_grad = norm_backward(
        latent[:, :KVR], inverse_latent, gain_latent, grad_latent_unit
    )
    grad_query_latent = grad_query_wide.astype(jnp.bfloat16)
    grad_latent = jnp.concatenate([grad_latent_part, grad_rope], axis=-1).astype(jnp.bfloat16)
    query_down_grad = left_transposed(normed_attn, grad_query_latent)
    latent_down_grad = left_transposed(normed_attn, grad_latent)

    def attention_back_term(row_start, row_count):
        return right_transposed(grad_query_latent, query_down_all) + right_transposed(
            grad_latent, latent_down_all
        )

    grad_normed_attn = sum_tokens(attention_back_term, half_rows)
    grad_incoming_attn, gain_attention_grad = norm_backward(
        incoming, inverse_attention, gain_attention, grad_normed_attn
    )
    input_grad = (grad_residual + grad_incoming_attn).astype(jnp.bfloat16)
    query_up_shard, latent_up_shard, output_shard = (
        lax.psum_scatter(query_up_grad, "dp", scatter_dimension=0, tiled=True),
        lax.psum_scatter(latent_up_grad, "dp", scatter_dimension=0, tiled=True),
        lax.psum_scatter(output_grad, "dp", scatter_dimension=0, tiled=True),
    )
    gains_grad = jnp.concatenate(
        [gain_attention_grad, gain_query_grad, gain_latent_grad, gain_ffn_grad]
    )
    query_down_shard, latent_down_shard, gains_shard = (
        lax.psum_scatter(query_down_grad, ("dp", "tensor"), scatter_dimension=0, tiled=True),
        lax.psum_scatter(latent_down_grad, ("dp", "tensor"), scatter_dimension=0, tiled=True),
        lax.psum_scatter(gains_grad, ("dp", "tensor"), scatter_dimension=0, tiled=True),
    )
    gains_out = adamw_update(gains, gains_first, gains_second, gains_shard, GAIN_RATE)
    query_down_out = adamw_update(
        query_down, query_down_first, query_down_second, query_down_shard, matrix_rate(D)
    )
    latent_down_out = adamw_update(
        latent_down, latent_down_first, latent_down_second, latent_down_shard, matrix_rate(D)
    )
    query_up_out = adamw_update(
        query_up, query_up_first, query_up_second, query_up_shard, matrix_rate(QR)
    )
    latent_up_out = adamw_update(
        latent_up, latent_up_first, latent_up_second, latent_up_shard, matrix_rate(KVR)
    )
    output_out = adamw_update(
        output_proj, output_proj_first, output_proj_second, output_shard, matrix_rate(H * DV // 64)
    )
    gate_out = adamw_update(
        gate_proj, gate_proj_first, gate_proj_second, gate_shard, matrix_rate(D)
    )
    up_out = adamw_update(up_proj, up_proj_first, up_proj_second, up_shard, matrix_rate(D))
    down_out = adamw_update(
        down_proj, down_proj_first, down_proj_second, down_shard, matrix_rate(FF // 8)
    )
    return (
        block_output,
        input_grad,
        gains_out[0],
        gains_out[1],
        gains_out[2],
        query_down_out[0],
        query_down_out[1],
        query_down_out[2],
        latent_down_out[0],
        latent_down_out[1],
        latent_down_out[2],
        query_up_out[0],
        query_up_out[1],
        query_up_out[2],
        latent_up_out[0],
        latent_up_out[1],
        latent_up_out[2],
        output_out[0],
        output_out[1],
        output_out[2],
        gate_out[0],
        gate_out[1],
        gate_out[2],
        up_out[0],
        up_out[1],
        up_out[2],
        down_out[0],
        down_out[1],
        down_out[2],
    )


def solution(mesh):
    in_specs = (
        P(("dp", "tensor"), None),
        P(("dp", "tensor"), None),
        P("dp"),
        P(("dp", "tensor")),
        P(("dp", "tensor")),
        P(("dp", "tensor")),
        P(("dp", "tensor"), None),
        P(("dp", "tensor"), None),
        P(("dp", "tensor"), None),
        P(("dp", "tensor"), None),
        P(("dp", "tensor"), None),
        P(("dp", "tensor"), None),
        P("dp", "tensor"),
        P("dp", "tensor"),
        P("dp", "tensor"),
        P("dp", "tensor"),
        P("dp", "tensor"),
        P("dp", "tensor"),
        P(("tensor", "dp"), None),
        P(("tensor", "dp"), None),
        P(("tensor", "dp"), None),
        P("dp", "tensor"),
        P("dp", "tensor"),
        P("dp", "tensor"),
        P("dp", "tensor"),
        P("dp", "tensor"),
        P("dp", "tensor"),
        P(("tensor", "dp"), None),
        P(("tensor", "dp"), None),
        P(("tensor", "dp"), None),
    )
    out_specs = (
        P(("dp", "tensor"), None),
        P(("dp", "tensor"), None),
        P(("dp", "tensor")),
        P(("dp", "tensor")),
        P(("dp", "tensor")),
        P(("dp", "tensor"), None),
        P(("dp", "tensor"), None),
        P(("dp", "tensor"), None),
        P(("dp", "tensor"), None),
        P(("dp", "tensor"), None),
        P(("dp", "tensor"), None),
        P("dp", "tensor"),
        P("dp", "tensor"),
        P("dp", "tensor"),
        P("dp", "tensor"),
        P("dp", "tensor"),
        P("dp", "tensor"),
        P(("tensor", "dp"), None),
        P(("tensor", "dp"), None),
        P(("tensor", "dp"), None),
        P("dp", "tensor"),
        P("dp", "tensor"),
        P("dp", "tensor"),
        P("dp", "tensor"),
        P("dp", "tensor"),
        P("dp", "tensor"),
        P(("tensor", "dp"), None),
        P(("tensor", "dp"), None),
        P(("tensor", "dp"), None),
    )
    return jax.shard_map(local, mesh=mesh, in_specs=in_specs, out_specs=out_specs, check_vma=False)
```

profile of v0, /device:TPU:0, one launch (start us, length us, event | category | flops | bytes accessed | tf_op | source)
XLA Modules:
  0.0 2685.1 jit_solution(1336760281249693487)
XLA Ops:
  8.1 42.2 %all-reduce = bf16[6144]{0:T(1024)(128)(2,1)S(1)} all-reduce(bf16[6144]{0:T(1024)(128)(2,1)S(1)} %dynamic-update-slice), channel_id=1, replica_groups=mesh['dp'=16,'tensor'=2] {'dp','tensor'}, use_global_device_ids=true, to_apply=%add | all-reduce | flops 6144 | bytes 24576
  61.2 33.3 %all-gather.13.cloned.1.call-done = bf16[512,2560]{1,0:T(8,128)(2,1)} async-done(((bf16[256,2560]{1,0:T(8,128)(2,1)}), bf16[512,2560]{1,0:T(8,128)(2,1)}) %all-gather.13.cloned.1.call-update) | async-done | bytes 2621456 | tf_op jit(solution)/shard_map/all_gather | solution.py:45
  94.5 59.7 %all-gather.15.cloned.1.call-done = bf16[2560,288]{1,0:T(8,128)(2,1)} async-done(((bf16[80,288]{1,0:T(8,128)(2,1)}), bf16[2560,288]{1,0:T(8,128)(2,1)}) %all-gather.15.cloned.1.call-update) | async-done | bytes 1474576 | tf_op jit(solution)/shard_map/all_gather | solution.py:177
  157.7 37.1 %all-gather.17.cloned.1.call-done = bf16[256,2560]{1,0:T(8,128)(2,1)} async-done(((bf16[16,2560]{1,0:T(8,128)(2,1)}), bf16[256,2560]{1,0:T(8,128)(2,1)}) %all-gather.17.cloned.1.call-update) | async-done | bytes 1310736 | tf_op jit(solution)/shard_map/all_gather | solution.py:187
  202.8 55.5 %all-gather.19.cloned.1.call-done = bf16[2560,768]{1,0:T(8,128)(2,1)} async-done(((bf16[80,768]{1,0:T(8,128)(2,1)}), bf16[2560,768]{1,0:T(8,128)(2,1)}) %all-gather.19.cloned.1.call-update) | async-done | bytes 3932176 | tf_op jit(solution)/shard_map/all_gather | solution.py:176
  263.8 40.7 %all-gather.21.cloned.1.call-done = bf16[768,1920]{1,0:T(8,128)(2,1)} async-done(((bf16[48,1920]{1,0:T(8,128)(2,1)}), bf16[768,1920]{1,0:T(8,128)(2,1)}) %all-gather.21.cloned.1.call-update) | async-done | bytes 2949136 | tf_op jit(solution)/shard_map/all_gather | solution.py:186
  331.6 37.3 %all-gather.23.cloned.1.call-done = bf16[1280,2560]{1,0:T(8,128)(2,1)} async-done(((bf16[80,2560]{1,0:T(8,128)(2,1)}), bf16[1280,2560]{1,0:T(8,128)(2,1)}) %all-gather.23.cloned.1.call-update) | async-done | bytes 6553616 | tf_op jit(solution)/shard_map/all_gather | solution.py:188
  377.5 36.0 %reduce-scatter.13.cloned.1.call-done = bf16[256,2560]{1,0:T(8,128)(2,1)} async-done(((bf16[512,2560]{1,0:T(8,128)(2,1)}), bf16[256,2560]{1,0:T(8,128)(2,1)}) %reduce-scatter.13.cloned.1.call-update) | async-done | bytes 1310736 | tf_op jit(solution)/shard_map/reduce_scatter | solution.py:49
  428.4 28.1 %all-gather.25.cloned.1.call-done = bf16[512,2560]{1,0:T(8,128)(2,1)} async-done(((bf16[256,2560]{1,0:T(8,128)(2,1)}), bf16[512,2560]{1,0:T(8,128)(2,1)}) %all-gather.25.cloned.1.call-update) | async-done | bytes 2621456 | tf_op jit(solution)/shard_map/all_gather | solution.py:45
  456.5 127.5 %all-gather.27.cloned.1.call-done = bf16[2560,3200]{1,0:T(8,128)(2,1)} async-done(((bf16[160,3200]{1,0:T(8,128)(2,1)}), bf16[2560,3200]{1,0:T(8,128)(2,1)}) %all-gather.27.cloned.1.call-update) | async-done | bytes 16384016 | tf_op jit(solution)/shard_map/all_gather | solution.py:245
  584.0 15.7 fusion.83
  599.6 109.8 %all-gather.29.cloned.1.call-done = bf16[2560,3200]{1,0:T(8,128)(2,1)} async-done(((bf16[160,3200]{1,0:T(8,128)(2,1)}), bf16[2560,3200]{1,0:T(8,128)(2,1)}) %all-gather.29.cloned.1.call-update) | async-done | bytes 16384016 | tf_op jit(solution)/shard_map/all_gather | solution.py:246
  709.5 15.8 fusion.84
  725.3 23.6 all-gather.33.cloned.1.call-done
  748.9 127.3 %all-gather.31.cloned.1.call-done = bf16[3200,2560]{1,0:T(8,128)(2,1)} async-done(((bf16[200,2560]{1,0:T(8,128)(2,1)}), bf16[3200,2560]{1,0:T(8,128)(2,1)}) %all-gather.31.cloned.1.call-update) | async-done | bytes 16384016 | tf_op jit(solution)/shard_map/all_gather | solution.py:247
  876.3 18.7 multiply_convert_fusion.1
  895.0 16.1 fusion.85
  925.6 35.9 %reduce-scatter.17.cloned.1.call-done = bf16[256,2560]{1,0:T(8,128)(2,1)} async-done(((bf16[512,2560]{1,0:T(8,128)(2,1)}), bf16[256,2560]{1,0:T(8,128)(2,1)}) %reduce-scatter.17.cloned.1.call-update) | async-done | bytes 1310736 | tf_op jit(solution)/shard_map/reduce_scatter | solution.py:49
  967.4 39.1 %all-gather.35.cloned.1.call-done = bf16[512,2560]{1,0:T(8,128)(2,1)} async-done(((bf16[256,2560]{1,0:T(8,128)(2,1)}), bf16[512,2560]{1,0:T(8,128)(2,1)}) %all-gather.35.cloned.1.call-update) | async-done | bytes 2621456 | tf_op jit(solution)/shard_map/all_gather | solution.py:45
  1037.1 19.4 multiply_convert_fusion
  1135.3 17.3 fusion.89
  1152.8 17.2 fusion.90
  1171.8 17.5 fusion.91
  1192.3 49.2 %reduce-scatter.27.cloned.1.call-done = f32[16,2560]{1,0:T(8,128)} async-done(((f32[256,2560]{1,0:T(8,128)}), f32[16,2560]{1,0:T(8,128)}) %reduce-scatter.27.cloned.1.call-update) | async-done | bytes 163856 | tf_op jit(solution)/shard_map/reduce_scatter | solution.py:372
  1243.3 36.9 %reduce-scatter.19.cloned.1.call-done = bf16[256,2560]{1,0:T(8,128)(2,1)} async-done(((bf16[512,2560]{1,0:T(8,128)(2,1)}), bf16[256,2560]{1,0:T(8,128)(2,1)}) %reduce-scatter.19.cloned.1.call-update) | async-done | bytes 1310736 | tf_op jit(solution)/shard_map/reduce_scatter | solution.py:49
  1282.6 40.2 %all-reduce.1 = f32[6144]{0:T(1024)S(1)} all-reduce(f32[6144]{0:T(1024)S(1)} %pad_maximum_fusion.12), channel_id=6, replica_groups=mesh['dp'=16,'tensor'=2] {'dp','tensor'}, use_global_device_ids=true, to_apply=%region_22.23.clone | all-reduce | flops 6144 | bytes 49152
  1328.6 78.6 %reduce-scatter.25.cloned.1.call-done = f32[48,1920]{1,0:T(8,128)} async-done(((f32[768,1920]{1,0:T(8,128)}), f32[48,1920]{1,0:T(8,128)}) %reduce-scatter.25.cloned.1.call-update) | async-done | bytes 368656 | tf_op jit(solution)/shard_map/reduce_scatter | solution.py:371
  1409.6 125.6 %reduce-scatter.21.cloned.1.call-done = f32[80,768]{1,0:T(8,128)} async-done(((f32[2560,768]{1,0:T(8,128)}), f32[80,768]{1,0:T(8,128)}) %reduce-scatter.21.cloned.1.call-update) | async-done | bytes 245776 | tf_op jit(solution)/shard_map/reduce_scatter | solution.py:379
  1537.1 139.9 %reduce-scatter.29.cloned.1.call-done = f32[80,2560]{1,0:T(8,128)} async-done(((f32[1280,2560]{1,0:T(8,128)}), f32[80,2560]{1,0:T(8,128)}) %reduce-scatter.29.cloned.1.call-update) | async-done | bytes 819216 | tf_op jit(solution)/shard_map/reduce_scatter | solution.py:373
  1680.5 328.3 %reduce-scatter.31.cloned.1.call-done = f32[160,3200]{1,0:T(8,128)} async-done(((f32[2560,3200]{1,0:T(8,128)}), f32[160,3200]{1,0:T(8,128)}) %reduce-scatter.31.cloned.1.call-update) | async-done | bytes 2048016 | tf_op jit(solution)/shard_map/reduce_scatter | solution.py:284
  2015.2 324.7 %reduce-scatter.33.cloned.1.call-done = f32[160,3200]{1,0:T(8,128)} async-done(((f32[2560,3200]{1,0:T(8,128)}), f32[160,3200]{1,0:T(8,128)}) %reduce-scatter.33.cloned.1.call-update) | async-done | bytes 2048016 | tf_op jit(solution)/shard_map/reduce_scatter | solution.py:285
  2346.9 324.6 %reduce-scatter.35.cloned.1.call-done = f32[200,2560]{1,0:T(8,128)} async-done(((f32[3200,2560]{1,0:T(8,128)}), f32[200,2560]{1,0:T(8,128)}) %reduce-scatter.35.cloned.1.call-update) | async-done | bytes 2048016 | tf_op jit(solution)/shard_map/reduce_scatter | solution.py:286
  (307 shorter events, 250.6 us)
Async XLA Ops:
  7.2 87.3 %all-gather.13.cloned.1.call-start = ((), (), s32[]{:S(2)}) async-start(), calls=%async_computation.12 | async-start | bytes 3932160 | tf_op jit(solution)/shard_map/all_gather | solution.py:45
  50.3 914.6 %copy-start.35 = (f32[2560]{0:T(1024)}, f32[2560]{0:T(1024)S(1)}, u32[]{:S(2)}) copy-start(f32[2560]{0:T(1024)S(1)} %get-tuple-element.129) | copy-start | bytes 30724
  55.5 98.8 %all-gather.15.cloned.1.call-start = ((), (), s32[]{:S(2)}) async-start(), calls=%async_computation.13 | async-start | bytes 2027520 | tf_op jit(solution)/shard_map/all_gather | solution.py:177
  56.3 138.5 %all-gather.17.cloned.1.call-start = ((), (), s32[]{:S(2)}) async-start(), calls=%async_computation.14 | async-start | bytes 1392640 | tf_op jit(solution)/shard_map/all_gather | solution.py:187
  57.0 201.3 %all-gather.19.cloned.1.call-start = ((), (), s32[]{:S(2)}) async-start(), calls=%async_computation.15 | async-start | bytes 4055040 | tf_op jit(solution)/shard_map/all_gather | solution.py:176
  57.7 246.7 %all-gather.21.cloned.1.call-start = ((), (), s32[]{:S(2)}) async-start(), calls=%async_computation.16 | async-start | bytes 3133440 | tf_op jit(solution)/shard_map/all_gather | solution.py:186
  58.5 310.4 %all-gather.23.cloned.1.call-start = ((), (), s32[]{:S(2)}) async-start(), calls=%async_computation.17 | async-start | bytes 6963200 | tf_op jit(solution)/shard_map/all_gather | solution.py:188
  59.4 354.2 %reduce-scatter.13.cloned.1.call-start = ((), (), s32[]{:S(2)}) async-start(), calls=%async_computation.18 | async-start | bytes 3932160 | tf_op jit(solution)/shard_map/reduce_scatter | solution.py:49
  59.5 245.0 %copy-start.51 = (f32[768]{0:T(1024)}, f32[768]{0:T(1024)S(1)}, u32[]{:S(2)}) copy-start(f32[768]{0:T(1024)S(1)} %slice.110) | copy-start | bytes 9220
  377.3 79.2 %all-gather.25.cloned.1.call-start = ((), (), s32[]{:S(2)}) async-start(), calls=%async_computation.19 | async-start | bytes 3932160 | tf_op jit(solution)/shard_map/all_gather | solution.py:45
  415.6 549.3 %copy-start.63 = (f32[256]{0:T(256)}, f32[256]{0:T(256)S(1)}, u32[]{:S(2)}) copy-start(f32[256]{0:T(256)S(1)} %add_rsqrt_fusion.2) | copy-start | bytes 3076
  417.3 166.7 %all-gather.27.cloned.1.call-start = ((), (), s32[]{:S(2)}) async-start(), calls=%async_computation.20 | async-start | bytes 17408000 | tf_op jit(solution)/shard_map/all_gather | solution.py:245
  420.0 289.5 %all-gather.29.cloned.1.call-start = ((), (), s32[]{:S(2)}) async-start(), calls=%async_computation.21 | async-start | bytes 17408000 | tf_op jit(solution)/shard_map/all_gather | solution.py:246
  422.7 326.2 %all-gather.33.cloned.1.call-start = ((), (), s32[]{:S(2)}) async-start(), calls=%async_computation.24 | async-start | bytes 3932160 | tf_op jit(solution)/shard_map/all_gather | solution.py:45
  425.5 450.8 %all-gather.31.cloned.1.call-start = ((), (), s32[]{:S(2)}) async-start(), calls=%async_computation.22 | async-start | bytes 17408000 | tf_op jit(solution)/shard_map/all_gather | solution.py:247
  428.3 533.2 %reduce-scatter.17.cloned.1.call-start = ((), (), s32[]{:S(2)}) async-start(), calls=%async_computation.25 | async-start | bytes 3932160 | tf_op jit(solution)/shard_map/reduce_scatter | solution.py:49
  925.6 80.9 %all-gather.35.cloned.1.call-start = ((), (), s32[]{:S(2)}) async-start(), calls=%async_computation.26 | async-start | bytes 3932160 | tf_op jit(solution)/shard_map/all_gather | solution.py:45
  967.3 222.2 %reduce-scatter.23.cloned.1.call-start = ((), (), s32[]{:S(2)}) async-start(), calls=%async_computation.29 | async-start | bytes 4055040 | tf_op jit(solution)/shard_map/reduce_scatter | solution.py:380
  1070.9 170.6 %reduce-scatter.27.cloned.1.call-start = ((), (), s32[]{:S(2)}) async-start(), calls=%async_computation.31 | async-start | bytes 2785280 | tf_op jit(solution)/shard_map/reduce_scatter | solution.py:372
  1075.1 205.1 %reduce-scatter.19.cloned.1.call-start = ((), (), s32[]{:S(2)}) async-start(), calls=%async_computation.27 | async-start | bytes 3932160 | tf_op jit(solution)/shard_map/reduce_scatter | solution.py:49
  1096.3 227.1 %reduce-scatter.15.cloned.1.call-start = ((), (), s32[]{:S(2)}) async-start(), calls=%async_computation.23 | async-start | bytes 3932160 | tf_op jit(solution)/shard_map/reduce_scatter | solution.py:49
  1111.2 296.0 %reduce-scatter.25.cloned.1.call-start = ((), (), s32[]{:S(2)}) async-start(), calls=%async_computation.30 | async-start | bytes 6266880 | tf_op jit(solution)/shard_map/reduce_scatter | solution.py:371
  1118.3 416.9 %reduce-scatter.21.cloned.1.call-start = ((), (), s32[]{:S(2)}) async-start(), calls=%async_computation.28 | async-start | bytes 8110080 | tf_op jit(solution)/shard_map/reduce_scatter | solution.py:379
  1123.7 553.3 %reduce-scatter.29.cloned.1.call-start = ((), (), s32[]{:S(2)}) async-start(), calls=%async_computation.32 | async-start | bytes 13926400 | tf_op jit(solution)/shard_map/reduce_scatter | solution.py:373
  1133.5 875.2 %reduce-scatter.31.cloned.1.call-start = ((), (), s32[]{:S(2)}) async-start(), calls=%async_computation.33 | async-start | bytes 34816000 | tf_op jit(solution)/shard_map/reduce_scatter | solution.py:284
  1152.6 1187.3 %reduce-scatter.33.cloned.1.call-start = ((), (), s32[]{:S(2)}) async-start(), calls=%async_computation.34 | async-start | bytes 34816000 | tf_op jit(solution)/shard_map/reduce_scatter | solution.py:285
  1170.0 1501.4 %reduce-scatter.35.cloned.1.call-start = ((), (), s32[]{:S(2)}) async-start(), calls=%async_computation.35 | async-start | bytes 34816000 | tf_op jit(solution)/shard_map/reduce_scatter | solution.py:286
  1328.6 206.6 %copy-start.30 = (f32[80,768]{1,0:T(8,128)S(1)}, f32[80,768]{1,0:T(8,128)}, u32[]{:S(2)}) copy-start(f32[80,768]{1,0:T(8,128)} %param.36) | copy-start | bytes 737284
  1328.6 206.6 %copy-start.41 = (f32[80,768]{1,0:T(8,128)S(1)}, f32[80,768]{1,0:T(8,128)}, u32[]{:S(2)}) copy-start(f32[80,768]{1,0:T(8,128)} %param.37) | copy-start | bytes 737284
  1328.6 348.4 %copy-start.19 = (f32[80,2560]{1,0:T(8,128)S(1)}, f32[80,2560]{1,0:T(8,128)}, u32[]{:S(2)}) copy-start(f32[80,2560]{1,0:T(8,128)} %param.48) | copy-start | bytes 2457604
  1537.1 471.6 %copy-start.14 = (f32[160,3200]{1,0:T(8,128)S(1)}, f32[160,3200]{1,0:T(8,128)}, u32[]{:S(2)}) copy-start(f32[160,3200]{1,0:T(8,128)} %param.51) | copy-start | bytes 6144004
  2015.2 656.3 %copy-start.15 = (f32[200,2560]{1,0:T(8,128)S(1)}, f32[200,2560]{1,0:T(8,128)}, u32[]{:S(2)}) copy-start(f32[200,2560]{1,0:T(8,128)} %param.57) | copy-start | bytes 6144004
  (74 other events, 2807.6 us)
Sparse Core Ops, SparseCore 0:
  55.6 38.8 all-gather.12
  98.0 56.2 all-gather.14
  157.1 37.6 all-gather.16
  198.1 60.1 all-gather.18
  260.9 43.4 all-gather.20
  307.1 61.7 all-gather.22
  377.4 36.1 reduce-scatter.12
  417.4 39.0 all-gather.24
  459.6 124.3 all-gather.26
  586.9 122.5 all-gather.28
  711.7 37.1 all-gather.32
  751.9 124.3 all-gather.30
  925.7 35.7 reduce-scatter.16
  967.4 39.0 all-gather.34
  1071.0 103.9 reduce-scatter.22
  1178.6 62.8 reduce-scatter.26
  1243.6 36.5 reduce-scatter.18
  1282.4 38.2 reduce-scatter.14
  1324.6 82.5 reduce-scatter.24
  1413.7 121.5 reduce-scatter.20
  1539.3 137.6 reduce-scatter.28
  1682.0 326.7 reduce-scatter.30
  2013.1 326.6 reduce-scatter.32
  2344.7 326.6 reduce-scatter.34
where the time goes:
time: 2690 us
  waiting for transfers between devices  2200 us (82%)
  matrix products  260 us (10%)
  other arithmetic  97.5 us (4%)
  blocking collectives  82.3 us (3%)
  local copies, waits for them, and re-layouts  27.9 us (1%)
    reduce_scatter x1, waiting for transfers between devices, local(): lax.psum_scatter(gate_grad, 'dp', scatter_dimension=0, tiled=True)  328 us
    reduce_scatter x1, waiting for transfers between devices, local(): lax.psum_scatter(up_grad, 'dp', scatter_dimension=0, tiled=True)  325 us
    reduce_scatter x1, waiting for transfers between devices, local(): lax.psum_scatter(down_grad, 'dp', scatter_dimension=0, tiled=True)  325 us
    reduce_scatter x1, waiting for transfers between devices, local(): lax.psum_scatter(output_grad, 'dp', scatter_dimension=0, tiled=True)  140 us
    all_gather x1, waiting for transfers between devices, local(): lax.all_gather(gate_proj.astype(jnp.bfloat16), 'dp', axis=0, tiled=True)  128 us
    all_gather x1, waiting for transfers between devices, local(): lax.all_gather(down_proj.astype(jnp.bfloat16), 'dp', axis=0, tiled=True)  127 us
    reduce_scatter x1, waiting for transfers between devices, local(): lax.psum_scatter(query_down_grad, ('dp', 'tensor'), scatter_dimension=0,...  126 us
    all_gather x4, waiting for transfers between devices, gather_tokens(): return lax.all_gather(local_rows, 'tensor', axis=0, tiled=True)  124 us
  transfers between devices with their start and end apart: 24, of which 22 were waited for; matrix products, arithmetic and copies ran while one was open for 8% of the time, Pallas kernels for 0%

commit v1 on v0

v1 whole, which is shorter than its diff:
```python
import functools
import math

import jax
import jax.numpy as jnp
from jax import lax
from jax.experimental import pallas as pl
from jax.experimental.pallas import tpu as pltpu
from jax.sharding import PartitionSpec as P

D = 2560
H = 40
DN = 64
DR = 32
DV = 64
QR = 768
KVR = 256
FF = 6400
STEP = 10
QH = 96
KH = 128


RESIDUAL = 1.4 / math.sqrt(62.0)
NORM_EPSILON = 1e-05
MOMENT_DECAY = 0.9
SQUARE_DECAY = 0.95
ADAM_EPSILON = 1e-08
WEIGHT_DECAY = 0.1
GAIN_RATE = 0.3
ROPE_BASE = 10000.0
MASKED = -1e30


def right_transposed(left_side, right_side):
    return lax.dot_general(
        left_side, right_side, (((1,), (1,)), ((), ())), preferred_element_type=jnp.float32
    )


def left_transposed(left_side, right_side):
    return lax.dot_general(
        left_side, right_side, (((0,), (0,)), ((), ())), preferred_element_type=jnp.float32
    )


def norm_forward(values, gain_values):
    inverse = lax.rsqrt(jnp.mean(values * values, axis=-1, keepdims=True) + NORM_EPSILON)
    return (values * inverse * gain_values, inverse)


def norm_backward(values, inverse, gain_values, grad_out):
    unit_values = values * inverse
    weighted = grad_out * gain_values
    grad_values = inverse * (
        weighted - unit_values * jnp.mean(weighted * unit_values, axis=-1, keepdims=True)
    )
    return (grad_values, jnp.sum(grad_out * unit_values, axis=0))


def rotate(values, rope_cosine, rope_sine):
    half_width = values.shape[-1] // 2
    first_half = values[..., :half_width]
    second_half = values[..., half_width:]
    return jnp.concatenate(
        [
            first_half * rope_cosine - second_half * rope_sine,
            second_half * rope_cosine + first_half * rope_sine,
        ],
        axis=-1,
    )


def unrotate(grads_in, rope_cosine, rope_sine):
    half_width = grads_in.shape[-1] // 2
    first_half = grads_in[..., :half_width]
    second_half = grads_in[..., half_width:]
    return jnp.concatenate(
        [
            first_half * rope_cosine + second_half * rope_sine,
            second_half * rope_cosine - first_half * rope_sine,
        ],
        axis=-1,
    )


def adamw_update(weight, first_moment, second_moment, gradient, step_rate):
    new_first = MOMENT_DECAY * first_moment + (1.0 - MOMENT_DECAY) * gradient
    new_second = SQUARE_DECAY * second_moment + (1.0 - SQUARE_DECAY) * gradient * gradient
    first_hat = new_first / (1.0 - MOMENT_DECAY**STEP)
    second_hat = new_second / (1.0 - SQUARE_DECAY**STEP)
    new_weight = weight - step_rate * (
        first_hat / (jnp.sqrt(second_hat) + ADAM_EPSILON) + WEIGHT_DECAY * weight
    )
    return (new_weight, new_first, new_second)


def matrix_rate(fan_in):
    return 2.0 / math.sqrt(fan_in)


PLANE = 4
LINE = 4
LINK = 1e5
MESH = pl.DeviceIdType.MESH
VMEM_LIMIT = 56 * 1024 * 1024
HBM_SPEC = pl.BlockSpec(memory_space=pl.ANY)
VMEM_SPEC = pl.BlockSpec(memory_space=pltpu.VMEM)


class Board:
    def __init__(self, send_sems, recv_sems, local_sems):
        self.sems = (send_sems, recv_sems, local_sems)
        self.remotes = 0
        self.locals = 0
        self.closing = []
        self.d = lax.axis_index("dp")
        self.t = lax.axis_index("tensor")
        self.z = self.d // PLANE
        self.i = self.d % PLANE
        self.middle = (self.z == 1) | (self.z == 2)
        self.known = {
            name: self.work_out(name) for name in NEAR_OCTET + NEAR_PLANE + NEAR_LINE
        }

    def place_xor(self, k):
        i = self.i
        return (i, i + 1 - 2 * (i % 2), i + 2 - 4 * (i // 2), 3 - i)[k]

    def line_xor(self, k):
        z = self.z
        return (z, z + 1 - 2 * (z % 2), z + 2 - 4 * (z // 2), 3 - z)[k]

    def device(self, name):
        return self.known[name]

    def work_out(self, name):
        if name == "y":
            return (self.d, 1 - self.t)
        kind, k = name
        if kind == "plane":
            return (self.z * PLANE + self.place_xor(k), self.t)
        return (self.line_xor(k) * PLANE + self.i, self.t)

    def greet(self, names):
        barrier = pltpu.get_barrier_semaphore()
        known = [name for name in names if name != "transposed"]
        for name in known:
            pl.semaphore_signal(
                barrier, inc=1, device_id=self.device(name), device_id_type=MESH
            )
        if len(known) == len(names):
            pl.semaphore_wait(barrier, len(known))
            return

        @pl.when(self.i != self.z)
        def _():
            pl.semaphore_signal(
                barrier,
                inc=1,
                device_id=(self.i * PLANE + self.z, self.t),
                device_id_type=MESH,
            )
            pl.semaphore_wait(barrier, len(known) + 1)

        @pl.when(self.i == self.z)
        def _():
            pl.semaphore_wait(barrier, len(known))

    def slot(self):
        self.remotes += 1
        return self.remotes - 1

    def make(self, slot, source, target, name):
        return pltpu.make_async_remote_copy(
            src_ref=source,
            dst_ref=target,
            send_sem=self.sems[0].at[slot],
            recv_sem=self.sems[1].at[slot],
            device_id=self.device(name),
            device_id_type=MESH,
        )

    def send(self, source, target, name):
        copy = self.make(self.slot(), source, target, name)
        copy.start()
        self.closing.append(copy.wait_send)
        return copy

    def move(self, source, target, close=True):
        copy = pltpu.make_async_copy(source, target, self.sems[2].at[self.locals])
        self.locals += 1
        copy.start()
        if close:
            self.closing.append(copy.wait)
        return copy


def octet_place(core, x, y, half):
    return ((core * 2 + x) * 2 + y) * 2 + half


def octet_gather_steps(board, own_ref, all_ref, begin=0.0):
    h = own_ref.shape[0] // 2
    unit = 2.2 * math.prod(own_ref.shape) / LINK

    def rows(place, count=1):
        return all_ref.at[pl.ds(place * h, count * h)]

    core, along_x, along_y = ("plane", 1), ("plane", 2), "y"
    first, second = own_ref.at[pl.ds(0, h)], own_ref.at[pl.ds(h, h)]
    first_x = board.send(first, rows(octet_place(0, 1, 0, 0)), along_x)
    second_y = board.send(second, rows(octet_place(0, 0, 1, 1)), along_y)
    first_y = board.send(first, rows(octet_place(0, 0, 1, 0)), along_y)
    second_x = board.send(second, rows(octet_place(0, 1, 0, 1)), along_x)
    arrivals = [board.send(own_ref, rows(octet_place(1, 0, 0, 0), 2), core)]
    board.move(own_ref, rows(0, 2))

    def onward(place, name):
        source = rows(octet_place(*place[0]))
        return board.send(source, rows(octet_place(*place[1])), name)

    yield begin + unit
    first_x.wait_recv()
    first_xy = onward(((0, 1, 0, 0), (0, 1, 1, 0)), along_y)
    arrivals.append(onward(((0, 1, 0, 0), (1, 1, 0, 0)), core))
    second_y.wait_recv()
    second_xy = onward(((0, 0, 1, 1), (0, 1, 1, 1)), along_x)
    arrivals.append(onward(((0, 0, 1, 1), (1, 0, 1, 1)), core))
    for n, (copy, place) in enumerate(
        (
            (first_y, (1, 0, 1, 0)),
            (second_x, (1, 1, 0, 1)),
            (first_xy, (1, 1, 1, 0)),
            (second_xy, (1, 1, 1, 1)),
        )
    ):
        yield begin + unit * (2 + n // 2)
        copy.wait_recv()
        arrivals.append(onward(((0,) + place[1:], place), core))
    yield begin + unit * 3.1
    for copy in arrivals:
        copy.wait_recv()


def add_rows(target, other):
    if target.shape[-2] % 16 == 0:
        count = target.shape[-2] // 16

        def part(step):
            return (pl.ds(pl.multiple_of(step * 16, 16), 16), slice(None))

    else:
        assert target.shape[-1] % 128 == 0
        count = target.shape[-1] // 128

        def part(step):
            return (slice(None), pl.ds(pl.multiple_of(step * 128, 128), 128))

    for lead in range(math.prod(target.shape[:-2])):
        a, b = target, other
        if len(target.shape) > 2:
            a, b = target.at[lead], other.at[lead]

        @pl.loop(0, count)
        def _(step):
            here = part(step)
            a[here] = (a[here].astype(jnp.float32) + b[here].astype(jnp.float32)).astype(a.dtype)


def octet_reduce_steps(board, terms_ref, sum_ref, mine, from_core, from_link, begin=0.0):
    h = sum_ref.shape[0] // 2
    unit = 2.2 * math.prod(sum_ref.shape) / LINK
    core, along_x, along_y = ("plane", 1), ("plane", 2), "y"
    order = (
        (1, 1, 0),
        (1, 1, 1),
        (0, 1, 0),
        (1, 0, 1),
        (1, 0, 0),
        (0, 1, 1),
        (0, 0, 0),
        (0, 0, 1),
    )
    over_core = {}
    loads = {}
    for x, y, half in order:
        place = octet_place(0, x, y, half)
        loads[place] = board.move(
            terms_ref.at[pl.ds(place * h, h)], mine.at[place], close=False
        )
        over_core[place] = board.send(
            terms_ref.at[pl.ds((8 + place) * h, h)], from_core.at[place], core
        )

    def add_core(x, y, half):
        place = octet_place(0, x, y, half)
        loads[place].wait()
        over_core[place].wait_recv()
        add_rows(mine.at[place], from_core.at[place])
        return place

    second = {}
    for n, (x, y, half) in enumerate(order[:4]):
        yield begin + 0.1 * unit * (n + 1)
        place = add_core(x, y, half)
        second[(x, y, half)] = board.send(
            mine.at[place], from_link.at[n], along_y if half == 0 else along_x
        )
    third = {}
    for n, (x, y, half) in enumerate(order[4:6]):
        yield begin + unit * 1.2
        place = add_core(x, y, half)
        second[(1, 1, half)].wait_recv()
        add_rows(mine.at[place], from_link.at[half])
        third[half] = board.send(
            mine.at[place], from_link.at[4 + n], along_x if half == 0 else along_y
        )
    for half, sent in ((0, (0, 1, 0)), (1, (1, 0, 1))):
        yield begin + unit * 3.1
        place = add_core(0, 0, half)
        second[sent].wait_recv()
        third[half].wait_recv()

        @pl.loop(0, h // 16)
        def _(step):
            rows = pl.ds(pl.multiple_of(step * 16, 16), 16)
            out_rows = pl.ds(pl.multiple_of(half * h + step * 16, 16), 16)
            sum_ref[out_rows, :] = (
                mine[place, rows, :].astype(jnp.float32)
                + from_link[2 + half, rows, :].astype(jnp.float32)
                + from_link[4 + half, rows, :].astype(jnp.float32)
            )


def line_gather_steps(board, shard_ref, whole_ref, begin=0.0):
    unit = 4.4 * math.prod(shard_ref.shape) / LINK
    z = board.z
    far, near = board.line_xor(2), ("line", 1)
    two = board.send(shard_ref, whole_ref.at[z], ("line", 2))
    one = board.send(shard_ref, whole_ref.at[z], near)
    three_slot, on_slot = board.slot(), board.slot()
    three = board.make(three_slot, shard_ref, whole_ref.at[z], ("line", 3))
    onward = pltpu.make_async_remote_copy(
        src_ref=whole_ref.at[far],
        dst_ref=whole_ref.at[far],
        send_sem=board.sems[0].at[on_slot],
        recv_sem=board.sems[1].at[three_slot],
        device_id=board.device(near),
        device_id_type=MESH,
    )

    @pl.when(board.middle)
    def _():
        three.start()

    keep = board.move(shard_ref, whole_ref.at[z], close=False)
    yield begin + 2.0 * unit
    two.wait_recv()

    @pl.when(board.middle)
    def _():
        onward.start()

    yield begin + 3.1 * unit
    keep.wait()
    one.wait_recv()
    three.wait_recv()

    @pl.when(board.middle)
    def _():
        three.wait_send()
        onward.wait_send()


def line_reduce_steps(board, terms_ref, got_ref, held, carried, begin=0.0):
    unit = 4.4 * math.prod(got_ref.shape[1:]) / LINK
    near, two_off, three_off = ("line", 1), ("line", 2), ("line", 3)
    z_near, z_two, z_three = (board.line_xor(k) for k in (1, 2, 3))
    carry = board.make(board.slot(), terms_ref.at[z_three], carried, near)
    direct = board.make(board.slot(), terms_ref.at[z_three], got_ref.at[2], three_off)
    two_slot = board.slot()
    two_end = board.make(two_slot, terms_ref.at[z_two], got_ref.at[1], two_off)
    two_mid = board.make(two_slot, held, got_ref.at[1], two_off)

    @pl.when(jnp.logical_not(board.middle))
    def _():
        carry.start()
        two_end.start()

    @pl.when(board.middle)
    def _():
        direct.start()

    one = board.send(terms_ref.at[z_near], got_ref.at[0], near)
    load = board.move(terms_ref.at[z_two], held, close=False)
    yield begin + 1.3 * unit
    load.wait()

    @pl.when(board.middle)
    def _():
        carry.wait_recv()
        add_rows(held, carried)
        two_mid.start()

    yield begin + 3.1 * unit
    one.wait_recv()
    two_end.wait_recv()
    two_end.wait_send()

    @pl.when(board.middle)
    def _():
        direct.wait_recv()
        direct.wait_send()

    @pl.when(jnp.logical_not(board.middle))
    def _():
        carry.wait_send()


def plane_exchange_steps(board, blocks_ref, given_ref, begin=0.0):
    copies = [
        board.send(
            blocks_ref.at[board.place_xor(k)], given_ref.at[board.i], ("plane", k)
        )
        for k in (3, 2, 1)
    ]
    keep = board.move(blocks_ref.at[board.i], given_ref.at[board.i], close=False)
    yield begin + 9.0 * math.prod(blocks_ref.shape[1:]) / LINK
    for copy in copies:
        copy.wait_recv()
    keep.wait()


def transpose_steps(board, shard_ref, given_ref, begin=0.0):
    slot, spot = board.slot(), board.locals
    board.locals += 1
    other = (board.i * PLANE + board.z, board.t)
    copy = pltpu.make_async_remote_copy(
        src_ref=shard_ref,
        dst_ref=given_ref,
        send_sem=board.sems[0].at[slot],
        recv_sem=board.sems[1].at[slot],
        device_id=other,
        device_id_type=MESH,
    )
    keep = pltpu.make_async_copy(shard_ref, given_ref, board.sems[2].at[spot])

    @pl.when(board.i != board.z)
    def _():
        copy.start()

    @pl.when(board.i == board.z)
    def _():
        keep.start()

    yield begin + 9.0 * math.prod(shard_ref.shape) / LINK

    @pl.when(board.i != board.z)
    def _():
        copy.wait()

    @pl.when(board.i == board.z)
    def _():
        keep.wait()


NEAR_OCTET = (("plane", 1), ("plane", 2), "y")
NEAR_PLANE = (("plane", 1), ("plane", 2), ("plane", 3))
NEAR_LINE = (("line", 1), ("line", 2), ("line", 3))


def hbm(shape):
    return (jax.ShapeDtypeStruct(shape, jnp.bfloat16), HBM_SPEC)


class OctetGather:
    near, remotes, moves = NEAR_OCTET, 13, 1

    def __init__(self, own):
        self.given = own
        self.outs = [hbm((8 * own.shape[0],) + own.shape[1:])]
        self.scratch = []

    def steps(self, board, own, outs, scratch):
        return octet_gather_steps(board, own, outs[0])

    def read(self, outs):
        return outs[0]


class OctetReduce:
    near, remotes, moves = NEAR_OCTET, 14, 8

    def __init__(self, terms):
        self.given = terms
        m, n = terms.shape[0] // 8, terms.shape[1]
        self.outs = [(jax.ShapeDtypeStruct((m, n), jnp.float32), VMEM_SPEC)]
        self.scratch = [pltpu.VMEM((k, m // 2, n), terms.dtype) for k in (8, 8, 6)]

    def steps(self, board, terms, outs, scratch):
        return octet_reduce_steps(board, terms, outs[0], *scratch)

    def read(self, outs):
        return outs[0]


class LineGather:
    near, remotes, moves = NEAR_LINE, 4, 1

    def __init__(self, shard):
        self.given = shard
        self.outs = [hbm((LINE,) + shard.shape)]
        self.scratch = []

    def steps(self, board, shard, outs, scratch):
        return line_gather_steps(board, shard, outs[0])

    def read(self, outs):
        return outs[0]

    def plain(self):
        return lax.all_gather(self.given, "dp", axis_index_groups=line_groups(), axis=0)


class LineReduce:
    near, remotes, moves = NEAR_LINE, 4, 1

    def __init__(self, terms):
        self.given = terms
        shape = terms.shape[1:]
        self.outs = [hbm((3,) + shape)]
        self.scratch = [pltpu.VMEM(shape, terms.dtype)] * 2

    def steps(self, board, terms, outs, scratch):
        return line_reduce_steps(board, terms, outs[0], *scratch)

    def read(self, outs):
        z = line_index()
        got = outs[0].astype(jnp.float32)
        middle = (z == 1) | (z == 2)
        own = take(self.given, z).astype(jnp.float32)
        return own + got[0] + got[1] + jnp.where(middle, got[2], 0.0)

    def plain(self):
        return lax.psum_scatter(
            self.given, "dp", axis_index_groups=line_groups(), scatter_dimension=0
        ).astype(jnp.float32)


class PlaneExchange:
    near, remotes, moves = NEAR_PLANE, 3, 1

    def __init__(self, blocks):
        self.given = blocks
        self.outs = [hbm(blocks.shape)]
        self.scratch = []

    def steps(self, board, blocks, outs, scratch):
        return plane_exchange_steps(board, blocks, outs[0])

    def read(self, outs):
        return outs[0]

    def plain(self):
        i = plane_index()
        whole = jnp.zeros_like(self.given)
        for k in range(PLANE):
            piece = take(self.given, i ^ k)
            if k:
                piece = swap(piece, k)
            whole = lax.dynamic_update_index_in_dim(whole, piece, i ^ k, 0)
        return whole


class GatherColumns:
    near, remotes, moves = NEAR_PLANE + NEAR_LINE, 7, 2

    def __init__(self, blocks):
        self.given = blocks
        self.outs = [hbm(blocks.shape), hbm((LINE,) + blocks.shape)]
        self.scratch = []

    def steps(self, board, blocks, outs, scratch):
        begin = 9.0 * math.prod(blocks.shape[1:]) / LINK
        yield from plane_exchange_steps(board, blocks, outs[0])
        yield from line_gather_steps(board, outs[0], outs[1], begin)

    def read(self, outs):
        return outs[1]

    def plain(self):
        return LineGather(PlaneExchange(self.given).plain()).plain()


class GatherPack:
    near, remotes, moves = NEAR_LINE + NEAR_OCTET, 17, 2

    def __init__(self, shard):
        self.given = shard
        self.outs = [hbm((LINE,) + shard.shape), hbm((8 * LINE,) + shard.shape)]
        self.scratch = []

    def steps(self, board, shard, outs, scratch):
        begin = 13.2 * math.prod(shard.shape) / LINK
        yield from line_gather_steps(board, shard, outs[0])
        yield from octet_gather_steps(board, outs[0], outs[1], begin)

    def read(self, outs):
        return outs[1]


class Transpose:
    near, remotes, moves = ("transposed",), 1, 1

    def __init__(self, shard, back=False):
        self.given = shard
        self.back = back
        self.outs = [hbm(shard.shape)]
        self.scratch = []

    def steps(self, board, shard, outs, scratch):
        return transpose_steps(board, shard, outs[0])

    def read(self, outs):
        return outs[0]

    def plain(self):
        line = lax.axis_size("dp") // PLANE
        pairs = [(i * line + z, z * PLANE + i) for i in range(PLANE) for z in range(line)]
        if self.back:
            pairs = [(b, a) for a, b in pairs]
        return lax.ppermute(self.given, "dp", pairs)


def communicate(collective_id, *tasks, compute=None):
    if lax.axis_size("dp") != PLANE * LINE:
        results = []
        for n, task in enumerate(tasks):
            alone = 4 * collective_id + n
            if isinstance(task, (OctetGather, OctetReduce)):
                results += run_kernel(alone, [task])
            elif isinstance(task, GatherPack):
                results += run_kernel(alone, [OctetGather(LineGather(task.given).plain())])
            else:
                results.append(task.plain())
        return results + (run_kernel(None, [], compute) if compute else [])
    return run_kernel(collective_id, tasks, compute)


def run_kernel(collective_id, tasks, compute=None):
    near = []
    for task in tasks:
        near += [name for name in task.near if name not in near]
    n_outs = [len(task.outs) for task in tasks]
    n_scratch = [len(task.scratch) for task in tasks]
    more_givens = compute.givens if compute else []
    more_outs = compute.outs if compute else []
    more_scratch = compute.scratch if compute else []

    def kernel(*refs):
        refs = list(refs)

        def first(count):
            part = refs[:count]
            del refs[:count]
            return part

        givens, compute_givens = first(len(tasks)), first(len(more_givens))
        outs, compute_outs = first(sum(n_outs)), first(len(more_outs))
        scratch, compute_scratch = first(sum(n_scratch)), first(len(more_scratch))
        running, closing = [], []
        if tasks:
            board = Board(*refs)
            closing = board.closing
            board.greet(near)
        for n, task in enumerate(tasks):
            steps = task.steps(
                board,
                givens[n],
                outs[sum(n_outs[:n]) : sum(n_outs[: n + 1])],
                scratch[sum(n_scratch[:n]) : sum(n_scratch[: n + 1])],
            )
            running.append((next(steps), n, steps))
        phases = []
        if compute:
            phases = compute.phases(compute_givens, compute_outs, compute_scratch)
        done = 0.0
        while running or phases:
            running.sort(key=lambda item: item[:2])
            if phases and not (running and running[0][0] <= done):
                phases.pop(0)()
                done += compute.phase_time
                continue
            when, n, steps = running.pop(0)
            when = next(steps, None)
            if when is not None:
                running.append((when, n, steps))
        for close in closing:
            close()

    sems = []
    if tasks:
        sems = [
            pltpu.SemaphoreType.DMA((sum(task.remotes for task in tasks),)),
            pltpu.SemaphoreType.DMA((sum(task.remotes for task in tasks),)),
            pltpu.SemaphoreType.DMA((sum(task.moves for task in tasks),)),
        ]
    outs = pl.pallas_call(
        kernel,
        out_shape=[shape for task in tasks for shape, _ in task.outs] + more_outs,
        in_specs=[HBM_SPEC] * len(tasks) + [VMEM_SPEC] * len(more_givens),
        out_specs=[spec for task in tasks for _, spec in task.outs]
        + [VMEM_SPEC] * len(more_outs),
        scratch_shapes=[shape for task in tasks for shape in task.scratch]
        + more_scratch
        + sems,
        compiler_params=pltpu.CompilerParams(
            collective_id=collective_id,
            has_side_effects=bool(tasks),
            vmem_limit_bytes=VMEM_LIMIT,
        ),
        cost_estimate=pl.CostEstimate(flops=0, bytes_accessed=2**28, transcendentals=0),
    )(*[task.given for task in tasks], *more_givens)
    results = [
        task.read(outs[sum(n_outs[:n]) : sum(n_outs[: n + 1])]) for n, task in enumerate(tasks)
    ]
    return results + ([outs[sum(n_outs) :]] if compute else [])


def take(array, position):
    return lax.dynamic_index_in_dim(array, position, 0, keepdims=False)


def line_index():
    return lax.axis_index("dp") // PLANE


def plane_index():
    return lax.axis_index("dp") % PLANE


def line_groups():
    size = lax.axis_size("dp")
    return [[i + PLANE * z for z in range(size // PLANE)] for i in range(PLANE)]


def swap(array, bits):
    size = lax.axis_size("dp")
    return lax.ppermute(array, "dp", [(d, d ^ bits) for d in range(size)])


HEAD = 128
ROW_BLOCK = 256


def column_dot(left_side, right_side):
    return jnp.dot(left_side, right_side, preferred_element_type=jnp.float32)


def lane_index(shape):
    return lax.broadcasted_iota(jnp.int32, shape, len(shape) - 1)


def turn(values, wave, low_wave, high_wave):
    half = DR // 2
    return (
        values * wave
        + pltpu.roll(values, HEAD - half, 1) * low_wave
        + pltpu.roll(values, half, 1) * high_wave
    )


def score_bias(keys_ref, bounds_ref, bias, pack, pack_rows):
    @pl.loop(0, pack_rows // ROW_BLOCK)
    def _(block):
        rows = pl.ds(pl.multiple_of(block * ROW_BLOCK, ROW_BLOCK), ROW_BLOCK)
        here = bounds_ref[pl.ds(pack * pack_rows + block * ROW_BLOCK, ROW_BLOCK), :]
        key = keys_ref[pack, 0:1, :]
        allowed = (key >= here[:, 0:1]) & (key <= here[:, 1:2])
        bias[rows, :] = jnp.where(allowed, 0.0, MASKED)


class AttentionForward:
    def __init__(self, tokens, keys, bounds, waves, query_up, latent_up, packs, heads):
        rows = tokens.shape[0]
        self.packs, self.heads, self.pack_rows = packs, heads, rows // packs
        self.givens = [tokens, keys, bounds, *waves, query_up, latent_up]
        low = jnp.bfloat16
        self.pairs = -(-heads // 2)
        self.outs = [
            jax.ShapeDtypeStruct((rows, heads * HEAD), low),
            jax.ShapeDtypeStruct((rows, heads * HEAD), low),
            jax.ShapeDtypeStruct((rows, self.pairs * HEAD), low),
            jax.ShapeDtypeStruct((rows, HEAD), jnp.float32),
        ]
        self.scratch = [
            pltpu.VMEM((self.pack_rows, self.pack_rows), jnp.float32),
            pltpu.VMEM((self.pack_rows, HEAD), low),
        ]
        self.phase_time = 10.0

    def phases(self, givens, outs, scratch):
        tokens, keys, bounds, wave, low_wave, high_wave, query_up, latent_up = givens
        queries, heads_out, mixed, totals = outs
        bias, keys_tile = scratch
        scale = QH ** (-0.5)
        size = self.pack_rows

        def run(pack):
            score_bias(keys, bounds, bias, pack, size)
            start = pack * size
            rope_key = tokens[start : start + size, QR + KVR : QR + KVR + HEAD]
            for n in range(self.pairs):
                mixed[start : start + size, n * HEAD : (n + 1) * HEAD] = jnp.zeros(
                    (size, HEAD), mixed.dtype
                )
            totals[start : start + size, :] = jnp.zeros((size, HEAD), jnp.float32)

            @pl.loop(0, self.heads)
            def _(head):
                lanes = pl.ds(pl.multiple_of(head * HEAD, HEAD), HEAD)
                pair = pl.ds(pl.multiple_of((head // 2) * HEAD, HEAD), HEAD)
                tile = column_dot(
                    tokens[start : start + size, QR : QR + KVR], latent_up[:, lanes]
                ).astype(jnp.bfloat16)
                heads_out[start : start + size, lanes] = tile
                lane = lane_index((size, HEAD))
                keys_tile[...] = jnp.where(
                    lane < DN,
                    tile.astype(jnp.float32),
                    pltpu.roll(rope_key.astype(jnp.float32), DN, 1),
                ).astype(jnp.bfloat16)

                @pl.loop(0, size // ROW_BLOCK)
                def _(block):
                    at = pl.multiple_of(start + block * ROW_BLOCK, ROW_BLOCK)
                    rows = pl.ds(at, ROW_BLOCK)
                    raw = column_dot(tokens[rows, 0:QR], query_up[:, lanes])
                    query = turn(
                        raw, wave[rows, :], low_wave[rows, :], high_wave[rows, :]
                    ).astype(jnp.bfloat16)
                    queries[rows, lanes] = query
                    scores = right_transposed(query, keys_tile[...]) * scale + bias[
                        pl.ds(pl.multiple_of(block * ROW_BLOCK, ROW_BLOCK), ROW_BLOCK), :
                    ]
                    top = jnp.max(scores, axis=1, keepdims=True)
                    exponent = jnp.exp(scores - top)
                    total = jnp.sum(exponent, axis=1, keepdims=True)
                    prob = (exponent * (1.0 / total)).astype(jnp.bfloat16)
                    out = column_dot(prob, heads_out[start : start + size, lanes])
                    lane = lane_index((ROW_BLOCK, HEAD))
                    totals[rows, :] = jnp.where(
                        lane == head, top + jnp.log(total), totals[rows, :]
                    )
                    even = head % 2 == 0
                    placed = jnp.where(even, pltpu.roll(out, DN, 1), out)
                    before = mixed[rows, pair].astype(jnp.float32)
                    mixed[rows, pair] = jnp.where(
                        (lane < DN) == even, placed, before
                    ).astype(mixed.dtype)

        return [functools.partial(run, pack) for pack in range(self.packs)]


class AttentionBackward:
    def __init__(
        self,
        queries,
        latent_heads,
        totals,
        grad_mixed,
        tokens,
        keys,
        bounds,
        waves,
        query_up,
        latent_up,
        packs,
        heads,
    ):
        rows = tokens.shape[0]
        self.packs, self.heads, self.pack_rows = packs, heads, rows // packs
        self.givens = [
            queries,
            latent_heads,
            totals,
            grad_mixed,
            tokens,
            keys,
            bounds,
            *waves,
            query_up,
            latent_up,
        ]
        low = jnp.bfloat16
        self.outs = [
            jax.ShapeDtypeStruct((rows, heads * HEAD), low),
            jax.ShapeDtypeStruct((rows, heads * HEAD), low),
            jax.ShapeDtypeStruct((rows, QR + KVR + HEAD), low),
        ]
        size = self.pack_rows
        self.scratch = [
            pltpu.VMEM((size, size), jnp.float32),
            pltpu.VMEM((size, HEAD), low),
            pltpu.VMEM((size, HEAD), jnp.float32),
            pltpu.VMEM((size, HEAD), jnp.float32),
            pltpu.VMEM((size, HEAD), jnp.float32),
        ]
        self.phase_time = 14.0

    def phases(self, givens, outs, scratch):
        (
            queries,
            heads_in,
            totals,
            grad_mixed,
            tokens,
            keys,
            bounds,
            wave,
            low_wave,
            high_wave,
            query_up,
            latent_up,
        ) = givens
        grad_queries, grad_heads, terms = outs
        bias, keys_tile, grad_key, grad_value, grad_rope = scratch
        scale = QH ** (-0.5)
        size = self.pack_rows

        def run(pack):
            score_bias(keys, bounds, bias, pack, size)
            start = pack * size
            rope_key = tokens[start : start + size, QR + KVR : QR + KVR + HEAD]
            grad_rope[...] = jnp.zeros_like(grad_rope)

            @pl.loop(0, self.heads)
            def _(head):
                lanes = pl.ds(pl.multiple_of(head * HEAD, HEAD), HEAD)
                pair = pl.ds(pl.multiple_of((head // 2) * HEAD, HEAD), HEAD)
                lane = lane_index((size, HEAD))
                keys_tile[...] = jnp.where(
                    lane < DN,
                    heads_in[start : start + size, lanes].astype(jnp.float32),
                    pltpu.roll(rope_key.astype(jnp.float32), DN, 1),
                ).astype(jnp.bfloat16)
                grad_key[...] = jnp.zeros_like(grad_key)
                grad_value[...] = jnp.zeros_like(grad_value)

                @pl.loop(0, size // ROW_BLOCK)
                def _(block):
                    at = pl.multiple_of(start + block * ROW_BLOCK, ROW_BLOCK)
                    rows = pl.ds(at, ROW_BLOCK)
                    lane = lane_index((ROW_BLOCK, HEAD))
                    query = queries[rows, lanes]
                    key_all = keys_tile[...]
                    scores = right_transposed(query, key_all) * scale + bias[
                        pl.ds(pl.multiple_of(block * ROW_BLOCK, ROW_BLOCK), ROW_BLOCK), :
                    ]
                    total = jnp.sum(
                        jnp.where(lane == head, totals[rows, :], 0.0), axis=1, keepdims=True
                    )
                    prob = jnp.exp(scores - total)
                    grad_pair = grad_mixed[rows, pair].astype(jnp.float32)
                    even = head % 2 == 0
                    grad_out = jnp.where(
                        lane < DN, 0.0, jnp.where(even, pltpu.roll(grad_pair, DN, 1), grad_pair)
                    ).astype(jnp.bfloat16)
                    grad_prob = right_transposed(grad_out, heads_in[start : start + size, lanes])
                    inner = jnp.sum(prob * grad_prob, axis=1, keepdims=True)
                    grad_score = (prob * (grad_prob - inner)).astype(jnp.bfloat16)
                    grad_value[...] += left_transposed(prob.astype(jnp.bfloat16), grad_out)
                    grad_key[...] += left_transposed(grad_score, query)
                    grad_query = column_dot(grad_score, key_all) * scale
                    grad_queries[rows, lanes] = turn(
                        grad_query, wave[rows, :], -low_wave[rows, :], -high_wave[rows, :]
                    ).astype(grad_queries.dtype)

                scaled = grad_key[...] * scale
                grad_rope[...] += scaled
                grad_heads[start : start + size, lanes] = jnp.where(
                    lane < DN, scaled, grad_value[...]
                ).astype(grad_heads.dtype)

            @pl.loop(0, size // ROW_BLOCK)
            def _(block):
                at = pl.multiple_of(start + block * ROW_BLOCK, ROW_BLOCK)
                rows = pl.ds(at, ROW_BLOCK)
                here = pl.ds(pl.multiple_of(block * ROW_BLOCK, ROW_BLOCK), ROW_BLOCK)
                terms[rows, 0:QR] = right_transposed(grad_queries[rows, :], query_up[...]).astype(
                    terms.dtype
                )
                terms[rows, QR : QR + KVR] = right_transposed(
                    grad_heads[rows, :], latent_up[...]
                ).astype(terms.dtype)
                terms[rows, QR + KVR :] = pltpu.roll(grad_rope[here, :], HEAD - DN, 1).astype(
                    terms.dtype
                )

        return [functools.partial(run, pack) for pack in range(self.packs)]


def positions(segment_ids):
    token_index = jnp.arange(segment_ids.shape[0], dtype=jnp.int32)
    doc_start = jnp.concatenate(
        [jnp.ones((1,), dtype=jnp.bool_), segment_ids[1:] != segment_ids[:-1]]
    )
    starts = lax.cummax(jnp.where(doc_start, token_index, 0), axis=0)
    return token_index - starts


def rope_tables(position):
    exponent = jnp.arange(DR // 2, dtype=jnp.float32) * (2.0 / DR)
    rope_angle = position[:, None] * (ROPE_BASE ** (-exponent))[None, :]
    return (jnp.cos(rope_angle), jnp.sin(rope_angle))


def local(
    inputs,
    cotangent,
    segment_ids,
    gains,
    gains_first,
    gains_second,
    query_down,
    query_down_first,
    query_down_second,
    latent_down,
    latent_down_first,
    latent_down_second,
    query_up,
    query_up_first,
    query_up_second,
    latent_up,
    latent_up_first,
    latent_up_second,
    output_proj,
    output_proj_first,
    output_proj_second,
    gate_proj,
    gate_proj_first,
    gate_proj_second,
    up_proj,
    up_proj_first,
    up_proj_second,
    down_proj,
    down_proj_first,
    down_proj_second,
):
    size = lax.axis_size("dp")
    tensor = lax.axis_size("tensor")
    line = size // PLANE
    z, i, t = line_index(), plane_index(), lax.axis_index("tensor")
    half_rows = inputs.shape[0]
    pack_rows = segment_ids.shape[0]
    packs = PLANE
    rows_all = packs * pack_rows
    low = jnp.bfloat16
    local_heads = H // (PLANE * tensor)
    units = FF // (PLANE * tensor)
    mixed_width = -(-local_heads // 2) * HEAD

    def column_blocks(weight, columns):
        return weight.astype(low).reshape(-1, PLANE, columns).transpose(1, 0, 2)

    def unit_blocks(weight):
        return (
            weight.astype(low)
            .reshape(weight.shape[0], line, PLANE, units // line)
            .transpose(2, 0, 1, 3)
            .reshape(PLANE, weight.shape[0], units)
        )

    down_rows = query_down.shape[0]
    pack_height = down_rows + 16
    gain_width = gains.shape[0]
    down_pack = jnp.concatenate(
        [
            jnp.concatenate([query_down, latent_down], axis=1).astype(low),
            jnp.pad(gains.astype(low)[None], ((0, 15), (0, QR + KVR + DR - gain_width))),
        ],
        axis=0,
    )
    def head_blocks(weight):
        blocks = weight.astype(low).reshape(-1, PLANE, local_heads, QH)
        blocks = jnp.pad(blocks, ((0, 0), (0, 0), (0, 0), (0, HEAD - QH)))
        return blocks.reshape(-1, PLANE, local_heads * HEAD).transpose(1, 0, 2)

    pack_all, query_up_all, latent_up_all, gate_plane, output_moved = communicate(
        1,
        GatherPack(down_pack),
        GatherColumns(head_blocks(query_up)),
        GatherColumns(column_blocks(latent_up, local_heads * KH)),
        PlaneExchange(unit_blocks(gate_proj)),
        Transpose(output_proj.astype(low)),
    )
    query_up_all = query_up_all.reshape(QR, local_heads * HEAD)
    latent_up_all = latent_up_all.reshape(KVR, local_heads * KH)
    down_octet = pack_all.reshape(2, 2, tensor, line, pack_height, QR + KVR + DR)
    down_blocks = jnp.zeros((PLANE, tensor, line, pack_height, QR + KVR + DR), low)
    for k in range(PLANE):
        for y in range(tensor):
            down_blocks = lax.dynamic_update_slice(
                down_blocks,
                down_octet[k % 2, k // 2, y][None, None],
                (i ^ k, (t + y) % tensor, 0, 0, 0),
            )
    down_blocks = down_blocks.transpose(2, 0, 1, 3, 4)
    down_both = down_blocks[..., :down_rows, :].reshape(D, QR + KVR + DR)
    gain_values = down_blocks[..., down_rows, :gain_width].reshape(-1).astype(jnp.float32)
    gain_attention = gain_values[:D]
    gain_query = gain_values[D : D + QR]
    gain_latent = gain_values[D + QR : D + QR + KVR]
    gain_ffn = gain_values[D + QR + KVR :]

    incoming = inputs.astype(jnp.float32)
    attn_unit, inverse_attention = norm_forward(incoming, gain_attention)
    normed_attn = attn_unit.astype(low)
    both_latent = jnp.dot(normed_attn, down_both, preferred_element_type=jnp.float32)
    query_latent = both_latent[:, :QR]
    latent = both_latent[:, QR:]
    query_unit, inverse_query = norm_forward(query_latent, gain_query)
    latent_unit, inverse_latent = norm_forward(latent[:, :KVR], gain_latent)
    own_position = lax.dynamic_slice_in_dim(positions(segment_ids), t * half_rows, half_rows)
    own_segment = lax.dynamic_slice_in_dim(segment_ids, t * half_rows, half_rows)
    own_cosine, own_sine = rope_tables(own_position.astype(jnp.float32))
    own_rope_key = rotate(latent[:, KVR:], own_cosine, own_sine)
    marks = jnp.stack(
        [own_segment // 16, own_segment % 16, own_position // 16, own_position % 16], axis=1
    )
    tokens_own = jnp.concatenate(
        [
            query_unit.astype(low),
            latent_unit.astype(low),
            own_rope_key.astype(low),
            marks.astype(low),
            jnp.zeros((half_rows, 128 - DR - 4), low),
        ],
        axis=1,
    )
    tokens_all, output_all = communicate(3, OctetGather(tokens_own), LineGather(output_moved))
    output_all = jnp.pad(
        output_all.reshape(local_heads * DV, D), ((0, mixed_width - local_heads * DV), (0, 0))
    )
    marks_all = tokens_all[:, QR + KVR + DR : QR + KVR + DR + 4].astype(jnp.float32)
    key_base = (marks_all[:, 0] * 16.0 + marks_all[:, 1]) * pack_rows
    position = marks_all[:, 2] * 16.0 + marks_all[:, 3]
    key = key_base + position
    keys = jnp.broadcast_to(key.reshape(packs, 1, pack_rows), (packs, 8, pack_rows))
    bounds = jnp.pad(jnp.stack([key_base, key], axis=1), ((0, 0), (0, HEAD - 2)))
    rope_cosine, rope_sine = rope_tables(position)
    nothing = jnp.zeros((rows_all, DR), jnp.float32)
    still = jnp.zeros((rows_all, DN), jnp.float32)
    waves = (
        jnp.concatenate([still + 1.0, rope_cosine, rope_cosine, nothing], axis=1),
        jnp.concatenate([still, -rope_sine, nothing, nothing[:, : DR // 2]], axis=1),
        jnp.concatenate([still, nothing[:, : DR // 2], rope_sine, nothing], axis=1),
    )
    grad_ffn, up_plane, gate_all, (queries, latent_heads, mixed_heads, log_totals) = communicate(
        2,
        OctetGather((RESIDUAL * cotangent.astype(jnp.float32)).astype(low)),
        PlaneExchange(unit_blocks(up_proj)),
        LineGather(gate_plane),
        compute=AttentionForward(
            tokens_all, keys, bounds, waves, query_up_all, latent_up_all, packs, local_heads
        ),
    )
    gate_all = gate_all.reshape(D, units)
    attention_terms = jnp.dot(mixed_heads, output_all, preferred_element_type=jnp.float32)
    attention_sum, up_all = communicate(
        4, OctetReduce(attention_terms.astype(low)), LineGather(up_plane)
    )
    up_all = up_all.reshape(D, units)
    residual = incoming + RESIDUAL * attention_sum

    ffn_unit, inverse_ffn = norm_forward(residual, gain_ffn)
    normed_ffn, down_all = communicate(
        5, OctetGather(ffn_unit.astype(low)), LineGather(down_proj.astype(low))
    )
    down_all = down_all.reshape(units, D)
    gate_value = jnp.dot(normed_ffn, gate_all, preferred_element_type=jnp.float32)
    up_value = jnp.dot(normed_ffn, up_all, preferred_element_type=jnp.float32)
    gate_sigmoid = lax.logistic(gate_value)
    silu_gate = gate_value * gate_sigmoid
    hidden = (silu_gate * up_value).astype(low)
    grad_hidden = right_transposed(grad_ffn, down_all)
    grad_gate = (
        grad_hidden * up_value * gate_sigmoid * (1.0 + gate_value * (1.0 - gate_sigmoid))
    ).astype(low)
    grad_up = (grad_hidden * silu_gate).astype(low)
    ffn_back_terms = right_transposed(grad_gate, gate_all) + right_transposed(grad_up, up_all)
    down_grad = left_transposed(hidden, grad_ffn).astype(low).reshape(line, -1, D)
    gate_grad = left_transposed(normed_ffn, grad_gate).astype(low)
    up_grad = left_transposed(normed_ffn, grad_up).astype(low)
    ffn_terms = jnp.dot(hidden, down_all, preferred_element_type=jnp.float32).astype(low)
    grad_normed_ffn, down_shard = communicate(
        6, OctetReduce(ffn_back_terms.astype(low)), LineReduce(down_grad)
    )
    outer_grad = cotangent.astype(jnp.float32)
    grad_incoming_ffn, gain_ffn_grad = norm_backward(
        residual, inverse_ffn, gain_ffn, grad_normed_ffn
    )
    grad_residual = outer_grad + grad_incoming_ffn

    grad_branch, gate_sum = communicate(
        7,
        OctetGather((RESIDUAL * grad_residual).astype(low)),
        LineReduce(gate_grad.reshape(line, PLANE, -1, units)),
    )
    output_grad = (
        left_transposed(mixed_heads, grad_branch)
        .astype(low)[: local_heads * DV]
        .reshape(line, -1, D)
    )
    grad_mixed = right_transposed(grad_branch, output_all).astype(low)
    ffn_sum, up_sum, (grad_query_heads, grad_latent_heads, grad_unit_terms) = communicate(
        8,
        OctetReduce(ffn_terms),
        LineReduce(up_grad.reshape(line, PLANE, -1, units)),
        compute=AttentionBackward(
            queries,
            latent_heads,
            log_totals,
            grad_mixed,
            tokens_all,
            keys,
            bounds,
            waves,
            query_up_all,
            latent_up_all,
            packs,
            local_heads,
        ),
    )
    block_output = (residual + RESIDUAL * ffn_sum).astype(low)
    query_up_grad = left_transposed(tokens_all[:, :QR], grad_query_heads).astype(low)
    latent_up_grad = left_transposed(tokens_all[:, QR : QR + KVR], grad_latent_heads).astype(low)
    grad_units, output_sum, gate_parts = communicate(
        9,
        OctetReduce(grad_unit_terms),
        LineReduce(output_grad),
        PlaneExchange(gate_sum.astype(low)),
    )
    grad_query_wide, gain_query_grad = norm_backward(
        query_latent, inverse_query, gain_query, grad_units[:, :QR]
    )
    grad_latent_part, gain_latent_grad = norm_backward(
        latent[:, :KVR], inverse_latent, gain_latent, grad_units[:, QR : QR + KVR]
    )
    grad_rope = unrotate(grad_units[:, QR + KVR : QR + KVR + DR], own_cosine, own_sine)
    grad_both = jnp.concatenate([grad_query_wide, grad_latent_part, grad_rope], axis=1).astype(low)
    down_both_grad = left_transposed(normed_attn, grad_both).astype(low)
    grad_normed_attn = right_transposed(grad_both, down_both)
    grad_incoming_attn, gain_attention_grad = norm_backward(
        incoming, inverse_attention, gain_attention, grad_normed_attn
    )
    input_grad = (grad_residual + grad_incoming_attn).astype(low)
    gains_grad = jnp.concatenate(
        [gain_attention_grad, gain_query_grad, gain_latent_grad, gain_ffn_grad]
    ).astype(low)
    pack_grad = jnp.concatenate(
        [
            down_both_grad.reshape(line, PLANE, tensor, down_rows, QR + KVR + DR),
            jnp.pad(
                gains_grad.reshape(line, PLANE, tensor, 1, gain_width),
                ((0, 0), (0, 0), (0, 0), (0, 15), (0, QR + KVR + DR - gain_width)),
            ),
        ],
        axis=3,
    ).transpose(1, 2, 0, 3, 4)
    pack_terms = jnp.concatenate(
        [
            lax.dynamic_slice(
                pack_grad,
                (i ^ (core + 2 * x), (t + y) % tensor, 0, 0, 0),
                (1, 1) + pack_grad.shape[2:],
            ).reshape(line * pack_height, QR + KVR + DR)
            for core in range(2)
            for x in range(2)
            for y in range(tensor)
        ],
        axis=0,
    )
    pack_octet, query_up_sum, latent_up_sum, up_parts, output_shard = communicate(
        10,
        OctetReduce(pack_terms),
        LineReduce(query_up_grad.reshape(line, PLANE, -1, local_heads * HEAD)),
        LineReduce(latent_up_grad.reshape(line, PLANE, -1, local_heads * KH)),
        PlaneExchange(up_sum.astype(low)),
        Transpose(output_sum.astype(low), back=True),
    )
    pack_sum, query_up_parts, latent_up_parts = communicate(
        11,
        LineReduce(pack_octet.astype(low).reshape(line, pack_height, QR + KVR + DR)),
        PlaneExchange(query_up_sum.astype(low)),
        PlaneExchange(latent_up_sum.astype(low)),
    )
    query_down_shard = pack_sum[:down_rows, :QR]
    latent_down_shard = pack_sum[:down_rows, QR:]
    gains_shard = pack_sum[down_rows, :gain_width]

    def unit_columns(blocks):
        return (
            blocks.astype(jnp.float32)
            .reshape(PLANE, -1, line, units // line)
            .transpose(1, 2, 0, 3)
            .reshape(-1, PLANE * units)
        )

    def head_columns(blocks):
        return blocks.astype(jnp.float32).transpose(1, 0, 2).reshape(blocks.shape[1], -1)

    gate_shard, up_shard = unit_columns(gate_parts), unit_columns(up_parts)
    query_up_parts = query_up_parts.reshape(PLANE, -1, local_heads, HEAD)[..., :QH]
    query_up_shard = head_columns(query_up_parts.reshape(PLANE, -1, local_heads * QH))
    latent_up_shard = head_columns(latent_up_parts)
    output_shard = output_shard.astype(jnp.float32)

    gains_out = adamw_update(gains, gains_first, gains_second, gains_shard, GAIN_RATE)
    query_down_out = adamw_update(
        query_down, query_down_first, query_down_second, query_down_shard, matrix_rate(D)
    )
    latent_down_out = adamw_update(
        latent_down, latent_down_first, latent_down_second, latent_down_shard, matrix_rate(D)
    )
    query_up_out = adamw_update(
        query_up, query_up_first, query_up_second, query_up_shard, matrix_rate(QR)
    )
    latent_up_out = adamw_update(
        latent_up, latent_up_first, latent_up_second, latent_up_shard, matrix_rate(KVR)
    )
    output_out = adamw_update(
        output_proj, output_proj_first, output_proj_second, output_shard, matrix_rate(H * DV // 64)
    )
    gate_out = adamw_update(
        gate_proj, gate_proj_first, gate_proj_second, gate_shard, matrix_rate(D)
    )
    up_out = adamw_update(up_proj, up_proj_first, up_proj_second, up_shard, matrix_rate(D))
    down_out = adamw_update(
        down_proj, down_proj_first, down_proj_second, down_shard, matrix_rate(FF // 8)
    )
    return (
        block_output,
        input_grad,
        gains_out[0],
        gains_out[1],
        gains_out[2],
        query_down_out[0],
        query_down_out[1],
        query_down_out[2],
        latent_down_out[0],
        latent_down_out[1],
        latent_down_out[2],
        query_up_out[0],
        query_up_out[1],
        query_up_out[2],
        latent_up_out[0],
        latent_up_out[1],
        latent_up_out[2],
        output_out[0],
        output_out[1],
        output_out[2],
        gate_out[0],
        gate_out[1],
        gate_out[2],
        up_out[0],
        up_out[1],
        up_out[2],
        down_out[0],
        down_out[1],
        down_out[2],
    )


def solution(mesh):
    in_specs = (
        P(("dp", "tensor"), None),
        P(("dp", "tensor"), None),
        P("dp"),
        P(("dp", "tensor")),
        P(("dp", "tensor")),
        P(("dp", "tensor")),
        P(("dp", "tensor"), None),
        P(("dp", "tensor"), None),
        P(("dp", "tensor"), None),
        P(("dp", "tensor"), None),
        P(("dp", "tensor"), None),
        P(("dp", "tensor"), None),
        P("dp", "tensor"),
        P("dp", "tensor"),
        P("dp", "tensor"),
        P("dp", "tensor"),
        P("dp", "tensor"),
        P("dp", "tensor"),
        P(("tensor", "dp"), None),
        P(("tensor", "dp"), None),
        P(("tensor", "dp"), None),
        P("dp", "tensor"),
        P("dp", "tensor"),
        P("dp", "tensor"),
        P("dp", "tensor"),
        P("dp", "tensor"),
        P("dp", "tensor"),
        P(("tensor", "dp"), None),
        P(("tensor", "dp"), None),
        P(("tensor", "dp"), None),
    )
    out_specs = (
        P(("dp", "tensor"), None),
        P(("dp", "tensor"), None),
        P(("dp", "tensor")),
        P(("dp", "tensor")),
        P(("dp", "tensor")),
        P(("dp", "tensor"), None),
        P(("dp", "tensor"), None),
        P(("dp", "tensor"), None),
        P(("dp", "tensor"), None),
        P(("dp", "tensor"), None),
        P(("dp", "tensor"), None),
        P("dp", "tensor"),
        P("dp", "tensor"),
        P("dp", "tensor"),
        P("dp", "tensor"),
        P("dp", "tensor"),
        P("dp", "tensor"),
        P(("tensor", "dp"), None),
        P(("tensor", "dp"), None),
        P(("tensor", "dp"), None),
        P("dp", "tensor"),
        P("dp", "tensor"),
        P("dp", "tensor"),
        P("dp", "tensor"),
        P("dp", "tensor"),
        P("dp", "tensor"),
        P(("tensor", "dp"), None),
        P(("tensor", "dp"), None),
        P(("tensor", "dp"), None),
    )
    return jax.shard_map(local, mesh=mesh, in_specs=in_specs, out_specs=out_specs, check_vma=False)
```

time: 2690 us -> 1120 us (0.42)
  waiting for transfers between devices: 2200 us -> 0 us
  Pallas kernels: 0 us -> 741 us
  blocking collectives: 82.3 us -> 0 us
  matrix products: 260 us -> 184 us
  local copies, waits for them, and re-layouts: 27.9 us -> 96.3 us
    reduce_scatter x12 -> x0, waiting for transfers between devices: 1480 us -> none  [the longest x1 328 us: local(): lax.psum_scatter(gate_grad, 'dp', scatter_dimension=0, tiled=True)]
    pallas_call x0 -> x11, Pallas kernels: none -> 741 us  [run_kernel(): pl.pallas_call(kernel, out_shape=[shape for task in tasks for shape, _ in...]
    all_gather x12 -> x0, waiting for transfers between devices: 719 us -> none  [the longest x1 128 us: local(): lax.all_gather(gate_proj.astype(jnp.bfloat16), 'dp', axis=0, tiled=True)]
    unnamed x2 -> x0, blocking collectives: 82.3 us -> none
    dot_general x12 -> x3, matrix products: 84.3 us -> 31 us  [the longest x1 16.8 us: local(): jnp.dot(hidden, down_all, preferred_element_type=jnp.float32).astype(low)]
    reshape x0 -> x21, local copies, waits for them, and re-layouts: none -> 47.8 us  [the longest x6 22.9 us: unit_columns(): return blocks.astype(jnp.float32).reshape(PLANE, -1, line, units // line)...]
    dot_general x8 -> x7, matrix products: 79.7 us -> 55.7 us  [left_transposed(): lax.dot_general(left_side, right_side, (((0,), (0,)), ((), ())), preferre...]
    dot_general x8 -> x5, matrix products: 65 us -> 63.7 us  [right_transposed(): lax.dot_general(left_side, right_side, (((1,), (1,)), ((), ())), preferre...]
  transfers between devices with their start and end apart: 24 -> 0, of which waited for: 22 -> 0; matrix products, arithmetic and copies ran while one was open for 8% -> 0% of each run, Pallas kernels for 0% -> 0%
where the time goes in v1:
time: 1120 us; the launch traced here: 1110 us
  Pallas kernels  741 us (66%)
  matrix products  184 us (16%)
  local copies, waits for them, and re-layouts  96.3 us (9%)
  other arithmetic  88.6 us (8%)
    pallas_call x11, Pallas kernels, run_kernel(): pl.pallas_call(kernel, out_shape=[shape for task in tasks for shape, _ in...  741 us
    dot_general x5, matrix products, right_transposed(): lax.dot_general(left_side, right_side, (((1,), (1,)), ((), ())), preferre...  63.7 us
    dot_general x7, matrix products, left_transposed(): lax.dot_general(left_side, right_side, (((0,), (0,)), ((), ())), preferre...  55.7 us
    sub x9, other arithmetic, adamw_update(): weight - step_rate * (first_hat / (jnp.sqrt(second_hat) + ADAM_EPSILON) +...  23.9 us
    reshape x6, local copies, waits for them, and re-layouts, unit_columns(): return blocks.astype(jnp.float32).reshape(PLANE, -1, line, units // line)...  22.9 us

profile of v1, /device:TPU:0, one launch (start us, length us, event | category | flops | bytes accessed | tf_op | source)
XLA Modules:
  0.0 1112.7 jit_solution(11049853345970534)
XLA Ops:
  17.0 5.3 reshape.384
  39.5 94.0 %shard_map.509 = (bf16[4,96,1056]{2,1,0:T(8,128)(2,1)}, bf16[32,96,1056]{2,1,0:T(8,128)(2,1)}, bf16[4,48,640]{2,1,0:T(8,128)(2,1)}, bf16[4,4,48,640]{3,2,1,0:T(8...) custom-call(bf16[96,1056]{1,0:T(8,128)(2,1)} %fusion.63.refs_0_, ...), custom_call_target="tpu_custom_call" | custom-call | bytes 268435456 | tf_op jit(solution)/shard_map/pallas_call | solution.py:709
  148.0 32.2 %shard_map.510 = (bf16[2048,1152]{1,0:T(8,128)(2,1)}, bf16[4,80,2560]{2,1,0:T(8,128)(2,1)}) custom-call(bf16[256,1152]{1,0:T(8,128)(2,1)} %concatenate.45.refs_0_, bf16[80,2560]{1,0:T(8,128)(2,1)} %get-tuple-element.69.refs_1_), custom_call_target="tpu_custom_call" | custom-call | bytes 268435456 | tf_op jit(solution)/shard_map/pallas_call | solution.py:709
  192.7 111.3 %shard_map.511 = (bf16[2048,2560]{1,0:T(8,128)(2,1)}, bf16[4,160,800]{2,1,0:T(8,128)(2,1)}, bf16[4,4,160,800]{3,2,1,0:T(8,128)(2,1)}, bf16[2048,640]{1,0:T(8,128...) custom-call(bf16[256,2560]{1,0:T(8,128)(2,1)} %fusion.9.refs_0_, ...), custom_call_target="tpu_custom_call" | custom-call | bytes 268435456 | tf_op jit(solution)/shard_map/pallas_call | solution.py:709
  304.1 9.6 convolution_convert_fusion.2.refs_0_
  313.7 79.6 %shard_map.512 = (f32[256,2560]{1,0:T(8,128)}, bf16[4,4,160,800]{3,2,1,0:T(8,128)(2,1)}) custom-call(bf16[2048,2560]{1,0:T(8,128)(2,1)} %convolution_convert_fusion.2.refs_0_, bf16[4,160,800]{2,1,0:T(8,128)(2,1)} %get-tuple-element.75.refs_1_), custom_call_target="tpu_custom_call" | custom-call | bytes 268435456 | tf_op jit(solution)/shard_map/pallas_call | solution.py:709
  398.9 73.6 %shard_map.513 = (bf16[2048,2560]{1,0:T(8,128)(2,1)}, bf16[4,200,2560]{2,1,0:T(8,128)(2,1)}) custom-call(bf16[256,2560]{1,0:T(8,128)(2,1)} %multiply_convert_fusion.4.refs_0_, bf16[200,2560]{1,0:T(8,128)(2,1)} %convert_element_type.216.refs_1_), custom_call_target="tpu_custom_call" | custom-call | bytes 268435456 | tf_op jit(solution)/shard_map/pallas_call | solution.py:709
  472.6 14.5 %fusion.108 = f32[2048,800]{0,1:T(8,128)} fusion(bf16[2048,2560]{1,0:T(8,128)(2,1)} %get-tuple-element.81, bf16[800,2560]{1,0:T(8,128)(2,1)} %bitcast.202), kind=kOutput, calls=%fused_computation.254 | convolution fusion | flops 8388608000 | bytes 21135360 | tf_op jit(solution)/shard_map/dot_general | solution.py:36
  487.1 13.0 %fusion.107 = f32[2048,800]{0,1:T(8,128)} fusion(bf16[2048,2560]{1,0:T(8,128)(2,1)S(1)} %copy-done.75, bf16[2560,800]{1,0:T(8,128)(2,1)} %bitcast.200), kind=kOutput, calls=%fused_computation.253 | convolution fusion | flops 8388608000 | bytes 21135360 | tf_op jit(solution)/shard_map/dot_general | solution.py:1183
  500.1 20.6 %multiply_convert_fusion = (bf16[2048,800]{0,1:T(8,128)(2,1)}, bf16[2048,800]{0,1:T(8,128)(2,1)S(1)}, bf16[2048,800]{0,1:T(8,128)(2,1)}) fusion(f32[2048,800]{0,1:T(8,128)} %fusion.108, f32[2048,800]{0,1:T(8,128)} %fusion.107, bf16[2048,2560]{1,0:T(8,128)(2,1)} %get-tuple-element.77, bf16[2560,800]{1,0:T(8,128)(2,1)} %bitcast.196), kind=kOutput, calls=%fused_computation.7 | convolution fusion | flops 8413184000 | bytes 37519360 | tf_op jit(solution)/shard_map/dot_general | solution.py:1182
  520.7 14.8 %convolution_convert_fusion.5 = bf16[800,2560]{1,0:T(8,128)(2,1)} fusion(bf16[2048,800]{0,1:T(8,128)(2,1)} %get-tuple-element.147, bf16[2048,2560]{1,0:T(8,128)(2,1)} %get-tuple-element.81), kind=kOutput, calls=%fused_computation.14 | convolution fusion | flops 8390656000 | bytes 17858560 | tf_op jit(solution)/shard_map/dot_general | solution.py:42
  535.5 13.0 %convolution_convert_fusion.3 = bf16[2560,800]{0,1:T(8,128)(2,1)} fusion(bf16[2048,800]{0,1:T(8,128)(2,1)S(1)} %copy-done.79, bf16[2048,2560]{1,0:T(8,128)(2,1)} %get-tuple-element.77), kind=kOutput, calls=%fused_computation.12 | convolution fusion | flops 8390656000 | bytes 17858560 | tf_op jit(solution)/shard_map/dot_general | solution.py:42
  548.5 10.2 convolution_convert_fusion.4
  558.7 7.2 copy.203
  565.9 7.2 copy.204
  573.1 16.8 %convolution_convert_fusion.1.refs_0_ = bf16[2048,2560]{1,0:T(8,128)(2,1)} fusion(bf16[2048,800]{0,1:T(8,128)(2,1)} %get-tuple-element.147, bf16[800,2560]{1,0:T(8,128)(2,1)} %bitcast.203), kind=kOutput, calls=%fused_computation.4 | convolution fusion | flops 8393850880 | bytes 17858560 | tf_op jit(solution)/shard_map/dot_general | solution.py:1196
  589.9 14.2 %fusion.109 = f32[2048,2560]{1,0:T(8,128)} fusion(bf16[2048,800]{0,1:T(8,128)(2,1)S(1)} %copy-done.80, bf16[2560,800]{1,0:T(8,128)(2,1)S(1)} %bitcast.199), kind=kOutput, calls=%fused_computation.255 | convolution fusion | flops 8388608000 | bytes 28344320 | tf_op jit(solution)/shard_map/dot_general | solution.py:36
  604.1 19.7 %add_convert_fusion.refs_0_ = bf16[2048,2560]{1,0:T(8,128)(2,1)} fusion(f32[2048,2560]{1,0:T(8,128)} %fusion.109, bf16[2048,800]{0,1:T(8,128)(2,1)} %copy-done.78, bf16[2560,800]{1,0:T(8,128)(2,1)} %bitcast.201), kind=kOutput, calls=%fused_computation | convolution fusion | flops 8399093760 | bytes 38830080 | tf_op jit(solution)/shard_map/dot_general | solution.py:36
  623.7 72.2 %shard_map.514 = (f32[256,2560]{1,0:T(8,128)}, bf16[3,200,2560]{2,1,0:T(8,128)(2,1)}) custom-call(bf16[2048,2560]{1,0:T(8,128)(2,1)} %add_convert_fusion.refs_0_, bf16[4,200,2560]{2,1,0:T(8,128)(2,1)} %bitcast.164), custom_call_target="tpu_custom_call" | custom-call | bytes 268435456 | tf_op jit(solution)/shard_map/pallas_call | solution.py:709
  703.6 4.8 multiply_subtract_fusion
  708.4 78.6 %shard_map.515 = (bf16[2048,2560]{1,0:T(8,128)(2,1)}, bf16[3,4,160,800]{3,2,1,0:T(8,128)(2,1)}) custom-call(bf16[256,2560]{1,0:T(8,128)(2,1)} %multiply_convert_fusion.3.refs_0_, bf16[4,4,160,800]{3,2,1,0:T(8,128)(2,1)} %bitcast.146), custom_call_target="tpu_custom_call" | custom-call | bytes 268435456 | tf_op jit(solution)/shard_map/pallas_call | solution.py:709
  787.1 10.1 convolution_convert_fusion.6.refs_5_
  797.2 89.6 %shard_map.516 = (f32[256,2560]{1,0:T(8,128)}, bf16[3,4,160,800]{3,2,1,0:T(8,128)(2,1)}, bf16[2048,640]{1,0:T(8,128)(2,1)}, bf16[2048,640]{1,0:T(8,128)(2,1)}, bf16[2048,1152]{1,0:T(8,128)(2,1)}) custom-call(bf16[2048,2560]{1,0:T(8,128)(2,1)} %convolution_convert_fusion.1.refs_0_, bf16[4,4,160,800]{3,2,1,0:T(8,128)(2,1)} %bitcast.148, ...), custom_call_target="tpu_custom_call" | custom-call | bytes 268435456 | tf_op jit(solution)/shard_map/pallas_call | solution.py:709
  890.5 5.6 fusion.29
  905.4 36.5 %shard_map.517 = (f32[256,1152]{1,0:T(8,128)}, bf16[3,80,2560]{2,1,0:T(8,128)(2,1)}, bf16[4,160,800]{2,1,0:T(8,128)(2,1)}) custom-call(bf16[2048,1152]{1,0:T(8,128)(2,1)} %get-tuple-element.88.refs_0_, bf16[4,80,2560]{2,1,0:T(8,128)(2,1)} %bitcast.154, bf16[4,160,800]{2,1,0:T(8,128)(2,1)} %fusion.32.refs_2_), custom_call_target="tpu_custom_call" | custom-call | bytes 268435456 | tf_op jit(solution)/shard_map/pallas_call | solution.py:709
  948.6 5.3 fusion.16
  967.4 4.8 reshape.428
  972.1 6.5 multiply_subtract_fusion.2
  982.7 8.6 copy.205
  1004.1 54.1 %shard_map.518 = (f32[384,1056]{1,0:T(8,128)}, bf16[3,4,48,640]{3,2,1,0:T(8,128)(2,1)}, bf16[3,4,16,640]{3,2,1,0:T(8,128)(2,1)}, bf16[4,160,800]{2,1,0:T(8,128)(2,1)}, bf16[80,2560]{1,0:T(8,128)(2,1)}) custom-call(bf16[3072,1056]{1,0:T(8,128)(2,1)} %copy-done.12, bf16[4,4,48,640]{3,2,1,0:T(8,128)(2,1)} %bitcast.183, bf16[4,4,16,640]{3,2,1,0:T(8,128)(2,1)} %bitcast.189, ...), custom_call_target="tpu_custom_call" | custom-call | bytes 268435456 | tf_op jit(solution)/shard_map/pallas_call | solution.py:709
  1064.3 19.6 %shard_map.519 = (bf16[3,96,1056]{2,1,0:T(8,128)(2,1)}, bf16[4,48,640]{2,1,0:T(8,128)(2,1)}, bf16[4,16,640]{2,1,0:T(8,128)(2,1)}) custom-call(bf16[4,96,1056]{2,1,0:T(8,128)(2,1)} %bitcast.170, bf16[4,48,640]{2,1,0:T(8,128)(2,1)} %fusion.62.refs_1_, bf16[4,16,640]{2,1,0:T(8,128)(2,1)} %fusion.84.refs_2_), custom_call_target="tpu_custom_call" | custom-call | bytes 268435456 | tf_op jit(solution)/shard_map/pallas_call | solution.py:709
  1106.1 6.4 multiply_subtract_fusion.1
  (319 shorter events, 150.8 us)
Async XLA Ops:
  0.7 11.3 %copy-start.29 = (f32[48,1920]{1,0:T(8,128)S(1)}, f32[48,1920]{1,0:T(8,128)}, u32[]{:S(2)}) copy-start(f32[48,1920]{1,0:T(8,128)} %param.42) | copy-start | bytes 1105924
  0.8 184.2 %copy-start.69 = (f32[16]{0:T(128)}, f32[16]{0:T(128)S(1)}, u32[]{:S(2)}) copy-start(f32[16]{0:T(128)S(1)} %negate_power_fusion) | copy-start | bytes 196
  4.0 11.2 %copy-start.23 = (f32[80,2560]{1,0:T(8,128)S(1)}, f32[80,2560]{1,0:T(8,128)}, u32[]{:S(2)}) copy-start(f32[80,2560]{1,0:T(8,128)} %param.48) | copy-start | bytes 2457604
  4.0 136.9 %copy-start.59 = (f32[256]{0:T(256)}, f32[256]{0:T(256)S(1)}, u32[]{:S(2)}) copy-start(f32[256]{0:T(256)S(1)} %add_rsqrt_fusion.3) | copy-start | bytes 3076
  5.5 140.5 %copy-start.67 = (f32[256]{0:T(256)}, f32[256]{0:T(256)S(1)}, u32[]{:S(2)}) copy-start(f32[256]{0:T(256)S(1)} %get-tuple-element.177) | copy-start | bytes 3076
  140.9 254.6 %copy-start.41 = (f32[2560]{0:T(1024)}, f32[2560]{0:T(1024)S(1)}, u32[]{:S(2)}) copy-start(f32[2560]{0:T(1024)S(1)} %get-tuple-element.166) | copy-start | bytes 30724
  145.7 34.6 %copy-start.63 = (f32[256]{0:T(256)}, f32[256]{0:T(256)S(1)}, u32[]{:S(2)}) copy-start(f32[256]{0:T(256)S(1)} %add_rsqrt_fusion.1) | copy-start | bytes 3076
  145.9 34.4 %copy-start.65 = (f32[256]{0:T(256)}, f32[256]{0:T(256)S(1)}, u32[]{:S(2)}) copy-start(f32[256]{0:T(256)S(1)} %add_rsqrt_fusion.2) | copy-start | bytes 3076
  192.7 111.3 %copy-start.76 = (bf16[4,80,2560]{2,1,0:T(8,128)(2,1)S(1)}, bf16[4,80,2560]{2,1,0:T(8,128)(2,1)}, u32[]{:S(2)}) copy-start(bf16[4,80,2560]{2,1,0:T(8,128)(2,1)} %get-tuple-element.74) | copy-start | bytes 4915204
  472.6 14.5 %copy-start.75 = (bf16[2048,2560]{1,0:T(8,128)(2,1)S(1)}, bf16[2048,2560]{1,0:T(8,128)(2,1)}, u32[]{:S(2)}) copy-start(bf16[2048,2560]{1,0:T(8,128)(2,1)} %get-tuple-element.77) | copy-start | bytes 31457284
  520.6 27.9 %copy-start.78 = (bf16[2048,800]{0,1:T(8,128)(2,1)}, bf16[2048,800]{0,1:T(8,128)(2,1)S(1)}, u32[]{:S(2)}) copy-start(bf16[2048,800]{0,1:T(8,128)(2,1)S(1)} %get-tuple-element.146) | copy-start | bytes 9830404
  520.6 14.9 %copy-start.79 = (bf16[2048,800]{0,1:T(8,128)(2,1)S(1)}, bf16[2048,800]{0,1:T(8,128)(2,1)}, u32[]{:S(2)}) copy-start(bf16[2048,800]{0,1:T(8,128)(2,1)} %get-tuple-element.145) | copy-start | bytes 9830404
  520.6 27.9 %slice-start.2 = ((s8[10485760]{0:T(1024)(128)(4,1)}), s8[4194304]{0:T(1024)(128)(4,1)S(1)}, s32[]{:S(2)}) async-start(s8[10485760]{0:T(1024)(128)(4,1)} %bitcast.194), calls=%async_computation.2 | async-start | bytes 8388608
  520.6 27.8 %slice-start.3 = ((s8[10485760]{0:T(1024)(128)(4,1)}), s8[4194304]{0:T(1024)(128)(4,1)S(1)}, s32[]{:S(2)}) async-start(s8[10485760]{0:T(1024)(128)(4,1)} %bitcast.194), calls=%async_computation.3 | async-start | bytes 8388608
  535.5 13.0 %slice-start.4 = ((s8[10485760]{0:T(1024)(128)(4,1)}), s8[2097152]{0:T(1024)(128)(4,1)S(1)}, s32[]{:S(2)}) async-start(s8[10485760]{0:T(1024)(128)(4,1)} %bitcast.194), calls=%async_computation.4 | async-start | bytes 4194304
  565.9 24.0 %slice-start.5 = ((s8[4587520]{0:T(1024)(128)(4,1)}), s8[393216]{0:T(1024)(128)(4,1)S(1)}, s32[]{:S(2)}) async-start(s8[4587520]{0:T(1024)(128)(4,1)} %bitcast.197), calls=%async_computation.5 | async-start | bytes 786432
  573.1 16.8 %slice-start.6 = ((s8[4587520]{0:T(1024)(128)(4,1)}), s8[4194304]{0:T(1024)(128)(4,1)S(1)}, s32[]{:S(2)}) async-start(s8[4587520]{0:T(1024)(128)(4,1)} %bitcast.197), calls=%async_computation.6 | async-start | bytes 8388608
  573.1 16.8 %copy-start.80 = (bf16[2048,800]{0,1:T(8,128)(2,1)S(1)}, bf16[2048,800]{0,1:T(8,128)(2,1)}, u32[]{:S(2)}) copy-start(bf16[2048,800]{0,1:T(8,128)(2,1)} %get-tuple-element.145) | copy-start | bytes 9830404
  623.7 72.2 %copy-start.1 = (f32[256,2560]{1,0:T(8,128)S(1)}, f32[256,2560]{1,0:T(8,128)}, u32[]{:S(2)}) copy-start(f32[256,2560]{1,0:T(8,128)} %copy-done) | copy-start | bytes 7864324
  623.7 72.2 %copy-start.42 = (f32[2560]{0:T(1024)S(1)}, f32[2560]{0:T(1024)}, u32[]{:S(2)}) copy-start(f32[2560]{0:T(1024)} %copy-done.41) | copy-start | bytes 30724
  623.7 72.2 %copy-start.58 = (f32[256]{0:T(256)S(1)}, f32[256]{0:T(256)}, u32[]{:S(2)}) copy-start(f32[256]{0:T(256)} %copy-done.57) | copy-start | bytes 3076
  708.4 178.4 %slice-start = ((s8[4718592]{0:T(1024)(128)(4,1)}), s8[4194304]{0:T(1024)(128)(4,1)S(1)}, s32[]{:S(2)}) async-start(s8[4718592]{0:T(1024)(128)(4,1)} %bitcast.150), calls=%async_computation | async-start | bytes 8388608
  787.1 99.8 %slice-start.1 = ((s8[4718592]{0:T(1024)(128)(4,1)}), s8[524288]{0:T(1024)(128)(4,1)S(1)}, s32[]{:S(2)}) async-start(s8[4718592]{0:T(1024)(128)(4,1)} %bitcast.150), calls=%async_computation.1 | async-start | bytes 1048576
  886.9 9.2 copy-start.74
  905.3 36.6 %copy-start.8 = (f32[256,1056]{1,0:T(8,128)S(1)}, f32[256,1056]{1,0:T(8,128)}, u32[]{:S(2)}) copy-start(f32[256,1056]{1,0:T(8,128)} %copy-done.7) | copy-start | bytes 3244036
  905.3 36.6 %copy-start.62 = (f32[256]{0:T(256)S(1)}, f32[256]{0:T(256)}, u32[]{:S(2)}) copy-start(f32[256]{0:T(256)} %copy-done.61) | copy-start | bytes 3076
  905.3 36.6 %copy-start.64 = (f32[256]{0:T(256)S(1)}, f32[256]{0:T(256)}, u32[]{:S(2)}) copy-start(f32[256]{0:T(256)} %copy-done.63) | copy-start | bytes 3076
  905.4 37.8 %copy-start.56 = (f32[768]{0:T(1024)S(1)}, f32[768]{0:T(1024)}, u32[]{:S(2)}) copy-start(f32[768]{0:T(1024)} %copy-done.55) | copy-start | bytes 9220
  905.4 37.8 %copy-start.66 = (f32[256]{0:T(256)S(1)}, f32[256]{0:T(256)}, u32[]{:S(2)}) copy-start(f32[256]{0:T(256)} %copy-done.65) | copy-start | bytes 3076
  1062.4 22.5 %copy-start.36 = (f32[16,2560]{1,0:T(8,128)S(1)}, f32[16,2560]{1,0:T(8,128)}, u32[]{:S(2)}) copy-start(f32[16,2560]{1,0:T(8,128)} %param.45) | copy-start | bytes 491524
  1062.4 22.5 %copy-start.51 = (f32[16,2560]{1,0:T(8,128)S(1)}, f32[16,2560]{1,0:T(8,128)}, u32[]{:S(2)}) copy-start(f32[16,2560]{1,0:T(8,128)} %param.46) | copy-start | bytes 491524
  1062.4 22.5 %copy-start.52 = (f32[16,2560]{1,0:T(8,128)S(1)}, f32[16,2560]{1,0:T(8,128)}, u32[]{:S(2)}) copy-start(f32[16,2560]{1,0:T(8,128)} %param.47) | copy-start | bytes 491524
  (56 other events, 199.8 us)

commit v2 on v1

--- a/solution.py
+++ b/solution.py
@@ -101,7 +101,7 @@
 
 PLANE = 4
 LINE = 4
-LINK = 1e5
+LINK = 8.4e4
 MESH = pl.DeviceIdType.MESH
 VMEM_LIMIT = 56 * 1024 * 1024
 HBM_SPEC = pl.BlockSpec(memory_space=pl.ANY)
@@ -114,6 +114,7 @@
         self.remotes = 0
         self.locals = 0
         self.closing = []
+        self.here = set()
         self.d = lax.axis_index("dp")
         self.t = lax.axis_index("tensor")
         self.z = self.d // PLANE
@@ -200,9 +201,13 @@
     return ((core * 2 + x) * 2 + y) * 2 + half
 
 
+def octet_unit(shape):
+    return 2.0 * math.prod(shape) / LINK
+
+
 def octet_gather_steps(board, own_ref, all_ref, begin=0.0):
     h = own_ref.shape[0] // 2
-    unit = 2.2 * math.prod(own_ref.shape) / LINK
+    unit = octet_unit(own_ref.shape)
 
     def rows(place, count=1):
         return all_ref.at[pl.ds(place * h, count * h)]
@@ -213,34 +218,45 @@
     second_y = board.send(second, rows(octet_place(0, 0, 1, 1)), along_y)
     first_y = board.send(first, rows(octet_place(0, 0, 1, 0)), along_y)
     second_x = board.send(second, rows(octet_place(0, 1, 0, 1)), along_x)
-    arrivals = [board.send(own_ref, rows(octet_place(1, 0, 0, 0), 2), core)]
+    whole_core = board.send(own_ref, rows(octet_place(1, 0, 0, 0), 2), core)
     board.move(own_ref, rows(0, 2))
 
-    def onward(place, name):
-        source = rows(octet_place(*place[0]))
-        return board.send(source, rows(octet_place(*place[1])), name)
-
+    def onward(start, end, name):
+        return board.send(rows(octet_place(*start)), rows(octet_place(*end)), name)
+
+    def to_core(*place):
+        return onward((0,) + place, (1,) + place, core)
+
+    yield begin + 0.25 * unit
+    whole_core.wait_recv()
+    board.here.add((1, 0, 0))
     yield begin + unit
     first_x.wait_recv()
-    first_xy = onward(((0, 1, 0, 0), (0, 1, 1, 0)), along_y)
-    arrivals.append(onward(((0, 1, 0, 0), (1, 1, 0, 0)), core))
+    first_xy = onward((0, 1, 0, 0), (0, 1, 1, 0), along_y)
+    core_x = [to_core(1, 0, 0)]
     second_y.wait_recv()
-    second_xy = onward(((0, 0, 1, 1), (0, 1, 1, 1)), along_x)
-    arrivals.append(onward(((0, 0, 1, 1), (1, 0, 1, 1)), core))
-    for n, (copy, place) in enumerate(
-        (
-            (first_y, (1, 0, 1, 0)),
-            (second_x, (1, 1, 0, 1)),
-            (first_xy, (1, 1, 1, 0)),
-            (second_xy, (1, 1, 1, 1)),
-        )
-    ):
-        yield begin + unit * (2 + n // 2)
+    second_xy = onward((0, 0, 1, 1), (0, 1, 1, 1), along_x)
+    core_y = [to_core(0, 1, 1)]
+    yield begin + 2.0 * unit
+    first_y.wait_recv()
+    core_y.append(to_core(0, 1, 0))
+    second_x.wait_recv()
+    core_x.append(to_core(1, 0, 1))
+    board.here.update(((0, 0, 1), (0, 1, 0)))
+    yield begin + 2.3 * unit
+    for copy in core_x + core_y:
         copy.wait_recv()
-        arrivals.append(onward(((0,) + place[1:], place), core))
-    yield begin + unit * 3.1
-    for copy in arrivals:
+    board.here.update(((1, 0, 1), (1, 1, 0)))
+    yield begin + 3.0 * unit
+    first_xy.wait_recv()
+    core_xy = [to_core(1, 1, 0)]
+    second_xy.wait_recv()
+    core_xy.append(to_core(1, 1, 1))
+    board.here.add((0, 1, 1))
+    yield begin + 3.3 * unit
+    for copy in core_xy:
         copy.wait_recv()
+    board.here.add((1, 1, 1))
 
 
 def add_rows(target, other):
@@ -270,7 +286,7 @@
 
 def octet_reduce_steps(board, terms_ref, sum_ref, mine, from_core, from_link, begin=0.0):
     h = sum_ref.shape[0] // 2
-    unit = 2.2 * math.prod(sum_ref.shape) / LINK
+    unit = octet_unit(sum_ref.shape)
     core, along_x, along_y = ("plane", 1), ("plane", 2), "y"
     order = (
         (1, 1, 0),
@@ -334,7 +350,7 @@
 
 
 def line_gather_steps(board, shard_ref, whole_ref, begin=0.0):
-    unit = 4.4 * math.prod(shard_ref.shape) / LINK
+    unit = 4.0 * math.prod(shard_ref.shape) / LINK
     z = board.z
     far, near = board.line_xor(2), ("line", 1)
     two = board.send(shard_ref, whole_ref.at[z], ("line", 2))
@@ -350,17 +366,14 @@
         device_id_type=MESH,
     )
 
-    @pl.when(board.middle)
-    def _():
-        three.start()
-
     keep = board.move(shard_ref, whole_ref.at[z], close=False)
-    yield begin + 2.0 * unit
+    yield begin + 1.9 * unit
     two.wait_recv()
 
     @pl.when(board.middle)
     def _():
         onward.start()
+        three.start()
 
     yield begin + 3.1 * unit
     keep.wait()
@@ -374,7 +387,7 @@
 
 
 def line_reduce_steps(board, terms_ref, got_ref, held, carried, begin=0.0):
-    unit = 4.4 * math.prod(got_ref.shape[1:]) / LINK
+    unit = 4.0 * math.prod(got_ref.shape[1:]) / LINK
     near, two_off, three_off = ("line", 1), ("line", 2), ("line", 3)
     z_near, z_two, z_three = (board.line_xor(k) for k in (1, 2, 3))
     carry = board.make(board.slot(), terms_ref.at[z_three], carried, near)
@@ -383,19 +396,26 @@
     two_end = board.make(two_slot, terms_ref.at[z_two], got_ref.at[1], two_off)
     two_mid = board.make(two_slot, held, got_ref.at[1], two_off)
 
+    one = board.make(board.slot(), terms_ref.at[z_near], got_ref.at[0], near)
+
     @pl.when(jnp.logical_not(board.middle))
     def _():
         carry.start()
-        two_end.start()
 
     @pl.when(board.middle)
     def _():
+        one.start()
         direct.start()
 
-    one = board.send(terms_ref.at[z_near], got_ref.at[0], near)
     load = board.move(terms_ref.at[z_two], held, close=False)
-    yield begin + 1.3 * unit
+    yield begin + 1.05 * unit
     load.wait()
+
+    @pl.when(jnp.logical_not(board.middle))
+    def _():
+        carry.wait_send()
+        two_end.start()
+        one.start()
 
     @pl.when(board.middle)
     def _():
@@ -405,6 +425,7 @@
 
     yield begin + 3.1 * unit
     one.wait_recv()
+    one.wait_send()
     two_end.wait_recv()
     two_end.wait_send()
 
@@ -412,10 +433,6 @@
     def _():
         direct.wait_recv()
         direct.wait_send()
-
-    @pl.when(jnp.logical_not(board.middle))
-    def _():
-        carry.wait_send()
 
 
 def plane_exchange_steps(board, blocks_ref, given_ref, begin=0.0):
@@ -631,6 +648,25 @@
         if self.back:
             pairs = [(b, a) for a, b in pairs]
         return lax.ppermute(self.given, "dp", pairs)
+
+
+class GatherMoved(Transpose):
+    near, remotes, moves = ("transposed",) + NEAR_LINE, 5, 2
+
+    def __init__(self, shard):
+        super().__init__(shard)
+        self.outs = [hbm(shard.shape), hbm((LINE,) + shard.shape)]
+
+    def steps(self, board, shard, outs, scratch):
+        begin = 9.0 * math.prod(shard.shape) / LINK
+        yield from transpose_steps(board, shard, outs[0])
+        yield from line_gather_steps(board, outs[0], outs[1], begin)
+
+    def read(self, outs):
+        return outs[1]
+
+    def plain(self):
+        return LineGather(super().plain()).plain()
 
 
 def communicate(collective_id, *tasks, compute=None):
@@ -657,6 +693,8 @@
     more_givens = compute.givens if compute else []
     more_outs = compute.outs if compute else []
     more_scratch = compute.scratch if compute else []
+    more_given_specs = compute.given_specs if compute else []
+    more_out_specs = compute.out_specs if compute else []
 
     def kernel(*refs):
         refs = list(refs)
@@ -684,13 +722,18 @@
             running.append((next(steps), n, steps))
         phases = []
         if compute:
-            phases = compute.phases(compute_givens, compute_outs, compute_scratch)
-        done = 0.0
+            phases = compute.phases(
+                compute_givens,
+                compute_outs,
+                compute_scratch,
+                board if tasks else None,
+                givens,
+                outs,
+            )
         while running or phases:
             running.sort(key=lambda item: item[:2])
-            if phases and not (running and running[0][0] <= done):
-                phases.pop(0)()
-                done += compute.phase_time
+            if phases and not (running and running[0][0] <= phases[0][0]):
+                phases.pop(0)[1]()
                 continue
             when, n, steps = running.pop(0)
             when = next(steps, None)
@@ -709,9 +752,9 @@
     outs = pl.pallas_call(
         kernel,
         out_shape=[shape for task in tasks for shape, _ in task.outs] + more_outs,
-        in_specs=[HBM_SPEC] * len(tasks) + [VMEM_SPEC] * len(more_givens),
+        in_specs=[HBM_SPEC] * len(tasks) + more_given_specs,
         out_specs=[spec for task in tasks for _, spec in task.outs]
-        + [VMEM_SPEC] * len(more_outs),
+        + more_out_specs,
         scratch_shapes=[shape for task in tasks for shape in task.scratch]
         + more_scratch
         + sems,
@@ -751,7 +794,7 @@
 
 
 HEAD = 128
-ROW_BLOCK = 256
+ROW_BLOCK = 64
 
 
 def column_dot(left_side, right_side):
@@ -796,71 +839,72 @@
         ]
         self.scratch = [
             pltpu.VMEM((self.pack_rows, self.pack_rows), jnp.float32),
-            pltpu.VMEM((self.pack_rows, HEAD), low),
+            pltpu.VMEM((self.pack_rows, heads * HEAD), jnp.float32),
+            pltpu.VMEM((self.pack_rows, self.pack_rows), jnp.float32),
+            pltpu.VMEM((self.pack_rows, self.pack_rows), low),
         ]
-        self.phase_time = 10.0
-
-    def phases(self, givens, outs, scratch):
+        self.phase_time = 12.0
+        self.given_specs = [VMEM_SPEC] * len(self.givens)
+        self.out_specs = [VMEM_SPEC] * len(self.outs)
+
+    def phases(self, givens, outs, scratch, board, task_givens, task_outs):
         tokens, keys, bounds, wave, low_wave, high_wave, query_up, latent_up = givens
         queries, heads_out, mixed, totals = outs
-        bias, keys_tile = scratch
+        bias, raw, held, prob_low = scratch
         scale = QH ** (-0.5)
         size = self.pack_rows
 
         def run(pack):
             score_bias(keys, bounds, bias, pack, size)
             start = pack * size
-            rope_key = tokens[start : start + size, QR + KVR : QR + KVR + HEAD]
+            whole = slice(start, start + size)
+            rope_key = pltpu.roll(
+                tokens[whole, QR + KVR : QR + KVR + HEAD].astype(jnp.float32), DN, 1
+            )
             for n in range(self.pairs):
-                mixed[start : start + size, n * HEAD : (n + 1) * HEAD] = jnp.zeros(
-                    (size, HEAD), mixed.dtype
-                )
-            totals[start : start + size, :] = jnp.zeros((size, HEAD), jnp.float32)
+                mixed[whole, n * HEAD : (n + 1) * HEAD] = jnp.zeros((size, HEAD), mixed.dtype)
+            totals[whole, :] = jnp.zeros((size, HEAD), jnp.float32)
+            heads_out[whole, :] = column_dot(
+                tokens[whole, QR : QR + KVR], latent_up[...]
+            ).astype(jnp.bfloat16)
+            raw[...] = column_dot(tokens[whole, 0:QR], query_up[...])
 
             @pl.loop(0, self.heads)
             def _(head):
                 lanes = pl.ds(pl.multiple_of(head * HEAD, HEAD), HEAD)
                 pair = pl.ds(pl.multiple_of((head // 2) * HEAD, HEAD), HEAD)
-                tile = column_dot(
-                    tokens[start : start + size, QR : QR + KVR], latent_up[:, lanes]
+                even = head % 2 == 0
+                tile = heads_out[whole, lanes]
+                key_all = jnp.where(
+                    lane_index((size, HEAD)) < DN, tile.astype(jnp.float32), rope_key
                 ).astype(jnp.bfloat16)
-                heads_out[start : start + size, lanes] = tile
-                lane = lane_index((size, HEAD))
-                keys_tile[...] = jnp.where(
-                    lane < DN,
-                    tile.astype(jnp.float32),
-                    pltpu.roll(rope_key.astype(jnp.float32), DN, 1),
+                query_all = turn(
+                    raw[:, lanes], wave[whole, :], low_wave[whole, :], high_wave[whole, :]
                 ).astype(jnp.bfloat16)
-
-                @pl.loop(0, size // ROW_BLOCK)
-                def _(block):
-                    at = pl.multiple_of(start + block * ROW_BLOCK, ROW_BLOCK)
-                    rows = pl.ds(at, ROW_BLOCK)
-                    raw = column_dot(tokens[rows, 0:QR], query_up[:, lanes])
-                    query = turn(
-                        raw, wave[rows, :], low_wave[rows, :], high_wave[rows, :]
-                    ).astype(jnp.bfloat16)
-                    queries[rows, lanes] = query
-                    scores = right_transposed(query, keys_tile[...]) * scale + bias[
-                        pl.ds(pl.multiple_of(block * ROW_BLOCK, ROW_BLOCK), ROW_BLOCK), :
-                    ]
+                queries[whole, lanes] = query_all
+                held[...] = right_transposed(query_all, key_all)
+                for block in range(size // ROW_BLOCK):
+                    part = slice(block * ROW_BLOCK, (block + 1) * ROW_BLOCK)
+                    rows = slice(start + block * ROW_BLOCK, start + (block + 1) * ROW_BLOCK)
+                    scores = held[part, :] * scale + bias[part, :]
                     top = jnp.max(scores, axis=1, keepdims=True)
                     exponent = jnp.exp(scores - top)
                     total = jnp.sum(exponent, axis=1, keepdims=True)
-                    prob = (exponent * (1.0 / total)).astype(jnp.bfloat16)
-                    out = column_dot(prob, heads_out[start : start + size, lanes])
-                    lane = lane_index((ROW_BLOCK, HEAD))
+                    prob_low[part, :] = (exponent * (1.0 / total)).astype(jnp.bfloat16)
                     totals[rows, :] = jnp.where(
-                        lane == head, top + jnp.log(total), totals[rows, :]
+                        lane_index((ROW_BLOCK, HEAD)) == head,
+                        top + jnp.log(total),
+                        totals[rows, :],
                     )
-                    even = head % 2 == 0
-                    placed = jnp.where(even, pltpu.roll(out, DN, 1), out)
-                    before = mixed[rows, pair].astype(jnp.float32)
-                    mixed[rows, pair] = jnp.where(
-                        (lane < DN) == even, placed, before
-                    ).astype(mixed.dtype)
-
-        return [functools.partial(run, pack) for pack in range(self.packs)]
+                out = column_dot(prob_low[...], tile)
+                lane = lane_index((size, HEAD))
+                placed = jnp.where(even, pltpu.roll(out, DN, 1), out)
+                before = mixed[whole, pair].astype(jnp.float32)
+                mixed[whole, pair] = jnp.where((lane < DN) == even, placed, before).astype(
+                    mixed.dtype
+                )
+
+        return [(self.phase_time * n, functools.partial(run, n)) for n in range(self.packs)]
 
 
 class AttentionBackward:
@@ -902,14 +946,17 @@
         size = self.pack_rows
         self.scratch = [
             pltpu.VMEM((size, size), jnp.float32),
-            pltpu.VMEM((size, HEAD), low),
-            pltpu.VMEM((size, HEAD), jnp.float32),
-            pltpu.VMEM((size, HEAD), jnp.float32),
+            pltpu.VMEM((size, size), jnp.float32),
+            pltpu.VMEM((size, size), jnp.float32),
+            pltpu.VMEM((size, size), low),
+            pltpu.VMEM((size, size), low),
             pltpu.VMEM((size, HEAD), jnp.float32),
         ]
-        self.phase_time = 14.0
-
-    def phases(self, givens, outs, scratch):
+        self.phase_time = 16.0
+        self.given_specs = [VMEM_SPEC] * len(self.givens)
+        self.out_specs = [VMEM_SPEC] * len(self.outs)
+
+    def phases(self, givens, outs, scratch, board, task_givens, task_outs):
         (
             queries,
             heads_in,
@@ -925,80 +972,256 @@
             latent_up,
         ) = givens
         grad_queries, grad_heads, terms = outs
-        bias, keys_tile, grad_key, grad_value, grad_rope = scratch
+        bias, held, grad_held, prob_low, score_low, grad_rope = scratch
         scale = QH ** (-0.5)
         size = self.pack_rows
 
         def run(pack):
             score_bias(keys, bounds, bias, pack, size)
             start = pack * size
-            rope_key = tokens[start : start + size, QR + KVR : QR + KVR + HEAD]
+            whole = slice(start, start + size)
+            rope_key = pltpu.roll(
+                tokens[whole, QR + KVR : QR + KVR + HEAD].astype(jnp.float32), DN, 1
+            )
             grad_rope[...] = jnp.zeros_like(grad_rope)
 
             @pl.loop(0, self.heads)
             def _(head):
                 lanes = pl.ds(pl.multiple_of(head * HEAD, HEAD), HEAD)
                 pair = pl.ds(pl.multiple_of((head // 2) * HEAD, HEAD), HEAD)
+                even = head % 2 == 0
                 lane = lane_index((size, HEAD))
-                keys_tile[...] = jnp.where(
-                    lane < DN,
-                    heads_in[start : start + size, lanes].astype(jnp.float32),
-                    pltpu.roll(rope_key.astype(jnp.float32), DN, 1),
+                tile = heads_in[whole, lanes]
+                query_all = queries[whole, lanes]
+                key_all = jnp.where(lane < DN, tile.astype(jnp.float32), rope_key).astype(
+                    jnp.bfloat16
+                )
+                grad_pair = grad_mixed[whole, pair].astype(jnp.float32)
+                grad_out = jnp.where(
+                    lane < DN, 0.0, jnp.where(even, pltpu.roll(grad_pair, DN, 1), grad_pair)
                 ).astype(jnp.bfloat16)
-                grad_key[...] = jnp.zeros_like(grad_key)
-                grad_value[...] = jnp.zeros_like(grad_value)
-
-                @pl.loop(0, size // ROW_BLOCK)
-                def _(block):
-                    at = pl.multiple_of(start + block * ROW_BLOCK, ROW_BLOCK)
-                    rows = pl.ds(at, ROW_BLOCK)
-                    lane = lane_index((ROW_BLOCK, HEAD))
-                    query = queries[rows, lanes]
-                    key_all = keys_tile[...]
-                    scores = right_transposed(query, key_all) * scale + bias[
-                        pl.ds(pl.multiple_of(block * ROW_BLOCK, ROW_BLOCK), ROW_BLOCK), :
-                    ]
-                    total = jnp.sum(
-                        jnp.where(lane == head, totals[rows, :], 0.0), axis=1, keepdims=True
-                    )
-                    prob = jnp.exp(scores - total)
-                    grad_pair = grad_mixed[rows, pair].astype(jnp.float32)
-                    even = head % 2 == 0
-                    grad_out = jnp.where(
-                        lane < DN, 0.0, jnp.where(even, pltpu.roll(grad_pair, DN, 1), grad_pair)
-                    ).astype(jnp.bfloat16)
-                    grad_prob = right_transposed(grad_out, heads_in[start : start + size, lanes])
+                total_all = jnp.sum(
+                    jnp.where(lane == head, totals[whole, :], 0.0), axis=1, keepdims=True
+                )
+                held[...] = right_transposed(query_all, key_all)
+                grad_held[...] = right_transposed(grad_out, tile)
+                for block in range(size // ROW_BLOCK):
+                    part = slice(block * ROW_BLOCK, (block + 1) * ROW_BLOCK)
+                    prob = jnp.exp(held[part, :] * scale + bias[part, :] - total_all[part])
+                    grad_prob = grad_held[part, :]
                     inner = jnp.sum(prob * grad_prob, axis=1, keepdims=True)
-                    grad_score = (prob * (grad_prob - inner)).astype(jnp.bfloat16)
-                    grad_value[...] += left_transposed(prob.astype(jnp.bfloat16), grad_out)
-                    grad_key[...] += left_transposed(grad_score, query)
-                    grad_query = column_dot(grad_score, key_all) * scale
-                    grad_queries[rows, lanes] = turn(
-                        grad_query, wave[rows, :], -low_wave[rows, :], -high_wave[rows, :]
-                    ).astype(grad_queries.dtype)
-
-                scaled = grad_key[...] * scale
-                grad_rope[...] += scaled
-                grad_heads[start : start + size, lanes] = jnp.where(
-                    lane < DN, scaled, grad_value[...]
-                ).astype(grad_heads.dtype)
-
-            @pl.loop(0, size // ROW_BLOCK)
-            def _(block):
-                at = pl.multiple_of(start + block * ROW_BLOCK, ROW_BLOCK)
-                rows = pl.ds(at, ROW_BLOCK)
-                here = pl.ds(pl.multiple_of(block * ROW_BLOCK, ROW_BLOCK), ROW_BLOCK)
-                terms[rows, 0:QR] = right_transposed(grad_queries[rows, :], query_up[...]).astype(
-                    terms.dtype
+                    prob_low[part, :] = prob.astype(jnp.bfloat16)
+                    score_low[part, :] = (prob * (grad_prob - inner)).astype(jnp.bfloat16)
+                grad_query = column_dot(score_low[...], key_all) * scale
+                grad_queries[whole, lanes] = turn(
+                    grad_query, wave[whole, :], -low_wave[whole, :], -high_wave[whole, :]
+                ).astype(grad_queries.dtype)
+                grad_value = left_transposed(prob_low[...], grad_out)
+                grad_key = left_transposed(score_low[...], query_all) * scale
+                grad_rope[...] += grad_key
+                grad_heads[whole, lanes] = jnp.where(lane < DN, grad_key, grad_value).astype(
+                    grad_heads.dtype
                 )
-                terms[rows, QR : QR + KVR] = right_transposed(
-                    grad_heads[rows, :], latent_up[...]
-                ).astype(terms.dtype)
-                terms[rows, QR + KVR :] = pltpu.roll(grad_rope[here, :], HEAD - DN, 1).astype(
-                    terms.dtype
+
+            terms[whole, 0:QR] = right_transposed(grad_queries[whole, :], query_up[...]).astype(
+                terms.dtype
+            )
+            terms[whole, QR : QR + KVR] = right_transposed(
+                grad_heads[whole, :], latent_up[...]
+            ).astype(terms.dtype)
+            terms[whole, QR + KVR :] = pltpu.roll(grad_rope[...], HEAD - DN, 1).astype(terms.dtype)
+
+        return [(self.phase_time * n, functools.partial(run, n)) for n in range(self.packs)]
+
+
+class FfnForward:
+    order = (
+        ((0, 0, 0), 0.0),
+        ((1, 0, 0), 0.26),
+        ((0, 0, 1), 2.01),
+        ((0, 1, 0), 2.02),
+        ((1, 0, 1), 2.31),
+        ((1, 1, 0), 2.32),
+        ((0, 1, 1), 3.01),
+        ((1, 1, 1), 3.31),
+    )
+
+    def __init__(self, gate, up, rows, unit):
+        self.givens = [gate, up]
+        self.given_specs = self.out_specs = [HBM_SPEC] * 2
+        depth, units = gate.shape
+        self.rows, self.unit = rows, unit
+        self.outs = [jax.ShapeDtypeStruct((8 * rows, units), jnp.float32)] * 2
+        self.scratch = [
+            pltpu.VMEM((2, depth, units), gate.dtype),
+            pltpu.VMEM((2, rows, depth), gate.dtype),
+            pltpu.VMEM((2, 2, rows, units), jnp.float32),
+            pltpu.SemaphoreType.DMA((2,)),
+            pltpu.SemaphoreType.DMA((2,)),
+            pltpu.SemaphoreType.DMA((2, 2)),
+        ]
+
+    def phases(self, givens, outs, scratch, board, task_givens, task_outs):
+        weights, tokens, staged, weight_sems, token_sems, out_sems = scratch
+        own, gathered = task_givens[0], task_outs[0]
+        loads = [
+            pltpu.make_async_copy(givens[n], weights.at[n], weight_sems.at[n]) for n in range(2)
+        ]
+        for load in loads:
+            load.start()
+        leaving = {}
+
+        def run(step, place):
+            spot = (place[0] * 2 + place[1]) * 2 + place[2]
+            rows = pl.ds(spot * self.rows, self.rows)
+            if spot:
+                assert place in board.here
+            slot = step % 2
+            fetch = pltpu.make_async_copy(
+                gathered.at[rows] if spot else own, tokens.at[slot], token_sems.at[slot]
+            )
+            fetch.start()
+            fetch.wait()
+            for n in range(2):
+                if step == 0:
+                    loads[n].wait()
+                if step >= 2:
+                    leaving.pop((slot, n)).wait()
+                staged[slot, n] = column_dot(tokens[slot], weights[n])
+                copy = pltpu.make_async_copy(
+                    staged.at[slot, n], outs[n].at[rows], out_sems.at[slot, n]
                 )
-
-        return [functools.partial(run, pack) for pack in range(self.packs)]
+                copy.start()
+                leaving[(slot, n)] = copy
+
+        def finish():
+            for copy in leaving.values():
+                copy.wait()
+
+        plan = [
+            (when * self.unit, functools.partial(run, step, place))
+            for step, (place, when) in enumerate(self.order)
+        ]
+        return plan + [(1e9, finish)]
+
+
+class FfnBackward:
+    CHUNK = 256
+
+    def __init__(self, normed, grad_gate, grad_up, hidden, down):
+        self.givens = [normed, grad_gate, grad_up, hidden, down]
+        self.given_specs = [HBM_SPEC] * 5
+        self.out_specs = [HBM_SPEC] * 3
+        rows, depth = normed.shape
+        units = hidden.shape[1]
+        low = normed.dtype
+        self.rows, self.depth, self.units = rows, depth, units
+        self.outs = [jax.ShapeDtypeStruct((depth, units), low)] * 2 + [
+            jax.ShapeDtypeStruct((rows, depth), low)
+        ]
+        self.scratch = [
+            pltpu.VMEM((rows, units), low),
+            pltpu.VMEM((rows, units), low),
+            pltpu.VMEM((units, depth), low),
+            pltpu.SemaphoreType.DMA((3,)),
+        ]
+
+    def phases(self, givens, outs, scratch, board, task_givens, task_outs):
+        normed, grad_gate, grad_up, hidden, down = givens
+        gate_held, up_held, down_held, sems = scratch
+        chunk, rows, units, depth = self.CHUNK, self.rows, self.units, self.depth
+        loads = [
+            pltpu.make_async_copy(source, target, sems.at[n])
+            for n, (source, target) in enumerate(
+                ((grad_gate, gate_held), (grad_up, up_held), (down, down_held))
+            )
+        ]
+        for load in loads:
+            load.start()
+
+        def gradients(first, count):
+            if first == 0:
+                loads[0].wait()
+                loads[1].wait()
+
+            def body(normed_part, gate_part, up_part):
+                left = normed_part[...]
+                gate_part[...] = left_transposed(left, gate_held[...]).astype(gate_part.dtype)
+                up_part[...] = left_transposed(left, up_held[...]).astype(up_part.dtype)
+
+            pltpu.emit_pipeline(
+                body,
+                grid=(count,),
+                in_specs=[pl.BlockSpec((rows, chunk), lambda n: (0, n + first))],
+                out_specs=[pl.BlockSpec((chunk, units), lambda n: (n + first, 0))] * 2,
+            )(normed, outs[0], outs[1])
+
+        def products(first, count):
+            if first == 0:
+                loads[2].wait()
+
+            def body(hidden_part, out_part):
+                out_part[...] = column_dot(hidden_part[...], down_held[...]).astype(out_part.dtype)
+
+            pltpu.emit_pipeline(
+                body,
+                grid=(count,),
+                in_specs=[pl.BlockSpec((chunk, units), lambda n: (n + first, 0))],
+                out_specs=[pl.BlockSpec((chunk, depth), lambda n: (n + first, 0))],
+            )(hidden, outs[2])
+
+        plan = []
+        when = 8.0
+        for first in range(0, depth // chunk, 2):
+            plan.append((when, functools.partial(gradients, first, 2)))
+            when += 6.0
+        for first in range(0, rows // chunk, 2):
+            plan.append((when, functools.partial(products, first, 2)))
+            when += 4.0
+        return plan
+
+
+class UnitUpdate:
+    def __init__(self, parts, weight, first_moment, second_moment, line):
+        self.givens = [parts, weight, first_moment, second_moment]
+        self.given_specs, self.out_specs = [VMEM_SPEC] * 4, [VMEM_SPEC] * 3
+        self.outs = [jax.ShapeDtypeStruct(weight.shape, jnp.float32)] * 3
+        self.scratch = []
+        self.line = line
+
+    def phases(self, givens, outs, scratch, board, task_givens, task_outs):
+        parts, weight, first_moment, second_moment = givens
+        rows, columns = weight.shape
+        width = columns // (PLANE * self.line)
+        step_rows = 16 if rows % 16 == 0 else rows
+
+        def run(half):
+            count = rows // step_rows
+            split = (0, count // 2, count)
+
+            @pl.loop(split[half], split[half + 1])
+            def _(step):
+                here = pl.ds(pl.multiple_of(step * step_rows, step_rows), step_rows)
+                pieces = [parts[i, here, :].astype(jnp.float32) for i in range(PLANE)]
+                gradient = jnp.concatenate(
+                    [
+                        pieces[i][:, z * width : (z + 1) * width]
+                        for z in range(self.line)
+                        for i in range(PLANE)
+                    ],
+                    axis=1,
+                )
+                results = adamw_update(
+                    weight[here, :],
+                    first_moment[here, :],
+                    second_moment[here, :],
+                    gradient,
+                    matrix_rate(D),
+                )
+                for out, result in zip(outs, results):
+                    out[here, :] = result
+
+        return [(8.0, functools.partial(run, 0)), (14.0, functools.partial(run, 1))]
 
 
 def positions(segment_ids):
@@ -1087,13 +1310,14 @@
         blocks = jnp.pad(blocks, ((0, 0), (0, 0), (0, 0), (0, HEAD - QH)))
         return blocks.reshape(-1, PLANE, local_heads * HEAD).transpose(1, 0, 2)
 
-    pack_all, query_up_all, latent_up_all, gate_plane, output_moved = communicate(
+    down_low = down_proj.astype(low)
+    pack_all, query_up_all, latent_up_all, gate_plane, down_first = communicate(
         1,
         GatherPack(down_pack),
         GatherColumns(head_blocks(query_up)),
         GatherColumns(column_blocks(latent_up, local_heads * KH)),
         PlaneExchange(unit_blocks(gate_proj)),
-        Transpose(output_proj.astype(low)),
+        LineGather(down_low[:, : D // 2]),
     )
     query_up_all = query_up_all.reshape(QR, local_heads * HEAD)
     latent_up_all = latent_up_all.reshape(KVR, local_heads * KH)
@@ -1139,7 +1363,9 @@
         ],
         axis=1,
     )
-    tokens_all, output_all = communicate(3, OctetGather(tokens_own), LineGather(output_moved))
+    tokens_all, output_all = communicate(
+        3, OctetGather(tokens_own), GatherMoved(output_proj.astype(low))
+    )
     output_all = jnp.pad(
         output_all.reshape(local_heads * DV, D), ((0, mixed_width - local_heads * DV), (0, 0))
     )
@@ -1175,12 +1401,19 @@
     residual = incoming + RESIDUAL * attention_sum
 
     ffn_unit, inverse_ffn = norm_forward(residual, gain_ffn)
-    normed_ffn, down_all = communicate(
-        5, OctetGather(ffn_unit.astype(low)), LineGather(down_proj.astype(low))
-    )
-    down_all = down_all.reshape(units, D)
-    gate_value = jnp.dot(normed_ffn, gate_all, preferred_element_type=jnp.float32)
-    up_value = jnp.dot(normed_ffn, up_all, preferred_element_type=jnp.float32)
+    normed_own = ffn_unit.astype(low)
+    tasks = (OctetGather(normed_own), LineGather(down_low[:, D // 2 :]))
+    if line == LINE:
+        normed_ffn, down_second, (gate_value, up_value) = communicate(
+            5,
+            *tasks,
+            compute=FfnForward(gate_all, up_all, half_rows, octet_unit((half_rows, D))),
+        )
+    else:
+        normed_ffn, down_second = communicate(5, *tasks)
+        gate_value = jnp.dot(normed_ffn, gate_all, preferred_element_type=jnp.float32)
+        up_value = jnp.dot(normed_ffn, up_all, preferred_element_type=jnp.float32)
+    down_all = jnp.concatenate([down_first, down_second], axis=2).reshape(units, D)
     gate_sigmoid = lax.logistic(gate_value)
     silu_gate = gate_value * gate_sigmoid
     hidden = (silu_gate * up_value).astype(low)
@@ -1191,11 +1424,11 @@
     grad_up = (grad_hidden * silu_gate).astype(low)
     ffn_back_terms = right_transposed(grad_gate, gate_all) + right_transposed(grad_up, up_all)
     down_grad = left_transposed(hidden, grad_ffn).astype(low).reshape(line, -1, D)
-    gate_grad = left_transposed(normed_ffn, grad_gate).astype(low)
-    up_grad = left_transposed(normed_ffn, grad_up).astype(low)
-    ffn_terms = jnp.dot(hidden, down_all, preferred_element_type=jnp.float32).astype(low)
-    grad_normed_ffn, down_shard = communicate(
-        6, OctetReduce(ffn_back_terms.astype(low)), LineReduce(down_grad)
+    grad_normed_ffn, down_shard, (gate_grad, up_grad, ffn_terms) = communicate(
+        6,
+        OctetReduce(ffn_back_terms.astype(low)),
+        LineReduce(down_grad),
+        compute=FfnBackward(normed_ffn, grad_gate, grad_up, hidden, down_all),
     )
     outer_grad = cotangent.astype(jnp.float32)
     grad_incoming_ffn, gain_ffn_grad = norm_backward(
@@ -1214,10 +1447,11 @@
         .reshape(line, -1, D)
     )
     grad_mixed = right_transposed(grad_branch, output_all).astype(low)
-    ffn_sum, up_sum, (grad_query_heads, grad_latent_heads, grad_unit_terms) = communicate(
+    ffn_sum, up_sum, gate_parts, (grad_query_heads, grad_latent_heads, grad_unit_terms) = communicate(
         8,
         OctetReduce(ffn_terms),
         LineReduce(up_grad.reshape(line, PLANE, -1, units)),
+        PlaneExchange(gate_sum.astype(low)),
         compute=AttentionBackward(
             queries,
             latent_heads,
@@ -1236,11 +1470,12 @@
     block_output = (residual + RESIDUAL * ffn_sum).astype(low)
     query_up_grad = left_transposed(tokens_all[:, :QR], grad_query_heads).astype(low)
     latent_up_grad = left_transposed(tokens_all[:, QR : QR + KVR], grad_latent_heads).astype(low)
-    grad_units, output_sum, gate_parts = communicate(
+    grad_units, output_sum, up_parts, gate_out = communicate(
         9,
         OctetReduce(grad_unit_terms),
         LineReduce(output_grad),
-        PlaneExchange(gate_sum.astype(low)),
+        PlaneExchange(up_sum.astype(low)),
+        compute=UnitUpdate(gate_parts, gate_proj, gate_proj_first, gate_proj_second, line),
     )
     grad_query_wide, gain_query_grad = norm_backward(
         query_latent, inverse_query, gain_query, grad_units[:, :QR]
@@ -1282,13 +1517,13 @@
         ],
         axis=0,
     )
-    pack_octet, query_up_sum, latent_up_sum, up_parts, output_shard = communicate(
+    pack_octet, query_up_sum, latent_up_sum, output_shard, up_out = communicate(
         10,
         OctetReduce(pack_terms),
         LineReduce(query_up_grad.reshape(line, PLANE, -1, local_heads * HEAD)),
         LineReduce(latent_up_grad.reshape(line, PLANE, -1, local_heads * KH)),
-        PlaneExchange(up_sum.astype(low)),
         Transpose(output_sum.astype(low), back=True),
+        compute=UnitUpdate(up_parts, up_proj, up_proj_first, up_proj_second, line),
     )
     pack_sum, query_up_parts, latent_up_parts = communicate(
         11,
@@ -1300,18 +1535,9 @@
     latent_down_shard = pack_sum[:down_rows, QR:]
     gains_shard = pack_sum[down_rows, :gain_width]
 
-    def unit_columns(blocks):
-        return (
-            blocks.astype(jnp.float32)
-            .reshape(PLANE, -1, line, units // line)
-            .transpose(1, 2, 0, 3)
-            .reshape(-1, PLANE * units)
-        )
-
     def head_columns(blocks):
         return blocks.astype(jnp.float32).transpose(1, 0, 2).reshape(blocks.shape[1], -1)
 
-    gate_shard, up_shard = unit_columns(gate_parts), unit_columns(up_parts)
     query_up_parts = query_up_parts.reshape(PLANE, -1, local_heads, HEAD)[..., :QH]
     query_up_shard = head_columns(query_up_parts.reshape(PLANE, -1, local_heads * QH))
     latent_up_shard = head_columns(latent_up_parts)
@@ -1333,10 +1559,6 @@
     output_out = adamw_update(
         output_proj, output_proj_first, output_proj_second, output_shard, matrix_rate(H * DV // 64)
     )
-    gate_out = adamw_update(
-        gate_proj, gate_proj_first, gate_proj_second, gate_shard, matrix_rate(D)
-    )
-    up_out = adamw_update(up_proj, up_proj_first, up_proj_second, up_shard, matrix_rate(D))
     down_out = adamw_update(
         down_proj, down_proj_first, down_proj_second, down_shard, matrix_rate(FF // 8)
     )

time: 1120 us -> 1060 us (0.946)
  matrix products: 184 us -> 120 us
  Pallas kernels: 741 us -> 776 us
  local copies, waits for them, and re-layouts: 96.3 us -> 71.5 us
    dot_general x3 -> x0, matrix products: 50.3 us -> none  [the longest x1 20.6 us: local(): jnp.dot(normed_ffn, gate_all, preferred_element_type=jnp.float32)]
    pallas_call x11, Pallas kernels: 741 us -> 776 us  [run_kernel(): pl.pallas_call(kernel, out_shape=[shape for task in tasks for shape, _ in...]
    dot_general x7 -> x5, matrix products: 55.7 us -> 29.9 us  [left_transposed(): lax.dot_general(left_side, right_side, (((0,), (0,)), ((), ())), preferre...]
    reshape x6 -> x0, local copies, waits for them, and re-layouts: 22.9 us -> none  [unit_columns(): return blocks.astype(jnp.float32).reshape(PLANE, -1, line, units // line)...]
    convert_element_type x2 -> x0, local copies, waits for them, and re-layouts: 14.4 us -> none  [the longest x1 7.2 us: local(): gate_grad = left_transposed(normed_ffn, grad_gate).astype(low)]
    sub x9 -> x7, other arithmetic: 23.9 us -> 11 us  [adamw_update(): weight - step_rate * (first_hat / (jnp.sqrt(second_hat) + ADAM_EPSILON) +...]
    dot_general x5, matrix products: 63.7 us -> 75.5 us  [right_transposed(): lax.dot_general(left_side, right_side, (((1,), (1,)), ((), ())), preferre...]
where the time goes in v2:
time: 1060 us; the launch traced here: 1050 us
  Pallas kernels  776 us (73%)
  matrix products  120 us (11%)
  other arithmetic  79.7 us (8%)
  local copies, waits for them, and re-layouts  71.5 us (7%)
    pallas_call x11, Pallas kernels, run_kernel(): pl.pallas_call(kernel, out_shape=[shape for task in tasks for shape, _ in...  776 us
    dot_general x5, matrix products, right_transposed(): lax.dot_general(left_side, right_side, (((1,), (1,)), ((), ())), preferre...  75.5 us
    dot_general x5, matrix products, left_transposed(): lax.dot_general(left_side, right_side, (((0,), (0,)), ((), ())), preferre...  29.9 us
    unnamed x177, local copies, waits for them, and re-layouts  22.2 us
    reshape x6, local copies, waits for them, and re-layouts, unit_blocks(): return weight.astype(low).reshape(weight.shape[0], line, PLANE, units //...  21.4 us

profile of v2, /device:TPU:0, one launch (start us, length us, event | category | flops | bytes accessed | tf_op | source)
XLA Modules:
  0.0 1049.6 jit_solution(4823589885083084080)
XLA Ops:
  17.0 5.3 reshape.364
  23.9 3.7 reshape.365.refs_3_
  28.7 5.3 reshape.359
  35.6 3.9 reshape.360.refs_1_
  42.5 93.5 %shard_map.509 = (bf16[4,96,1056]{2,1,0:T(8,128)(2,1)}, bf16[32,96,1056]{2,1,0:T(8,128)(2,1)}, bf16[4,48,640]{2,1,0:T(8,128)(2,1)}, bf16[4,4,48,640]{3,2,1,0:T(8...) custom-call(bf16[96,1056]{1,0:T(8,128)(2,1)} %fusion.61.refs_0_, ...), custom_call_target="tpu_custom_call" | custom-call | bytes 268435456 | tf_op jit(solution)/shard_map/pallas_call | solution.py:752
  144.0 4.6 fusion.53
  150.9 60.4 %shard_map.510 = (bf16[2048,1152]{1,0:T(8,128)(2,1)}, bf16[80,2560]{1,0:T(8,128)(2,1)}, bf16[4,80,2560]{2,1,0:T(8,128)(2,1)}) custom-call(bf16[256,1152]{1,0:T(8,128)(2,1)} %concatenate.48.refs_0_, bf16[80,2560]{1,0:T(8,128)(2,1)} %convert_element_type.202.refs_1_), custom_call_target="tpu_custom_call" | custom-call | bytes 268435456 | tf_op jit(solution)/shard_map/pallas_call | solution.py:752
  216.0 3.7 multiply_sine_fusion
  219.9 3.9 pad_maximum_fusion.1
  223.8 102.3 %shard_map.511 = (bf16[2048,2560]{1,0:T(8,128)(2,1)}, bf16[4,160,800]{2,1,0:T(8,128)(2,1)}, bf16[4,4,160,800]{3,2,1,0:T(8,128)(2,1)}, bf16[2048,640]{1,0:T(8,128...) custom-call(bf16[256,2560]{1,0:T(8,128)(2,1)} %fusion.9.refs_0_, ...), custom_call_target="tpu_custom_call" | custom-call | bytes 268435456 | tf_op jit(solution)/shard_map/pallas_call | solution.py:752
  326.1 9.6 convolution_convert_fusion.1.refs_0_
  335.7 79.6 %shard_map.512 = (f32[256,2560]{1,0:T(8,128)}, bf16[4,4,160,800]{3,2,1,0:T(8,128)(2,1)}) custom-call(bf16[2048,2560]{1,0:T(8,128)(2,1)} %convolution_convert_fusion.1.refs_0_, bf16[4,160,800]{2,1,0:T(8,128)(2,1)} %get-tuple-element.85.refs_1_), custom_call_target="tpu_custom_call" | custom-call | bytes 268435456 | tf_op jit(solution)/shard_map/pallas_call | solution.py:752
  418.9 69.1 %shard_map.513 = (bf16[2048,2560]{1,0:T(8,128)(2,1)}, bf16[4,200,1280]{2,1,0:T(8,128)(2,1)}, f32[2048,800]{1,0:T(8,128)}, f32[2048,800]{1,0:T(8,128)}) custom-call(bf16[256,2560]{1,0:T(8,128)(2,1)} %multiply_convert_fusion.4.refs_0_, bf16[200,1280]{1,0:T(8,128)(2,1)} %get-tuple-element.182.refs_1_, bf16[2560,800]{1,0:T(8,128)(2,1)} %bitcast.158, ...), custom_call_target="tpu_custom_call" | custom-call | bytes 268435456 | tf_op jit(solution)/shard_map/pallas_call | solution.py:752
  488.0 3.8 pad_maximum_fusion
  491.8 23.1 %multiply_convert_fusion = (bf16[2048,800]{1,0:T(8,128)(2,1)}, bf16[2048,800]{1,0:T(8,128)(2,1)}, bf16[2048,800]{1,0:T(8,128)(2,1)}) fusion(f32[2048,800]{1,0:T(8,128)} %get-tuple-element.92, f32[2048,800]{1,0:T(8,128)} %get-tuple-element.93, bf16[2048,2560]{1,0:T(8,128)(2,1)} %get-tuple-element.87, bf16[800,2560]{1,0:T(8,128)(2,1)} %bitcast.136), kind=kOutput, calls=%fused_computation.5 | convolution fusion | flops 8413184000 | bytes 37519360 | tf_op jit(solution)/shard_map/dot_general | solution.py:36
  514.9 14.1 %convolution_convert_fusion.2 = bf16[800,2560]{1,0:T(8,128)(2,1)} fusion(bf16[2048,800]{1,0:T(8,128)(2,1)} %get-tuple-element.161.refs_5_, bf16[2048,2560]{1,0:T(8,128)(2,1)} %get-tuple-element.87), kind=kOutput, calls=%fused_computation.11 | convolution fusion | flops 8390656000 | bytes 17858560 | tf_op jit(solution)/shard_map/dot_general | solution.py:42
  529.1 17.1 %fusion.104 = f32[2048,2560]{1,0:T(8,128)} fusion(bf16[2048,800]{1,0:T(8,128)(2,1)S(1)} %copy-done.18, bf16[2560,800]{1,0:T(8,128)(2,1)} %bitcast.159), kind=kOutput, calls=%fused_computation.244 | convolution fusion | flops 8388608000 | bytes 28344320 | tf_op jit(solution)/shard_map/dot_general | solution.py:36
  546.2 19.4 %add_convert_fusion.refs_0_ = bf16[2048,2560]{1,0:T(8,128)(2,1)} fusion(f32[2048,2560]{1,0:T(8,128)} %fusion.104, bf16[2048,800]{1,0:T(8,128)(2,1)} %get-tuple-element.163.refs_4_, bf16[2560,800]{1,0:T(8,128)(2,1)} %bitcast.161), kind=kOutput, calls=%fused_computation | convolution fusion | flops 8399093760 | bytes 38830080 | tf_op jit(solution)/shard_map/dot_general | solution.py:36
  565.6 77.3 %shard_map.514 = (f32[256,2560]{1,0:T(8,128)}, bf16[3,200,2560]{2,1,0:T(8,128)(2,1)}, bf16[2560,800]{1,0:T(8,128)(2,1)}, bf16[2560,800]{1,0:T(8,128)(2,1)}, bf16[2048,2560]{1,0:T(8,128)(2,1)}) custom-call(bf16[2048,2560]{1,0:T(8,128)(2,1)} %add_convert_fusion.refs_0_, bf16[4,200,2560]{2,1,0:T(8,128)(2,1)} %bitcast.152, ...), custom_call_target="tpu_custom_call" | custom-call | bytes 268435456 | tf_op jit(solution)/shard_map/pallas_call | solution.py:752
  650.6 4.8 multiply_subtract_fusion
  655.4 78.3 %shard_map.515 = (bf16[2048,2560]{1,0:T(8,128)(2,1)}, bf16[3,4,160,800]{3,2,1,0:T(8,128)(2,1)}) custom-call(bf16[256,2560]{1,0:T(8,128)(2,1)} %multiply_convert_fusion.3.refs_0_, bf16[4,4,160,800]{3,2,1,0:T(8,128)(2,1)} %bitcast.142), custom_call_target="tpu_custom_call" | custom-call | bytes 268435456 | tf_op jit(solution)/shard_map/pallas_call | solution.py:752
  733.7 10.6 %convolution_convert_fusion.3.refs_6_ = bf16[2048,384]{1,0:T(8,128)(2,1)} fusion(bf16[2048,2560]{1,0:T(8,128)(2,1)} %get-tuple-element.103, bf16[320,2560]{1,0:T(8,128)(2,1)S(1)} %bitcast.187), kind=kOutput, calls=%fused_computation.26 | convolution fusion | flops 4027318272 | bytes 13697024 | tf_op jit(solution)/shard_map/dot_general | solution.py:36
  744.3 4.5 fusion.105
  753.7 91.8 %shard_map.516 = (f32[256,2560]{1,0:T(8,128)}, bf16[3,4,160,800]{3,2,1,0:T(8,128)(2,1)}, bf16[4,160,800]{2,1,0:T(8,128)(2,1)}, bf16[2048,640]{1,0:T(8,128)(2,1)}...) custom-call(bf16[2048,2560]{1,0:T(8,128)(2,1)} %get-tuple-element.95.refs_0_, bf16[4,4,160,800]{3,2,1,0:T(8,128)(2,1)} %bitcast.140, ...), custom_call_target="tpu_custom_call" | custom-call | bytes 268435456 | tf_op jit(solution)/shard_map/pallas_call | solution.py:752
  845.6 3.6 convolution_convert_fusion.4
  849.2 3.6 fusion.27
  856.3 47.0 %shard_map.517 = (f32[256,1152]{1,0:T(8,128)}, bf16[3,80,2560]{2,1,0:T(8,128)(2,1)}, bf16[4,160,800]{2,1,0:T(8,128)(2,1)}, f32[160,3200]{1,0:T(8,128)}, f32[160,3200]{1,0:T(8,128)}, /*index=5*/f32[160,3200]{1,0:T(8,128)}) custom-call(bf16[2048,1152]{1,0:T(8,128)(2,1)} %get-tuple-element.105.refs_0_, bf16[4,80,2560]{2,1,0:T(8,128)(2,1)} %bitcast.138, ...), custom_call_target="tpu_custom_call" | custom-call | bytes 268435456 | tf_op jit(solution)/shard_map/pallas_call | solution.py:752
  910.0 5.3 fusion.16
  922.1 4.1 convolution_convert_fusion
  926.2 8.6 copy.195
  942.6 57.6 %shard_map.518 = (f32[384,1056]{1,0:T(8,128)}, bf16[3,4,48,640]{3,2,1,0:T(8,128)(2,1)}, bf16[3,4,16,640]{3,2,1,0:T(8,128)(2,1)}, bf16[80,2560]{1,0:T(8,128)(2,1)...) custom-call(bf16[3072,1056]{1,0:T(8,128)(2,1)} %copy-done.11, bf16[4,4,48,640]{3,2,1,0:T(8,128)(2,1)} %bitcast.175, ...), custom_call_target="tpu_custom_call" | custom-call | bytes 268435456 | tf_op jit(solution)/shard_map/pallas_call | solution.py:752
  1006.4 19.2 %shard_map.519 = (bf16[3,96,1056]{2,1,0:T(8,128)(2,1)}, bf16[4,48,640]{2,1,0:T(8,128)(2,1)}, bf16[4,16,640]{2,1,0:T(8,128)(2,1)}) custom-call(bf16[4,96,1056]{2,1,0:T(8,128)(2,1)} %bitcast.162, bf16[4,48,640]{2,1,0:T(8,128)(2,1)} %fusion.60.refs_1_, bf16[4,16,640]{2,1,0:T(8,128)(2,1)} %fusion.82.refs_2_), custom_call_target="tpu_custom_call" | custom-call | bytes 268435456 | tf_op jit(solution)/shard_map/pallas_call | solution.py:752
  (298 shorter events, 108.1 us)
Async XLA Ops:
  0.7 11.3 %copy-start.34 = (f32[48,1920]{1,0:T(8,128)S(1)}, f32[48,1920]{1,0:T(8,128)}, u32[]{:S(2)}) copy-start(f32[48,1920]{1,0:T(8,128)} %param.42) | copy-start | bytes 1105924
  0.8 215.3 %copy-start.70 = (f32[16]{0:T(128)}, f32[16]{0:T(128)S(1)}, u32[]{:S(2)}) copy-start(f32[16]{0:T(128)S(1)} %negate_power_fusion) | copy-start | bytes 196
  4.0 11.2 %copy-start.21 = (f32[80,2560]{1,0:T(8,128)S(1)}, f32[80,2560]{1,0:T(8,128)}, u32[]{:S(2)}) copy-start(f32[80,2560]{1,0:T(8,128)} %param.48) | copy-start | bytes 2457604
  4.0 139.4 %copy-start.60 = (f32[256]{0:T(256)}, f32[256]{0:T(256)S(1)}, u32[]{:S(2)}) copy-start(f32[256]{0:T(256)S(1)} %add_rsqrt_fusion.3) | copy-start | bytes 3076
  5.5 143.6 %copy-start.68 = (f32[256]{0:T(256)}, f32[256]{0:T(256)S(1)}, u32[]{:S(2)}) copy-start(f32[256]{0:T(256)S(1)} %get-tuple-element.195) | copy-start | bytes 3076
  9.6 6.3 copy-start.15
  34.0 5.5 copy-start.12
  143.3 5.6 copy-start.62
  143.3 6.3 copy-start.58
  148.8 62.6 %copy-start.64 = (f32[256]{0:T(256)}, f32[256]{0:T(256)S(1)}, u32[]{:S(2)}) copy-start(f32[256]{0:T(256)S(1)} %add_rsqrt_fusion.1) | copy-start | bytes 3076
  148.9 63.7 %copy-start.66 = (f32[256]{0:T(256)}, f32[256]{0:T(256)S(1)}, u32[]{:S(2)}) copy-start(f32[256]{0:T(256)S(1)} %add_rsqrt_fusion.2) | copy-start | bytes 3076
  223.8 102.3 %copy-start.77 = (bf16[4,80,2560]{2,1,0:T(8,128)(2,1)S(1)}, bf16[4,80,2560]{2,1,0:T(8,128)(2,1)}, u32[]{:S(2)}) copy-start(bf16[4,80,2560]{2,1,0:T(8,128)(2,1)} %get-tuple-element.84) | copy-start | bytes 4915204
  335.7 79.6 %copy-start.1 = (bf16[256,2560]{1,0:T(8,128)(2,1)S(1)}, bf16[256,2560]{1,0:T(8,128)(2,1)}, u32[]{:S(2)}) copy-start(bf16[256,2560]{1,0:T(8,128)(2,1)} %param.30) | copy-start | bytes 3932164
  418.9 69.1 %copy-start.33 = (bf16[4,200,1280]{2,1,0:T(8,128)(2,1)S(1)}, bf16[4,200,1280]{2,1,0:T(8,128)(2,1)}, u32[]{:S(2)}) copy-start(bf16[4,200,1280]{2,1,0:T(8,128)(2,1)} %get-tuple-element.88) | copy-start | bytes 6144004
  514.9 14.1 %copy-start.18 = (bf16[2048,800]{1,0:T(8,128)(2,1)S(1)}, bf16[2048,800]{1,0:T(8,128)(2,1)}, u32[]{:S(2)}) copy-start(bf16[2048,800]{1,0:T(8,128)(2,1)} %get-tuple-element.162.refs_3_) | copy-start | bytes 9830404
  655.4 78.3 %copy-start.78 = (bf16[4,80,2560]{2,1,0:T(8,128)(2,1)S(1)}, bf16[4,80,2560]{2,1,0:T(8,128)(2,1)}, u32[]{:S(2)}) copy-start(bf16[4,80,2560]{2,1,0:T(8,128)(2,1)} %get-tuple-element.84) | copy-start | bytes 4915204
  733.7 10.6 %copy-start.75 = (bf16[2048,2560]{1,0:T(8,128)(2,1)S(1)}, bf16[2048,2560]{1,0:T(8,128)(2,1)}, u32[]{:S(2)}) copy-start(bf16[2048,2560]{1,0:T(8,128)(2,1)} %get-tuple-element.103) | copy-start | bytes 31457284
  733.7 10.6 %copy-start.79 = (bf16[2048,384]{1,0:T(8,128)(2,1)S(1)}, bf16[2048,384]{1,0:T(8,128)(2,1)}, u32[]{:S(2)}) copy-start(bf16[2048,384]{1,0:T(8,128)(2,1)} %get-tuple-element.83) | copy-start | bytes 4718596
  744.3 5.7 copy-start.20
  750.7 94.9 %slice-start = ((s8[4718592]{0:T(1024)(128)(4,1)}), s8[4194304]{0:T(1024)(128)(4,1)S(1)}, s32[]{:S(2)}) async-start(s8[4718592]{0:T(1024)(128)(4,1)} %bitcast.134), calls=%async_computation | async-start | bytes 8388608
  753.7 91.9 %slice-start.1 = ((s8[4718592]{0:T(1024)(128)(4,1)}), s8[524288]{0:T(1024)(128)(4,1)S(1)}, s32[]{:S(2)}) async-start(s8[4718592]{0:T(1024)(128)(4,1)} %bitcast.134), calls=%async_computation.1 | async-start | bytes 1048576
  856.3 47.0 %copy-start.7 = (f32[256,1056]{1,0:T(8,128)S(1)}, f32[256,1056]{1,0:T(8,128)}, u32[]{:S(2)}) copy-start(f32[256,1056]{1,0:T(8,128)} %copy-done.6) | copy-start | bytes 3244036
  856.3 47.0 %copy-start.63 = (f32[256]{0:T(256)S(1)}, f32[256]{0:T(256)}, u32[]{:S(2)}) copy-start(f32[256]{0:T(256)} %copy-done.62) | copy-start | bytes 3076
  856.3 47.0 %copy-start.65 = (f32[256]{0:T(256)S(1)}, f32[256]{0:T(256)}, u32[]{:S(2)}) copy-start(f32[256]{0:T(256)} %copy-done.64) | copy-start | bytes 3076
  856.3 48.3 %copy-start.59 = (f32[768]{0:T(1024)S(1)}, f32[768]{0:T(1024)}, u32[]{:S(2)}) copy-start(f32[768]{0:T(1024)} %copy-done.58) | copy-start | bytes 9220
  856.3 48.3 %copy-start.67 = (f32[256]{0:T(256)S(1)}, f32[256]{0:T(256)}, u32[]{:S(2)}) copy-start(f32[256]{0:T(256)} %copy-done.66) | copy-start | bytes 3076
  909.9 5.4 copy-start.2
  909.9 5.4 copy-start.5
  910.0 5.4 copy-start.24
  1004.4 22.1 %copy-start.41 = (f32[16,2560]{1,0:T(8,128)S(1)}, f32[16,2560]{1,0:T(8,128)}, u32[]{:S(2)}) copy-start(f32[16,2560]{1,0:T(8,128)} %param.45) | copy-start | bytes 491524
  1004.4 22.1 %copy-start.54 = (f32[16,2560]{1,0:T(8,128)S(1)}, f32[16,2560]{1,0:T(8,128)}, u32[]{:S(2)}) copy-start(f32[16,2560]{1,0:T(8,128)} %param.46) | copy-start | bytes 491524
  1004.4 22.1 %copy-start.55 = (f32[16,2560]{1,0:T(8,128)S(1)}, f32[16,2560]{1,0:T(8,128)}, u32[]{:S(2)}) copy-start(f32[16,2560]{1,0:T(8,128)} %param.47) | copy-start | bytes 491524
  (50 other events, 147.8 us)

commit v3 on v2

--- a/solution.py
+++ b/solution.py
@@ -349,6 +349,83 @@
             )
 
 
+OCTET_ORDER = ((1, 1), (0, 1), (1, 0), (0, 0))
+
+
+def octet_reduce_inside_steps(
+    board, sum_ref, outgoing, mine, from_core, from_link, piece_time, begin=0.0
+):
+    h = sum_ref.shape[0] // 2
+    unit = octet_unit(sum_ref.shape)
+    core, along_x, along_y = ("plane", 1), ("plane", 2), "y"
+    board.terms = (outgoing, mine)
+    over_core, second, third = {}, {}, {}
+
+    def add_core(x, y, half):
+        place = octet_place(0, x, y, half)
+        over_core[place].wait_recv()
+        add_rows(mine.at[place], from_core.at[place])
+        return place
+
+    def pass_second(x, y, half, n):
+        place = add_core(x, y, half)
+        second[(x, y, half)] = board.send(
+            mine.at[place], from_link.at[n], along_y if half == 0 else along_x
+        )
+
+    for n, (x, y) in enumerate(OCTET_ORDER):
+        yield begin + piece_time * (2 * n + 0.5)
+        for half in range(2):
+            place = octet_place(0, x, y, half)
+            over_core[place] = board.send(outgoing.at[place], from_core.at[place], core)
+        yield begin + piece_time * (2 * n + 1.5)
+        if n == 0:
+            pass_second(1, 1, 0, 0)
+            pass_second(1, 1, 1, 1)
+        elif n == 1:
+            pass_second(0, 1, 0, 2)
+        elif n == 2:
+            pass_second(1, 0, 1, 3)
+    for n, (x, y, half) in enumerate(((1, 0, 0), (0, 1, 1))):
+        yield begin + max(unit * 1.2 + 2.0 * piece_time, 7.6 * piece_time)
+        place = add_core(x, y, half)
+        second[(1, 1, half)].wait_recv()
+        add_rows(mine.at[place], from_link.at[half])
+        third[half] = board.send(
+            mine.at[place], from_link.at[4 + n], along_x if half == 0 else along_y
+        )
+    for half, sent in ((0, (0, 1, 0)), (1, (1, 0, 1))):
+        yield begin + unit * 3.1 + 2.0 * piece_time
+        place = add_core(0, 0, half)
+        second[sent].wait_recv()
+        third[half].wait_recv()
+
+        @pl.loop(0, h // 16)
+        def _(step):
+            rows = pl.ds(pl.multiple_of(step * 16, 16), 16)
+            out_rows = pl.ds(pl.multiple_of(half * h + step * 16, 16), 16)
+            sum_ref[out_rows, :] = (
+                mine[place, rows, :].astype(jnp.float32)
+                + from_link[2 + half, rows, :].astype(jnp.float32)
+                + from_link[4 + half, rows, :].astype(jnp.float32)
+            )
+
+
+def octet_pieces(board, m, piece_time, product):
+    def run(core, x, y):
+        value = product(((core * 2 + x) * 2 + y) * m)
+        target = board.terms[0 if core else 1]
+        for half in range(2):
+            place = octet_place(0, x, y, half)
+            target[place] = value[half * (m // 2) : (half + 1) * (m // 2)].astype(target.dtype)
+
+    plan = []
+    for x, y in OCTET_ORDER:
+        for core in (1, 0):
+            plan.append((piece_time * len(plan), functools.partial(run, core, x, y)))
+    return plan
+
+
 def line_gather_steps(board, shard_ref, whole_ref, begin=0.0):
     unit = 4.0 * math.prod(shard_ref.shape) / LINK
     z = board.z
@@ -367,7 +444,7 @@
     )
 
     keep = board.move(shard_ref, whole_ref.at[z], close=False)
-    yield begin + 1.9 * unit
+    yield begin + 2.0 * unit
     two.wait_recv()
 
     @pl.when(board.middle)
@@ -593,14 +670,16 @@
 class GatherColumns:
     near, remotes, moves = NEAR_PLANE + NEAR_LINE, 7, 2
 
-    def __init__(self, blocks):
+    def __init__(self, blocks, hold=0.0):
         self.given = blocks
         self.outs = [hbm(blocks.shape), hbm((LINE,) + blocks.shape)]
         self.scratch = []
+        self.hold = hold
 
     def steps(self, board, blocks, outs, scratch):
-        begin = 9.0 * math.prod(blocks.shape[1:]) / LINK
+        begin = max(self.hold, 9.0 * math.prod(blocks.shape[1:]) / LINK)
         yield from plane_exchange_steps(board, blocks, outs[0])
+        yield begin
         yield from line_gather_steps(board, outs[0], outs[1], begin)
 
     def read(self, outs):
@@ -667,6 +746,105 @@
 
     def plain(self):
         return LineGather(super().plain()).plain()
+
+
+class OctetReduceInside:
+    near, remotes, moves = NEAR_OCTET, 14, 0
+
+    def __init__(self, m, n, piece_time):
+        self.given = None
+        self.outs = [(jax.ShapeDtypeStruct((m, n), jnp.float32), VMEM_SPEC)]
+        self.scratch = [pltpu.VMEM((k, m // 2, n), jnp.bfloat16) for k in (8, 8, 8, 6)]
+        self.piece_time = piece_time
+
+    def steps(self, board, given, outs, scratch):
+        return octet_reduce_inside_steps(board, outs[0], *scratch, self.piece_time)
+
+    def read(self, outs):
+        return outs[0]
+
+
+class Later:
+    def __init__(self, task, when):
+        self.task, self.when = task, when
+        self.near, self.remotes, self.moves = task.near, task.remotes, task.moves
+        self.given, self.outs, self.scratch = task.given, task.outs, task.scratch
+        self.read, self.plain = task.read, getattr(task, "plain", None)
+
+    def steps(self, *where):
+        yield self.when
+        yield from self.task.steps(*where)
+
+
+class Together:
+    def __init__(self, first, second):
+        self.parts = (first, second)
+        self.givens = first.givens + second.givens
+        self.outs = first.outs + second.outs
+        self.scratch = first.scratch + second.scratch
+        self.given_specs = first.given_specs + second.given_specs
+        self.out_specs = first.out_specs + second.out_specs
+
+    def phases(self, givens, outs, scratch, *rest):
+        a = self.parts[0]
+        cuts = len(a.givens), len(a.outs), len(a.scratch)
+        plan = a.phases(givens[: cuts[0]], outs[: cuts[1]], scratch[: cuts[2]], *rest)
+        plan = plan + self.parts[1].phases(
+            givens[cuts[0] :], outs[cuts[1] :], scratch[cuts[2] :], *rest
+        )
+        return sorted(plan, key=lambda item: item[0])
+
+
+class PieceProduct:
+    def __init__(self, left, right, m, piece_time, columns=False):
+        self.givens, self.outs, self.scratch = [left, right], [], []
+        self.given_specs, self.out_specs = [VMEM_SPEC] * 2, []
+        self.m, self.piece_time, self.columns = m, piece_time, columns
+
+    def phases(self, givens, outs, scratch, board, task_givens, task_outs):
+        left, right = givens
+
+        def product(row):
+            if self.columns:
+                return left_transposed(left[:, row : row + self.m], right[...])
+            return column_dot(left[row : row + self.m, :], right[...])
+
+        return octet_pieces(board, self.m, self.piece_time, product)
+
+
+class UnitBlocks:
+    def __init__(self, gate, up, line):
+        self.givens = [gate, up]
+        rows, columns = gate.shape
+        self.given_specs, self.out_specs = [VMEM_SPEC] * 2, [VMEM_SPEC] * 2
+        self.outs = [
+            jax.ShapeDtypeStruct((PLANE, rows, columns // PLANE), jnp.bfloat16)
+        ] * 2
+        self.scratch = []
+        self.line = line
+
+    def phases(self, givens, outs, scratch, board, task_givens, task_outs):
+        rows, columns = givens[0].shape
+        width = columns // (PLANE * self.line)
+        step_rows = 16 if rows % 16 == 0 else rows
+
+        def run(source, target):
+            @pl.loop(0, rows // step_rows)
+            def _(step):
+                here = pl.ds(pl.multiple_of(step * step_rows, step_rows), step_rows)
+                values = source[here, :]
+                for i in range(PLANE):
+                    target[i, here, :] = jnp.concatenate(
+                        [
+                            values[:, (z * PLANE + i) * width : (z * PLANE + i + 1) * width]
+                            for z in range(self.line)
+                        ],
+                        axis=1,
+                    ).astype(target.dtype)
+
+        return [
+            (1.0 + 6.0 * n, functools.partial(run, givens[n], outs[n])) for n in range(2)
+        ]
 
 
 def communicate(collective_id, *tasks, compute=None):
@@ -690,6 +868,7 @@
         near += [name for name in task.near if name not in near]
     n_outs = [len(task.outs) for task in tasks]
     n_scratch = [len(task.scratch) for task in tasks]
+    inputs = [task.given for task in tasks if task.given is not None]
     more_givens = compute.givens if compute else []
     more_outs = compute.outs if compute else []
     more_scratch = compute.scratch if compute else []
@@ -704,7 +883,8 @@
             del refs[:count]
             return part
 
-        givens, compute_givens = first(len(tasks)), first(len(more_givens))
+        givens = [None if task.given is None else first(1)[0] for task in tasks]
+        compute_givens = first(len(more_givens))
         outs, compute_outs = first(sum(n_outs)), first(len(more_outs))
         scratch, compute_scratch = first(sum(n_scratch)), first(len(more_scratch))
         running, closing = [], []
@@ -752,7 +932,7 @@
     outs = pl.pallas_call(
         kernel,
         out_shape=[shape for task in tasks for shape, _ in task.outs] + more_outs,
-        in_specs=[HBM_SPEC] * len(tasks) + more_given_specs,
+        in_specs=[HBM_SPEC] * len(inputs) + more_given_specs,
         out_specs=[spec for task in tasks for _, spec in task.outs]
         + more_out_specs,
         scratch_shapes=[shape for task in tasks for shape in task.scratch]
@@ -764,7 +944,7 @@
             vmem_limit_bytes=VMEM_LIMIT,
         ),
         cost_estimate=pl.CostEstimate(flops=0, bytes_accessed=2**28, transcendentals=0),
-    )(*[task.given for task in tasks], *more_givens)
+    )(*inputs, *more_givens)
     results = [
         task.read(outs[sum(n_outs[:n]) : sum(n_outs[: n + 1])]) for n, task in enumerate(tasks)
     ]
@@ -843,7 +1023,7 @@
             pltpu.VMEM((self.pack_rows, self.pack_rows), jnp.float32),
             pltpu.VMEM((self.pack_rows, self.pack_rows), low),
         ]
-        self.phase_time = 12.0
+        self.phase_time = 9.5
         self.given_specs = [VMEM_SPEC] * len(self.givens)
         self.out_specs = [VMEM_SPEC] * len(self.outs)
 
@@ -854,22 +1034,24 @@
         scale = QH ** (-0.5)
         size = self.pack_rows
 
-        def run(pack):
-            score_bias(keys, bounds, bias, pack, size)
+        def run(pack, part):
+            first, last = (0, self.heads // 2 + 1) if part == 0 else (self.heads // 2 + 1, self.heads)
             start = pack * size
             whole = slice(start, start + size)
             rope_key = pltpu.roll(
                 tokens[whole, QR + KVR : QR + KVR + HEAD].astype(jnp.float32), DN, 1
             )
-            for n in range(self.pairs):
-                mixed[whole, n * HEAD : (n + 1) * HEAD] = jnp.zeros((size, HEAD), mixed.dtype)
-            totals[whole, :] = jnp.zeros((size, HEAD), jnp.float32)
-            heads_out[whole, :] = column_dot(
-                tokens[whole, QR : QR + KVR], latent_up[...]
-            ).astype(jnp.bfloat16)
-            raw[...] = column_dot(tokens[whole, 0:QR], query_up[...])
-
-            @pl.loop(0, self.heads)
+            if part == 0:
+                score_bias(keys, bounds, bias, pack, size)
+                for n in range(self.pairs):
+                    mixed[whole, n * HEAD : (n + 1) * HEAD] = jnp.zeros((size, HEAD), mixed.dtype)
+                totals[whole, :] = jnp.zeros((size, HEAD), jnp.float32)
+                heads_out[whole, :] = column_dot(
+                    tokens[whole, QR : QR + KVR], latent_up[...]
+                ).astype(jnp.bfloat16)
+                raw[...] = column_dot(tokens[whole, 0:QR], query_up[...])
+
+            @pl.loop(first, last)
             def _(head):
                 lanes = pl.ds(pl.multiple_of(head * HEAD, HEAD), HEAD)
                 pair = pl.ds(pl.multiple_of((head // 2) * HEAD, HEAD), HEAD)
@@ -904,7 +1086,10 @@
                     mixed.dtype
                 )
 
-        return [(self.phase_time * n, functools.partial(run, n)) for n in range(self.packs)]
+        return [
+            (self.phase_time * n, functools.partial(run, n // 2, n % 2))
+            for n in range(2 * self.packs)
+        ]
 
 
 class AttentionBackward:
@@ -952,7 +1137,7 @@
             pltpu.VMEM((size, size), low),
             pltpu.VMEM((size, HEAD), jnp.float32),
         ]
-        self.phase_time = 16.0
+        self.phase_time = 9.0
         self.given_specs = [VMEM_SPEC] * len(self.givens)
         self.out_specs = [VMEM_SPEC] * len(self.outs)
 
@@ -976,16 +1161,18 @@
         scale = QH ** (-0.5)
         size = self.pack_rows
 
-        def run(pack):
-            score_bias(keys, bounds, bias, pack, size)
+        def run(pack, part):
+            first, last = (0, self.heads // 2 + 1) if part == 0 else (self.heads // 2 + 1, self.heads)
             start = pack * size
             whole = slice(start, start + size)
             rope_key = pltpu.roll(
                 tokens[whole, QR + KVR : QR + KVR + HEAD].astype(jnp.float32), DN, 1
             )
-            grad_rope[...] = jnp.zeros_like(grad_rope)
-
-            @pl.loop(0, self.heads)
+            if part == 0:
+                score_bias(keys, bounds, bias, pack, size)
+                grad_rope[...] = jnp.zeros_like(grad_rope)
+
+            @pl.loop(first, last)
             def _(head):
                 lanes = pl.ds(pl.multiple_of(head * HEAD, HEAD), HEAD)
                 pair = pl.ds(pl.multiple_of((head // 2) * HEAD, HEAD), HEAD)
@@ -1023,6 +1210,8 @@
                     grad_heads.dtype
                 )
 
+            if part == 0:
+                return
             terms[whole, 0:QR] = right_transposed(grad_queries[whole, :], query_up[...]).astype(
                 terms.dtype
             )
@@ -1031,7 +1220,10 @@
             ).astype(terms.dtype)
             terms[whole, QR + KVR :] = pltpu.roll(grad_rope[...], HEAD - DN, 1).astype(terms.dtype)
 
-        return [(self.phase_time * n, functools.partial(run, n)) for n in range(self.packs)]
+        return [
+            (self.phase_time * n, functools.partial(run, n // 2, n % 2))
+            for n in range(2 * self.packs)
+        ]
 
 
 class FfnForward:
@@ -1108,42 +1300,44 @@
 class FfnBackward:
     CHUNK = 256
 
-    def __init__(self, normed, grad_gate, grad_up, hidden, down):
-        self.givens = [normed, grad_gate, grad_up, hidden, down]
+    def __init__(self, normed, grad_gate, grad_up, gate, up, m, piece_time):
+        self.givens = [normed, grad_gate, grad_up, gate, up]
         self.given_specs = [HBM_SPEC] * 5
-        self.out_specs = [HBM_SPEC] * 3
+        self.out_specs = [HBM_SPEC] * 2
         rows, depth = normed.shape
-        units = hidden.shape[1]
+        units = gate.shape[1]
         low = normed.dtype
         self.rows, self.depth, self.units = rows, depth, units
-        self.outs = [jax.ShapeDtypeStruct((depth, units), low)] * 2 + [
-            jax.ShapeDtypeStruct((rows, depth), low)
-        ]
+        self.m, self.piece_time = m, piece_time
+        self.outs = [jax.ShapeDtypeStruct((depth, units), low)] * 2
         self.scratch = [
             pltpu.VMEM((rows, units), low),
             pltpu.VMEM((rows, units), low),
-            pltpu.VMEM((units, depth), low),
-            pltpu.SemaphoreType.DMA((3,)),
+            pltpu.VMEM((depth, units), low),
+            pltpu.VMEM((depth, units), low),
+            pltpu.SemaphoreType.DMA((4,)),
         ]
 
     def phases(self, givens, outs, scratch, board, task_givens, task_outs):
-        normed, grad_gate, grad_up, hidden, down = givens
-        gate_held, up_held, down_held, sems = scratch
+        normed = givens[0]
+        held, sems = scratch[:4], scratch[4]
+        gate_held, up_held, gate_weight, up_weight = held
         chunk, rows, units, depth = self.CHUNK, self.rows, self.units, self.depth
         loads = [
-            pltpu.make_async_copy(source, target, sems.at[n])
-            for n, (source, target) in enumerate(
-                ((grad_gate, gate_held), (grad_up, up_held), (down, down_held))
-            )
+            pltpu.make_async_copy(givens[n + 1], held[n], sems.at[n]) for n in (0, 2, 1, 3)
         ]
         for load in loads:
             load.start()
 
+        def product(row):
+            while loads:
+                loads.pop(0).wait()
+            part = slice(row, row + self.m)
+            return right_transposed(gate_held[part, :], gate_weight[...]) + right_transposed(
+                up_held[part, :], up_weight[...]
+            )
+
         def gradients(first, count):
-            if first == 0:
-                loads[0].wait()
-                loads[1].wait()
-
             def body(normed_part, gate_part, up_part):
                 left = normed_part[...]
                 gate_part[...] = left_transposed(left, gate_held[...]).astype(gate_part.dtype)
@@ -1156,9 +1350,33 @@
                 out_specs=[pl.BlockSpec((chunk, units), lambda n: (n + first, 0))] * 2,
             )(normed, outs[0], outs[1])
 
+        plan = octet_pieces(board, self.m, self.piece_time, product)
+        when = plan[-1][0] + self.piece_time
+        for first in range(0, depth // chunk, 2):
+            plan.append((when, functools.partial(gradients, first, 2)))
+            when += 6.0
+        return plan
+
+
+class FfnProducts:
+    CHUNK = 256
+
+    def __init__(self, hidden, down):
+        self.givens = [hidden, down]
+        self.given_specs, self.out_specs = [HBM_SPEC] * 2, [HBM_SPEC]
+        self.outs = [jax.ShapeDtypeStruct((hidden.shape[0], down.shape[1]), down.dtype)]
+        self.scratch = [pltpu.VMEM(down.shape, down.dtype), pltpu.SemaphoreType.DMA]
+
+    def phases(self, givens, outs, scratch, board, task_givens, task_outs):
+        hidden, down = givens
+        down_held, sem = scratch
+        chunk = self.CHUNK
+        load = pltpu.make_async_copy(down, down_held, sem)
+        load.start()
+
         def products(first, count):
             if first == 0:
-                loads[2].wait()
+                load.wait()
 
             def body(hidden_part, out_part):
                 out_part[...] = column_dot(hidden_part[...], down_held[...]).astype(out_part.dtype)
@@ -1166,19 +1384,14 @@
             pltpu.emit_pipeline(
                 body,
                 grid=(count,),
-                in_specs=[pl.BlockSpec((chunk, units), lambda n: (n + first, 0))],
-                out_specs=[pl.BlockSpec((chunk, depth), lambda n: (n + first, 0))],
-            )(hidden, outs[2])
-
-        plan = []
-        when = 8.0
-        for first in range(0, depth // chunk, 2):
-            plan.append((when, functools.partial(gradients, first, 2)))
-            when += 6.0
-        for first in range(0, rows // chunk, 2):
-            plan.append((when, functools.partial(products, first, 2)))
-            when += 4.0
-        return plan
+                in_specs=[pl.BlockSpec((chunk, hidden.shape[1]), lambda n: (n + first, 0))],
+                out_specs=[pl.BlockSpec((chunk, down.shape[1]), lambda n: (n + first, 0))],
+            )(hidden, outs[0])
+
+        return [
+            (2.0 + 2.0 * first, functools.partial(products, first, 2))
+            for first in range(0, hidden.shape[0] // chunk, 2)
+        ]
 
 
 class UnitUpdate:
@@ -1221,7 +1434,7 @@
                 for out, result in zip(outs, results):
                     out[here, :] = result
 
-        return [(8.0, functools.partial(run, 0)), (14.0, functools.partial(run, 1))]
+        return [(12.5, functools.partial(run, 0)), (18.5, functools.partial(run, 1))]
 
 
 def positions(segment_ids):
@@ -1287,14 +1500,6 @@
     def column_blocks(weight, columns):
         return weight.astype(low).reshape(-1, PLANE, columns).transpose(1, 0, 2)
 
-    def unit_blocks(weight):
-        return (
-            weight.astype(low)
-            .reshape(weight.shape[0], line, PLANE, units // line)
-            .transpose(2, 0, 1, 3)
-            .reshape(PLANE, weight.shape[0], units)
-        )
-
     down_rows = query_down.shape[0]
     pack_height = down_rows + 16
     gain_width = gains.shape[0]
@@ -1310,14 +1515,13 @@
         blocks = jnp.pad(blocks, ((0, 0), (0, 0), (0, 0), (0, HEAD - QH)))
         return blocks.reshape(-1, PLANE, local_heads * HEAD).transpose(1, 0, 2)
 
-    down_low = down_proj.astype(low)
-    pack_all, query_up_all, latent_up_all, gate_plane, down_first = communicate(
+    pack_all, query_up_all, latent_up_all, output_moved, (gate_blocks, up_blocks) = communicate(
         1,
         GatherPack(down_pack),
-        GatherColumns(head_blocks(query_up)),
-        GatherColumns(column_blocks(latent_up, local_heads * KH)),
-        PlaneExchange(unit_blocks(gate_proj)),
-        LineGather(down_low[:, : D // 2]),
+        GatherColumns(head_blocks(query_up), 16.0),
+        GatherColumns(column_blocks(latent_up, local_heads * KH), 16.0),
+        Later(Transpose(output_proj.astype(low)), 16.0),
+        compute=UnitBlocks(gate_proj, up_proj, line),
     )
     query_up_all = query_up_all.reshape(QR, local_heads * HEAD)
     latent_up_all = latent_up_all.reshape(KVR, local_heads * KH)
@@ -1363,8 +1567,8 @@
         ],
         axis=1,
     )
-    tokens_all, output_all = communicate(
-        3, OctetGather(tokens_own), GatherMoved(output_proj.astype(low))
+    tokens_all, output_all, gate_plane = communicate(
+        3, OctetGather(tokens_own), LineGather(output_moved), PlaneExchange(gate_blocks)
     )
     output_all = jnp.pad(
         output_all.reshape(local_heads * DV, D), ((0, mixed_width - local_heads * DV), (0, 0))
@@ -1386,34 +1590,42 @@
     grad_ffn, up_plane, gate_all, (queries, latent_heads, mixed_heads, log_totals) = communicate(
         2,
         OctetGather((RESIDUAL * cotangent.astype(jnp.float32)).astype(low)),
-        PlaneExchange(unit_blocks(up_proj)),
+        PlaneExchange(up_blocks),
         LineGather(gate_plane),
         compute=AttentionForward(
             tokens_all, keys, bounds, waves, query_up_all, latent_up_all, packs, local_heads
         ),
     )
     gate_all = gate_all.reshape(D, units)
-    attention_terms = jnp.dot(mixed_heads, output_all, preferred_element_type=jnp.float32)
-    attention_sum, up_all = communicate(
-        4, OctetReduce(attention_terms.astype(low)), LineGather(up_plane)
-    )
+    if line == LINE:
+        attention_sum, up_all, _ = communicate(
+            4,
+            OctetReduceInside(half_rows, D, 2.0),
+            LineGather(up_plane),
+            compute=PieceProduct(mixed_heads, output_all, half_rows, 2.0),
+        )
+    else:
+        attention_terms = jnp.dot(mixed_heads, output_all, preferred_element_type=jnp.float32)
+        attention_sum, up_all = communicate(
+            4, OctetReduce(attention_terms.astype(low)), LineGather(up_plane)
+        )
     up_all = up_all.reshape(D, units)
     residual = incoming + RESIDUAL * attention_sum
 
     ffn_unit, inverse_ffn = norm_forward(residual, gain_ffn)
     normed_own = ffn_unit.astype(low)
-    tasks = (OctetGather(normed_own), LineGather(down_low[:, D // 2 :]))
+    tasks = (OctetGather(normed_own), LineGather(down_proj.astype(low)))
     if line == LINE:
-        normed_ffn, down_second, (gate_value, up_value) = communicate(
+        normed_ffn, down_all, (gate_value, up_value) = communicate(
             5,
             *tasks,
             compute=FfnForward(gate_all, up_all, half_rows, octet_unit((half_rows, D))),
         )
     else:
-        normed_ffn, down_second = communicate(5, *tasks)
+        normed_ffn, down_all = communicate(5, *tasks)
         gate_value = jnp.dot(normed_ffn, gate_all, preferred_element_type=jnp.float32)
         up_value = jnp.dot(normed_ffn, up_all, preferred_element_type=jnp.float32)
-    down_all = jnp.concatenate([down_first, down_second], axis=2).reshape(units, D)
+    down_all = down_all.reshape(units, D)
     gate_sigmoid = lax.logistic(gate_value)
     silu_gate = gate_value * gate_sigmoid
     hidden = (silu_gate * up_value).astype(low)
@@ -1422,24 +1634,32 @@
         grad_hidden * up_value * gate_sigmoid * (1.0 + gate_value * (1.0 - gate_sigmoid))
     ).astype(low)
     grad_up = (grad_hidden * silu_gate).astype(low)
-    ffn_back_terms = right_transposed(grad_gate, gate_all) + right_transposed(grad_up, up_all)
     down_grad = left_transposed(hidden, grad_ffn).astype(low).reshape(line, -1, D)
-    grad_normed_ffn, down_shard, (gate_grad, up_grad, ffn_terms) = communicate(
-        6,
-        OctetReduce(ffn_back_terms.astype(low)),
-        LineReduce(down_grad),
-        compute=FfnBackward(normed_ffn, grad_gate, grad_up, hidden, down_all),
-    )
+    if line == LINE:
+        grad_normed_ffn, down_shard, (gate_grad, up_grad) = communicate(
+            6,
+            OctetReduceInside(half_rows, D, 5.0),
+            LineReduce(down_grad),
+            compute=FfnBackward(normed_ffn, grad_gate, grad_up, gate_all, up_all, half_rows, 5.0),
+        )
+    else:
+        back_terms = right_transposed(grad_gate, gate_all) + right_transposed(grad_up, up_all)
+        gate_grad = left_transposed(normed_ffn, grad_gate).astype(low)
+        up_grad = left_transposed(normed_ffn, grad_up).astype(low)
+        grad_normed_ffn, down_shard = communicate(
+            6, OctetReduce(back_terms.astype(low)), LineReduce(down_grad)
+        )
     outer_grad = cotangent.astype(jnp.float32)
     grad_incoming_ffn, gain_ffn_grad = norm_backward(
         residual, inverse_ffn, gain_ffn, grad_normed_ffn
     )
     grad_residual = outer_grad + grad_incoming_ffn
 
-    grad_branch, gate_sum = communicate(
+    grad_branch, gate_sum, (ffn_terms,) = communicate(
         7,
         OctetGather((RESIDUAL * grad_residual).astype(low)),
         LineReduce(gate_grad.reshape(line, PLANE, -1, units)),
+        compute=FfnProducts(hidden, down_all),
     )
     output_grad = (
         left_transposed(mixed_heads, grad_branch)
@@ -1485,7 +1705,6 @@
     )
     grad_rope = unrotate(grad_units[:, QR + KVR : QR + KVR + DR], own_cosine, own_sine)
     grad_both = jnp.concatenate([grad_query_wide, grad_latent_part, grad_rope], axis=1).astype(low)
-    down_both_grad = left_transposed(normed_attn, grad_both).astype(low)
     grad_normed_attn = right_transposed(grad_both, down_both)
     grad_incoming_attn, gain_attention_grad = norm_backward(
         incoming, inverse_attention, gain_attention, grad_normed_attn
@@ -1494,36 +1713,57 @@
     gains_grad = jnp.concatenate(
         [gain_attention_grad, gain_query_grad, gain_latent_grad, gain_ffn_grad]
     ).astype(low)
-    pack_grad = jnp.concatenate(
-        [
-            down_both_grad.reshape(line, PLANE, tensor, down_rows, QR + KVR + DR),
-            jnp.pad(
-                gains_grad.reshape(line, PLANE, tensor, 1, gain_width),
-                ((0, 0), (0, 0), (0, 0), (0, 15), (0, QR + KVR + DR - gain_width)),
-            ),
-        ],
-        axis=3,
-    ).transpose(1, 2, 0, 3, 4)
-    pack_terms = jnp.concatenate(
+    shards = size * tensor
+    left_blocks = normed_attn.reshape(half_rows, line, PLANE, tensor, down_rows)
+    left_blocks = jnp.pad(left_blocks, ((0, 0), (0, 0), (0, 0), (0, 0), (0, 16)))
+    spots = jnp.arange(pack_height)[None, None, :] == down_rows
+    shard_index = jnp.arange(shards)
+    left_marks = (
+        (shard_index[:, None, None] == shard_index[None, :, None]) & spots
+    ).astype(low)
+    left_blocks = jnp.concatenate(
+        [left_blocks, left_marks.reshape(shards, line, PLANE, tensor, pack_height)], axis=0
+    ).transpose(2, 3, 0, 1, 4)
+    pack_left = jnp.concatenate(
         [
             lax.dynamic_slice(
-                pack_grad,
+                left_blocks,
                 (i ^ (core + 2 * x), (t + y) % tensor, 0, 0, 0),
-                (1, 1) + pack_grad.shape[2:],
-            ).reshape(line * pack_height, QR + KVR + DR)
+                (1, 1) + left_blocks.shape[2:],
+            ).reshape(half_rows + shards, line * pack_height)
             for core in range(2)
             for x in range(2)
             for y in range(tensor)
         ],
+        axis=1,
+    )
+    pack_right = jnp.concatenate(
+        [
+            grad_both,
+            jnp.pad(
+                gains_grad.reshape(shards, gain_width),
+                ((0, 0), (0, QR + KVR + DR - gain_width)),
+            ),
+        ],
         axis=0,
     )
+    pack_rows_all = line * pack_height
+    up_update = UnitUpdate(up_parts, up_proj, up_proj_first, up_proj_second, line)
+    if line == LINE:
+        pack_task = OctetReduceInside(pack_rows_all, QR + KVR + DR, 1.5)
+        tail_compute = Together(
+            PieceProduct(pack_left, pack_right, pack_rows_all, 1.5, columns=True), up_update
+        )
+    else:
+        pack_task = OctetReduce(left_transposed(pack_left, pack_right).astype(low))
+        tail_compute = up_update
     pack_octet, query_up_sum, latent_up_sum, output_shard, up_out = communicate(
         10,
-        OctetReduce(pack_terms),
+        pack_task,
         LineReduce(query_up_grad.reshape(line, PLANE, -1, local_heads * HEAD)),
         LineReduce(latent_up_grad.reshape(line, PLANE, -1, local_heads * KH)),
         Transpose(output_sum.astype(low), back=True),
-        compute=UnitUpdate(up_parts, up_proj, up_proj_first, up_proj_second, line),
+        compute=tail_compute,
     )
     pack_sum, query_up_parts, latent_up_parts = communicate(
         11,

time: 1060 us -> 1030 us (0.972)
  matrix products: 120 us -> 72.2 us
    dot_general x5 -> x3, matrix products: 75.5 us -> 38.9 us  [right_transposed(): lax.dot_general(left_side, right_side, (((1,), (1,)), ((), ())), preferre...]
    dynamic_update_slice x8, local copies, waits for them, and re-layouts: 1 us -> 17.5 us  [local(): lax.dynamic_update_slice(down_blocks, down_octet[k % 2, k // 2, y][None,...]
    reshape x6 -> x8, local copies, waits for them, and re-layouts: 21.4 us -> 10.2 us  [local(): pack_left = jnp.concatenate([lax.dynamic_slice(left_blocks, (i ^ core + 2...]
    unnamed x177 -> x121, local copies, waits for them, and re-layouts: 22.2 us -> 26.4 us
    dot_general x5 -> x4, matrix products: 29.9 us -> 28.4 us  [left_transposed(): lax.dot_general(left_side, right_side, (((0,), (0,)), ((), ())), preferre...]
where the time goes in v3:
time: 1030 us; the launch traced here: 1020 us
  Pallas kernels  784 us (76%)
  local copies, waits for them, and re-layouts  81.1 us (8%)
  other arithmetic  81.1 us (8%)
  matrix products  72.2 us (7%)
    pallas_call x11, Pallas kernels, run_kernel(): pl.pallas_call(kernel, out_shape=[shape for task in tasks for shape, _ in...  784 us
    dot_general x3, matrix products, right_transposed(): lax.dot_general(left_side, right_side, (((1,), (1,)), ((), ())), preferre...  38.9 us
    dot_general x4, matrix products, left_transposed(): lax.dot_general(left_side, right_side, (((0,), (0,)), ((), ())), preferre...  28.4 us
    unnamed x121, local copies, waits for them, and re-layouts  26.4 us

profile of v3, /device:TPU:0, one launch (start us, length us, event | category | flops | bytes accessed | tf_op | source)
XLA Modules:
  0.0 1019.9 jit_solution(530358615657002181)
XLA Ops:
  5.5 87.4 %shard_map.509 = (bf16[4,96,1056]{2,1,0:T(8,128)(2,1)}, bf16[32,96,1056]{2,1,0:T(8,128)(2,1)}, bf16[4,48,640]{2,1,0:T(8,128)(2,1)}, bf16[4,4,48,640]{3,2,1,0:T(8...) custom-call(bf16[96,1056]{1,0:T(8,128)(2,1)} %fusion.58.refs_0_, ...), custom_call_target="tpu_custom_call" | custom-call | bytes 268435456 | tf_op jit(solution)/shard_map/pallas_call | solution.py:932
  93.0 3.7 broadcast_in_dim.39
  114.1 5.7 slice.257
  121.7 5.0 fusion.100
  130.6 55.4 %shard_map.510 = (bf16[2048,1152]{1,0:T(8,128)(2,1)}, bf16[4,80,2560]{2,1,0:T(8,128)(2,1)}, bf16[4,160,800]{2,1,0:T(8,128)(2,1)}) custom-call(bf16[256,1152]{1,0:T(8,128)(2,1)} %concatenate.48.refs_0_, bf16[80,2560]{1,0:T(8,128)(2,1)} %get-tuple-element.82.refs_1_, bf16[4,160,800]{2,1,0:T(8,128)(2,1)} %get-tuple-element.83.refs_2_), custom_call_target="tpu_custom_call" | custom-call | bytes 268435456 | tf_op jit(solution)/shard_map/pallas_call | solution.py:932
  188.8 3.7 multiply_sine_fusion
  192.7 3.9 pad_maximum_fusion
  199.8 103.8 %shard_map.511 = (bf16[2048,2560]{1,0:T(8,128)(2,1)}, bf16[4,160,800]{2,1,0:T(8,128)(2,1)}, bf16[4,4,160,800]{3,2,1,0:T(8,128)(2,1)}, bf16[2048,640]{1,0:T(8,128...) custom-call(bf16[256,2560]{1,0:T(8,128)(2,1)} %fusion.8.refs_0_, ...), custom_call_target="tpu_custom_call" | custom-call | bytes 268435456 | tf_op jit(solution)/shard_map/pallas_call | solution.py:932
  305.0 80.6 %shard_map.512 = (f32[256,2560]{1,0:T(8,128)}, bf16[4,4,160,800]{3,2,1,0:T(8,128)(2,1)}) custom-call(bf16[4,160,800]{2,1,0:T(8,128)(2,1)} %get-tuple-element.88.refs_0_, bf16[2048,384]{1,0:T(8,128)(2,1)} %get-tuple-element.89.refs_1_, bf16[384,2560]{1,0:T(8,128)(2,1)} %pad.27.refs_2_), custom_call_target="tpu_custom_call" | custom-call | bytes 268435456 | tf_op jit(solution)/shard_map/pallas_call | solution.py:932
  391.0 76.0 %shard_map.513 = (bf16[2048,2560]{1,0:T(8,128)(2,1)}, bf16[4,200,2560]{2,1,0:T(8,128)(2,1)}, f32[2048,800]{1,0:T(8,128)}, f32[2048,800]{1,0:T(8,128)}) custom-call(bf16[256,2560]{1,0:T(8,128)(2,1)} %multiply_convert_fusion.4.refs_0_, bf16[200,2560]{1,0:T(8,128)(2,1)} %convert_element_type.187.refs_1_, bf16[2560,800]{1,0:T(8,128)(2,1)} %bitcast.122, ...), custom_call_target="tpu_custom_call" | custom-call | bytes 268435456 | tf_op jit(solution)/shard_map/pallas_call | solution.py:932
  467.0 22.9 %multiply_convert_fusion = (bf16[2048,800]{1,0:T(8,128)(2,1)}, bf16[2048,800]{1,0:T(8,128)(2,1)}, bf16[2048,800]{1,0:T(8,128)(2,1)}) fusion(f32[2048,800]{1,0:T(8,128)} %get-tuple-element.94, f32[2048,800]{1,0:T(8,128)} %get-tuple-element.95, bf16[2048,2560]{1,0:T(8,128)(2,1)} %get-tuple-element.96, bf16[800,2560]{1,0:T(8,128)(2,1)} %bitcast.147), kind=kOutput, calls=%fused_computation | convolution fusion | flops 8413184000 | bytes 37519360 | tf_op jit(solution)/shard_map/dot_general | solution.py:36
  489.9 14.4 %convolution_convert_fusion = bf16[800,2560]{1,0:T(8,128)(2,1)} fusion(bf16[2048,800]{1,0:T(8,128)(2,1)} %get-tuple-element.167.refs_2_, bf16[2048,2560]{1,0:T(8,128)(2,1)} %get-tuple-element.96), kind=kOutput, calls=%fused_computation.5 | convolution fusion | flops 8390656000 | bytes 17858560 | tf_op jit(solution)/shard_map/dot_general | solution.py:42
  504.2 74.7 %shard_map.514 = (f32[256,2560]{1,0:T(8,128)}, bf16[3,200,2560]{2,1,0:T(8,128)(2,1)}, bf16[2560,800]{1,0:T(8,128)(2,1)}, bf16[2560,800]{1,0:T(8,128)(2,1)}) custom-call(bf16[4,200,2560]{2,1,0:T(8,128)(2,1)} %bitcast.140, bf16[2048,2560]{1,0:T(8,128)(2,1)} %get-tuple-element.97.refs_1_, bf16[2048,800]{1,0:T(8,128)(2,1)} %get-tuple-element.166.refs_2_, ...), custom_call_target="tpu_custom_call" | custom-call | bytes 268435456 | tf_op jit(solution)/shard_map/pallas_call | solution.py:932
  579.0 5.3 convert_element_type.217
  584.3 8.3 multiply_subtract_fusion
  596.0 78.5 %shard_map.515 = (bf16[2048,2560]{1,0:T(8,128)(2,1)}, bf16[3,4,160,800]{3,2,1,0:T(8,128)(2,1)}, bf16[2048,2560]{1,0:T(8,128)(2,1)}) custom-call(bf16[256,2560]{1,0:T(8,128)(2,1)} %multiply_convert_fusion.3.refs_0_, bf16[4,4,160,800]{3,2,1,0:T(8,128)(2,1)} %bitcast.130, bf16[2048,800]{1,0:T(8,128)(2,1)} %get-tuple-element.167.refs_2_, bf16[800,2560]{1,0:T(8,128)(2,1)} %bitcast.148), custom_call_target="tpu_custom_call" | custom-call | bytes 268435456 | tf_op jit(solution)/shard_map/pallas_call | solution.py:932
  674.5 9.5 convolution_convert_fusion.1.refs_6_
  684.6 2.9 fusion.29.refs_2_
  687.5 92.2 %shard_map.516 = (f32[256,2560]{1,0:T(8,128)}, bf16[3,4,160,800]{3,2,1,0:T(8,128)(2,1)}, bf16[4,160,800]{2,1,0:T(8,128)(2,1)}, bf16[2048,640]{1,0:T(8,128)(2,1)}...) custom-call(bf16[2048,2560]{1,0:T(8,128)(2,1)} %get-tuple-element.101.refs_0_, ...), custom_call_target="tpu_custom_call" | custom-call | bytes 268435456 | tf_op jit(solution)/shard_map/pallas_call | solution.py:932
  779.6 2.6 convert_element_type.199
  782.3 3.0 fusion.30.refs_2_
  785.2 7.2 fusion.101
  793.7 47.2 %shard_map.517 = (f32[256,1152]{1,0:T(8,128)}, bf16[3,80,2560]{2,1,0:T(8,128)(2,1)}, bf16[4,160,800]{2,1,0:T(8,128)(2,1)}, f32[160,3200]{1,0:T(8,128)}, f32[160,3200]{1,0:T(8,128)}, /*index=5*/f32[160,3200]{1,0:T(8,128)}) custom-call(bf16[2048,1152]{1,0:T(8,128)(2,1)} %get-tuple-element.109.refs_0_, bf16[4,80,2560]{2,1,0:T(8,128)(2,1)} %bitcast.126, ...), custom_call_target="tpu_custom_call" | custom-call | bytes 268435456 | tf_op jit(solution)/shard_map/pallas_call | solution.py:932
  847.4 6.5 fusion.15
  855.0 2.4 copy.211
  883.9 2.6 fusion.51.refs_2_
  886.5 3.1 convolution_convert_fusion.2
  889.6 3.6 fusion.25
  893.3 65.6 %shard_map.518 = (f32[384,1056]{1,0:T(8,128)}, bf16[3,4,48,640]{3,2,1,0:T(8,128)(2,1)}, bf16[3,4,16,640]{3,2,1,0:T(8,128)(2,1)}, bf16[80,2560]{1,0:T(8,128)(2,1)...) custom-call(bf16[4,4,48,640]{3,2,1,0:T(8,128)(2,1)} %bitcast.154, ...), custom_call_target="tpu_custom_call" | custom-call | bytes 268435456 | tf_op jit(solution)/shard_map/pallas_call | solution.py:932
  965.5 22.1 %shard_map.519 = (bf16[3,96,1056]{2,1,0:T(8,128)(2,1)}, bf16[4,48,640]{2,1,0:T(8,128)(2,1)}, bf16[4,16,640]{2,1,0:T(8,128)(2,1)}) custom-call(bf16[4,96,1056]{2,1,0:T(8,128)(2,1)} %bitcast.145, bf16[4,48,640]{2,1,0:T(8,128)(2,1)} %fusion.57.refs_1_, bf16[4,16,640]{2,1,0:T(8,128)(2,1)} %fusion.79.refs_2_), custom_call_target="tpu_custom_call" | custom-call | bytes 268435456 | tf_op jit(solution)/shard_map/pallas_call | solution.py:932
  993.3 2.5 multiply_subtract_fusion.2
  1004.0 2.8 fusion.14
  (243 shorter events, 112.9 us)
Async XLA Ops:
  0.7 3.4 copy-start.28
  0.7 3.4 copy-start.35
  0.7 3.4 copy-start.46
  0.7 4.1 copy-start.33
  114.1 6.8 copy-start.2
  121.7 5.0 copy-start.11
  126.7 59.3 %copy-start.5 = (f32[256,1056]{1,0:T(8,128)}, f32[256,1056]{1,0:T(8,128)S(1)}, u32[]{:S(2)}) copy-start(f32[256,1056]{1,0:T(8,128)S(1)} %fusion.100) | copy-start | bytes 3244036
  199.8 103.8 %copy-start.25 = (bf16[4,80,2560]{2,1,0:T(8,128)(2,1)S(1)}, bf16[4,80,2560]{2,1,0:T(8,128)(2,1)}, u32[]{:S(2)}) copy-start(bf16[4,80,2560]{2,1,0:T(8,128)(2,1)} %get-tuple-element.90) | copy-start | bytes 4915204
  305.0 80.6 %copy-start.3 = (bf16[256,2560]{1,0:T(8,128)(2,1)S(1)}, bf16[256,2560]{1,0:T(8,128)(2,1)}, u32[]{:S(2)}) copy-start(bf16[256,2560]{1,0:T(8,128)(2,1)} %param.30) | copy-start | bytes 3932164
  584.3 8.3 copy-start
  596.0 78.5 %copy-start.26 = (bf16[4,80,2560]{2,1,0:T(8,128)(2,1)S(1)}, bf16[4,80,2560]{2,1,0:T(8,128)(2,1)}, u32[]{:S(2)}) copy-start(bf16[4,80,2560]{2,1,0:T(8,128)(2,1)} %get-tuple-element.90) | copy-start | bytes 4915204
  674.5 9.5 copy-start.13
  793.7 47.2 %copy-start.6 = (f32[256,1056]{1,0:T(8,128)S(1)}, f32[256,1056]{1,0:T(8,128)}, u32[]{:S(2)}) copy-start(f32[256,1056]{1,0:T(8,128)} %copy-done.5) | copy-start | bytes 3244036
  840.9 3.8 copy-start.12
  882.1 4.3 copy-start.51
  882.1 7.5 slice-start
  883.9 5.7 slice-start.1
  958.9 5.7 copy-start.24
  993.2 4.0 copy-start.38
  993.2 4.0 copy-start.39
  993.2 5.0 copy-start.42
  993.3 5.0 copy-start.43
  993.3 6.4 copy-start.44
  993.3 6.4 copy-start.41
  993.3 7.3 copy-start.37
  995.8 4.8 copy-start.30
  995.8 4.8 copy-start.31
  996.0 3.8 copy-start.34
  996.0 3.8 copy-start.40
  996.0 6.5 copy-start.17
  998.3 4.2 copy-start.16
  1000.6 3.4 copy-start.9
  (22 other events, 54.0 us)

commit v4 on v3

--- a/solution.py
+++ b/solution.py
@@ -548,7 +548,7 @@
     def _():
         keep.start()
 
-    yield begin + 9.0 * math.prod(shard_ref.shape) / LINK
+    yield begin + 16.0 * math.prod(shard_ref.shape) / LINK
 
     @pl.when(board.i != board.z)
     def _():
@@ -631,7 +631,7 @@
 
     def read(self, outs):
         z = line_index()
-        got = outs[0].astype(jnp.float32)
+        got = [outs[0][k].astype(jnp.float32) for k in range(3)]
         middle = (z == 1) | (z == 2)
         own = take(self.given, z).astype(jnp.float32)
         return own + got[0] + got[1] + jnp.where(middle, got[2], 0.0)
@@ -773,7 +773,8 @@
 
     def steps(self, *where):
         yield self.when
-        yield from self.task.steps(*where)
+        for when in self.task.steps(*where):
+            yield self.when + when
 
 
 class Together:
@@ -806,7 +807,10 @@
 
         def product(row):
             if self.columns:
-                return left_transposed(left[:, row : row + self.m], right[...])
+                spot = row // self.m
+                tensor = board.t if spot % 2 == 0 else 1 - board.t
+                place = board.place_xor(spot // 4 + spot // 2 % 2 * 2) * 2 + tensor
+                return left_transposed(left[place], right[...])
             return column_dot(left[row : row + self.m, :], right[...])
 
         return octet_pieces(board, self.m, self.piece_time, product)
@@ -828,8 +832,10 @@
         width = columns // (PLANE * self.line)
         step_rows = 16 if rows % 16 == 0 else rows
 
-        def run(source, target):
-            @pl.loop(0, rows // step_rows)
+        count = rows // step_rows
+
+        def run(source, target, first, last):
+            @pl.loop(first, last)
             def _(step):
                 here = pl.ds(pl.multiple_of(step * step_rows, step_rows), step_rows)
                 values = source[here, :]
@@ -843,7 +849,10 @@
                     ).astype(target.dtype)
 
         return [
-            (1.0 + 6.0 * n, functools.partial(run, givens[n], outs[n])) for n in range(2)
+            (16.5, functools.partial(run, givens[0], outs[0], 0, count // 2)),
+            (20.0, functools.partial(run, givens[0], outs[0], count // 2, count)),
+            (26.0, functools.partial(run, givens[1], outs[1], 0, count // 2)),
+            (36.0, functools.partial(run, givens[1], outs[1], count // 2, count)),
         ]
 
 
@@ -872,8 +881,14 @@
     more_givens = compute.givens if compute else []
     more_outs = compute.outs if compute else []
     more_scratch = compute.scratch if compute else []
-    more_given_specs = compute.given_specs if compute else []
-    more_out_specs = compute.out_specs if compute else []
+    given_staged = [spec is VMEM_SPEC for spec in compute.given_specs] if compute else []
+    out_staged = [spec is VMEM_SPEC for spec in compute.out_specs] if compute else []
+    staging = [
+        pltpu.VMEM(array.shape, array.dtype)
+        for arrays, staged in ((more_givens, given_staged), (more_outs, out_staged))
+        for array, flag in zip(arrays, staged)
+        if flag
+    ]
 
     def kernel(*refs):
         refs = list(refs)
@@ -887,6 +902,26 @@
         compute_givens = first(len(more_givens))
         outs, compute_outs = first(sum(n_outs)), first(len(more_outs))
         scratch, compute_scratch = first(sum(n_scratch)), first(len(more_scratch))
+        staged, loads, stores = first(len(staging)), [], []
+        if staging:
+            stage_sems = first(1)[0]
+        copies = 0
+        for n, flag in enumerate(given_staged):
+            if flag:
+                held = staged[copies]
+                loads.append(
+                    pltpu.make_async_copy(compute_givens[n], held, stage_sems.at[copies])
+                )
+                compute_givens[n] = held
+                copies += 1
+        for n, flag in enumerate(out_staged):
+            if flag:
+                held = staged[copies]
+                stores.append(
+                    pltpu.make_async_copy(held, compute_outs[n], stage_sems.at[copies])
+                )
+                compute_outs[n] = held
+                copies += 1
         running, closing = [], []
         if tasks:
             board = Board(*refs)
@@ -901,6 +936,8 @@
             )
             running.append((next(steps), n, steps))
         phases = []
+        for load in loads:
+            load.start()
         if compute:
             phases = compute.phases(
                 compute_givens,
@@ -913,7 +950,12 @@
         while running or phases:
             running.sort(key=lambda item: item[:2])
             if phases and not (running and running[0][0] <= phases[0][0]):
+                while loads:
+                    loads.pop(0).wait()
                 phases.pop(0)[1]()
+                if not phases:
+                    for store in stores:
+                        store.start()
                 continue
             when, n, steps = running.pop(0)
             when = next(steps, None)
@@ -921,6 +963,8 @@
                 running.append((when, n, steps))
         for close in closing:
             close()
+        for store in stores:
+            store.wait()
 
     sems = []
     if tasks:
@@ -932,11 +976,13 @@
     outs = pl.pallas_call(
         kernel,
         out_shape=[shape for task in tasks for shape, _ in task.outs] + more_outs,
-        in_specs=[HBM_SPEC] * len(inputs) + more_given_specs,
+        in_specs=[HBM_SPEC] * (len(inputs) + len(more_givens)),
         out_specs=[spec for task in tasks for _, spec in task.outs]
-        + more_out_specs,
+        + [HBM_SPEC] * len(more_outs),
         scratch_shapes=[shape for task in tasks for shape in task.scratch]
         + more_scratch
+        + staging
+        + ([pltpu.SemaphoreType.DMA((len(staging),))] if staging else [])
         + sems,
         compiler_params=pltpu.CompilerParams(
             collective_id=collective_id,
@@ -1394,47 +1440,41 @@
         ]
 
 
-class UnitUpdate:
-    def __init__(self, parts, weight, first_moment, second_moment, line):
-        self.givens = [parts, weight, first_moment, second_moment]
-        self.given_specs, self.out_specs = [VMEM_SPEC] * 4, [VMEM_SPEC] * 3
-        self.outs = [jax.ShapeDtypeStruct(weight.shape, jnp.float32)] * 3
+class UnitGradient:
+    def __init__(self, parts, line, when):
+        self.givens = [parts]
+        self.given_specs, self.out_specs = [VMEM_SPEC], [VMEM_SPEC]
+        self.outs = [
+            jax.ShapeDtypeStruct((parts.shape[1], PLANE * parts.shape[2]), jnp.bfloat16)
+        ]
         self.scratch = []
-        self.line = line
+        self.line, self.when = line, when
 
     def phases(self, givens, outs, scratch, board, task_givens, task_outs):
-        parts, weight, first_moment, second_moment = givens
-        rows, columns = weight.shape
+        parts, target = givens[0], outs[0]
+        rows, columns = target.shape
         width = columns // (PLANE * self.line)
         step_rows = 16 if rows % 16 == 0 else rows
-
-        def run(half):
-            count = rows // step_rows
-            split = (0, count // 2, count)
-
-            @pl.loop(split[half], split[half + 1])
+        count = rows // step_rows
+
+        def run(first, last):
+            @pl.loop(first, last)
             def _(step):
                 here = pl.ds(pl.multiple_of(step * step_rows, step_rows), step_rows)
                 pieces = [parts[i, here, :].astype(jnp.float32) for i in range(PLANE)]
-                gradient = jnp.concatenate(
+                target[here, :] = jnp.concatenate(
                     [
                         pieces[i][:, z * width : (z + 1) * width]
                         for z in range(self.line)
                         for i in range(PLANE)
                     ],
                     axis=1,
-                )
-                results = adamw_update(
-                    weight[here, :],
-                    first_moment[here, :],
-                    second_moment[here, :],
-                    gradient,
-                    matrix_rate(D),
-                )
-                for out, result in zip(outs, results):
-                    out[here, :] = result
-
-        return [(12.5, functools.partial(run, 0)), (18.5, functools.partial(run, 1))]
+                ).astype(target.dtype)
+
+        return [
+            (self.when, functools.partial(run, 0, count // 2)),
+            (self.when + 6.0, functools.partial(run, count // 2, count)),
+        ]
 
 
 def positions(segment_ids):
@@ -1525,18 +1565,19 @@
     )
     query_up_all = query_up_all.reshape(QR, local_heads * HEAD)
     latent_up_all = latent_up_all.reshape(KVR, local_heads * KH)
-    down_octet = pack_all.reshape(2, 2, tensor, line, pack_height, QR + KVR + DR)
-    down_blocks = jnp.zeros((PLANE, tensor, line, pack_height, QR + KVR + DR), low)
-    for k in range(PLANE):
-        for y in range(tensor):
-            down_blocks = lax.dynamic_update_slice(
-                down_blocks,
-                down_octet[k % 2, k // 2, y][None, None],
-                (i ^ k, (t + y) % tensor, 0, 0, 0),
-            )
-    down_blocks = down_blocks.transpose(2, 0, 1, 3, 4)
-    down_both = down_blocks[..., :down_rows, :].reshape(D, QR + KVR + DR)
-    gain_values = down_blocks[..., down_rows, :gain_width].reshape(-1).astype(jnp.float32)
+    pack_lines = pack_all.reshape(2 * 2 * tensor * line, pack_height, QR + KVR + DR)
+    found = [
+        take(
+            pack_lines,
+            ((((i ^ place) % 2) * 2 + (i ^ place) // 2) * tensor + (t + side) % tensor) * line + zz,
+        )
+        for zz in range(line)
+        for place in range(PLANE)
+        for side in range(tensor)
+    ]
+    down_both = jnp.concatenate([block[:down_rows] for block in found], axis=0)
+    gain_values = jnp.concatenate([block[down_rows, :gain_width] for block in found], axis=0)
+    gain_values = gain_values.astype(jnp.float32)
     gain_attention = gain_values[:D]
     gain_query = gain_values[D : D + QR]
     gain_latent = gain_values[D + QR : D + QR + KVR]
@@ -1568,7 +1609,7 @@
         axis=1,
     )
     tokens_all, output_all, gate_plane = communicate(
-        3, OctetGather(tokens_own), LineGather(output_moved), PlaneExchange(gate_blocks)
+        3, OctetGather(tokens_own), LineGather(output_moved), Later(PlaneExchange(gate_blocks), 14.0)
     )
     output_all = jnp.pad(
         output_all.reshape(local_heads * DV, D), ((0, mixed_width - local_heads * DV), (0, 0))
@@ -1590,7 +1631,7 @@
     grad_ffn, up_plane, gate_all, (queries, latent_heads, mixed_heads, log_totals) = communicate(
         2,
         OctetGather((RESIDUAL * cotangent.astype(jnp.float32)).astype(low)),
-        PlaneExchange(up_blocks),
+        Later(PlaneExchange(up_blocks), 30.0),
         LineGather(gate_plane),
         compute=AttentionForward(
             tokens_all, keys, bounds, waves, query_up_all, latent_up_all, packs, local_heads
@@ -1671,7 +1712,7 @@
         8,
         OctetReduce(ffn_terms),
         LineReduce(up_grad.reshape(line, PLANE, -1, units)),
-        PlaneExchange(gate_sum.astype(low)),
+        Later(PlaneExchange(gate_sum.astype(low)), 30.0),
         compute=AttentionBackward(
             queries,
             latent_heads,
@@ -1690,12 +1731,12 @@
     block_output = (residual + RESIDUAL * ffn_sum).astype(low)
     query_up_grad = left_transposed(tokens_all[:, :QR], grad_query_heads).astype(low)
     latent_up_grad = left_transposed(tokens_all[:, QR : QR + KVR], grad_latent_heads).astype(low)
-    grad_units, output_sum, up_parts, gate_out = communicate(
+    grad_units, output_sum, up_parts, (gate_shard,) = communicate(
         9,
         OctetReduce(grad_unit_terms),
         LineReduce(output_grad),
-        PlaneExchange(up_sum.astype(low)),
-        compute=UnitUpdate(gate_parts, gate_proj, gate_proj_first, gate_proj_second, line),
+        Later(PlaneExchange(up_sum.astype(low)), 14.0),
+        compute=UnitGradient(gate_parts, line, 10.5),
     )
     grad_query_wide, gain_query_grad = norm_backward(
         query_latent, inverse_query, gain_query, grad_units[:, :QR]
@@ -1724,19 +1765,7 @@
     left_blocks = jnp.concatenate(
         [left_blocks, left_marks.reshape(shards, line, PLANE, tensor, pack_height)], axis=0
     ).transpose(2, 3, 0, 1, 4)
-    pack_left = jnp.concatenate(
-        [
-            lax.dynamic_slice(
-                left_blocks,
-                (i ^ (core + 2 * x), (t + y) % tensor, 0, 0, 0),
-                (1, 1) + left_blocks.shape[2:],
-            ).reshape(half_rows + shards, line * pack_height)
-            for core in range(2)
-            for x in range(2)
-            for y in range(tensor)
-        ],
-        axis=1,
-    )
+    left_blocks = left_blocks.reshape(PLANE * tensor, half_rows + shards, line * pack_height)
     pack_right = jnp.concatenate(
         [
             grad_both,
@@ -1748,16 +1777,25 @@
         axis=0,
     )
     pack_rows_all = line * pack_height
-    up_update = UnitUpdate(up_parts, up_proj, up_proj_first, up_proj_second, line)
+    up_order = UnitGradient(up_parts, line, 15.0)
     if line == LINE:
         pack_task = OctetReduceInside(pack_rows_all, QR + KVR + DR, 1.5)
         tail_compute = Together(
-            PieceProduct(pack_left, pack_right, pack_rows_all, 1.5, columns=True), up_update
+            PieceProduct(left_blocks, pack_right, pack_rows_all, 1.5, columns=True), up_order
         )
     else:
+        pack_left = jnp.concatenate(
+            [
+                take(left_blocks, (i ^ (core + 2 * x)) * tensor + (t + y) % tensor)
+                for core in range(2)
+                for x in range(2)
+                for y in range(tensor)
+            ],
+            axis=1,
+        )
         pack_task = OctetReduce(left_transposed(pack_left, pack_right).astype(low))
-        tail_compute = up_update
-    pack_octet, query_up_sum, latent_up_sum, output_shard, up_out = communicate(
+        tail_compute = up_order
+    pack_octet, query_up_sum, latent_up_sum, output_shard, up_found = communicate(
         10,
         pack_task,
         LineReduce(query_up_grad.reshape(line, PLANE, -1, local_heads * HEAD)),
@@ -1798,6 +1836,20 @@
     )
     output_out = adamw_update(
         output_proj, output_proj_first, output_proj_second, output_shard, matrix_rate(H * DV // 64)
+    )
+    gate_out = adamw_update(
+        gate_proj,
+        gate_proj_first,
+        gate_proj_second,
+        gate_shard.astype(jnp.float32),
+        matrix_rate(D),
+    )
+    up_out = adamw_update(
+        up_proj,
+        up_proj_first,
+        up_proj_second,
+        up_found[0].astype(jnp.float32),
+        matrix_rate(D),
     )
     down_out = adamw_update(
         down_proj, down_proj_first, down_proj_second, down_shard, matrix_rate(FF // 8)

time: 1030 us -> 1000 us (0.971)
  Pallas kernels: 784 us -> 750 us
    pallas_call x11, Pallas kernels: 784 us -> 750 us  [run_kernel(): pl.pallas_call(kernel, out_shape=[shape for task in tasks for shape, _ in...]
    unnamed x121 -> x139, local copies, waits for them, and re-layouts: 26.4 us -> 52.5 us
    dynamic_update_slice x8 -> x0, local copies, waits for them, and re-layouts: 17.5 us -> none  [local(): lax.dynamic_update_slice(down_blocks, down_octet[k % 2, k // 2, y][None,...]
    convert_element_type x8 -> x0, other arithmetic: 13.7 us -> none  [the longest x7 12.7 us: read(): got = outs[0].astype(jnp.float32)]
    sub x7 -> x9, other arithmetic: 15.8 us -> 28 us  [adamw_update(): weight - step_rate * (first_hat / (jnp.sqrt(second_hat) + ADAM_EPSILON) +...]
where the time goes in v4:
time: 1000 us; the launch traced here: 994 us
  Pallas kernels  750 us (75%)
  local copies, waits for them, and re-layouts  85.1 us (9%)
  other arithmetic  82.3 us (8%)
  matrix products  75 us (8%)
    pallas_call x11, Pallas kernels, run_kernel(): pl.pallas_call(kernel, out_shape=[shape for task in tasks for shape, _ in...  750 us
    unnamed x139, local copies, waits for them, and re-layouts  52.5 us
    dot_general x3, matrix products, right_transposed(): lax.dot_general(left_side, right_side, (((1,), (1,)), ((), ())), preferre...  39.4 us
    dot_general x4, matrix products, left_transposed(): lax.dot_general(left_side, right_side, (((0,), (0,)), ((), ())), preferre...  30.6 us
    sub x9, other arithmetic, adamw_update(): weight - step_rate * (first_hat / (jnp.sqrt(second_hat) + ADAM_EPSILON) +...  28 us

profile of v4, /device:TPU:0, one launch (start us, length us, event | category | flops | bytes accessed | tf_op | source)
XLA Modules:
  0.0 994.3 jit_solution(10827723184410424459)
XLA Ops:
  5.6 73.4 %shard_map.509 = (bf16[4,96,1056]{2,1,0:T(8,128)(2,1)}, bf16[32,96,1056]{2,1,0:T(8,128)(2,1)}, bf16[4,48,640]{2,1,0:T(8,128)(2,1)}, bf16[4,4,48,640]{3,2,1,0:T(8...) custom-call(bf16[96,1056]{1,0:T(8,128)(2,1)} %fusion.44.refs_0_, ...), custom_call_target="tpu_custom_call" | custom-call | bytes 268435456 | tf_op jit(solution)/shard_map/pallas_call | solution.py:976
  136.5 5.0 fusion.120
  145.4 43.1 %shard_map.510 = (bf16[2048,1152]{1,0:T(8,128)(2,1)}, bf16[4,80,2560]{2,1,0:T(8,128)(2,1)}, bf16[4,160,800]{2,1,0:T(8,128)(2,1)}) custom-call(bf16[256,1152]{1,0:T(8,128)(2,1)} %concatenate.53.refs_0_, bf16[80,2560]{1,0:T(8,128)(2,1)} %get-tuple-element.78.refs_1_, bf16[4,160,800]{2,1,0:T(8,128)(2,1)} %get-tuple-element.79.refs_2_), custom_call_target="tpu_custom_call" | custom-call | bytes 268435456 | tf_op jit(solution)/shard_map/pallas_call | solution.py:976
  191.2 3.7 multiply_sine_fusion
  195.1 3.9 pad_maximum_fusion
  202.3 115.2 %shard_map.511 = (bf16[2048,2560]{1,0:T(8,128)(2,1)}, bf16[4,160,800]{2,1,0:T(8,128)(2,1)}, bf16[4,4,160,800]{3,2,1,0:T(8,128)(2,1)}, bf16[2048,640]{1,0:T(8,128...) custom-call(bf16[256,2560]{1,0:T(8,128)(2,1)} %fusion.8.refs_0_, ...), custom_call_target="tpu_custom_call" | custom-call | bytes 268435456 | tf_op jit(solution)/shard_map/pallas_call | solution.py:976
  318.8 78.5 %shard_map.512 = (f32[256,2560]{1,0:T(8,128)}, bf16[4,4,160,800]{3,2,1,0:T(8,128)(2,1)}) custom-call(bf16[4,160,800]{2,1,0:T(8,128)(2,1)} %get-tuple-element.84.refs_0_, bf16[2048,384]{1,0:T(8,128)(2,1)} %get-tuple-element.85.refs_1_, bf16[384,2560]{1,0:T(8,128)(2,1)} %pad.27.refs_2_), custom_call_target="tpu_custom_call" | custom-call | bytes 268435456 | tf_op jit(solution)/shard_map/pallas_call | solution.py:976
  402.7 74.4 %shard_map.513 = (bf16[2048,2560]{1,0:T(8,128)(2,1)}, bf16[4,200,2560]{2,1,0:T(8,128)(2,1)}, f32[2048,800]{1,0:T(8,128)}, f32[2048,800]{1,0:T(8,128)}) custom-call(bf16[256,2560]{1,0:T(8,128)(2,1)} %multiply_convert_fusion.4.refs_0_, bf16[200,2560]{1,0:T(8,128)(2,1)} %convert_element_type.252.refs_1_, bf16[2560,800]{1,0:T(8,128)(2,1)} %bitcast.262, ...), custom_call_target="tpu_custom_call" | custom-call | bytes 268435456 | tf_op jit(solution)/shard_map/pallas_call | solution.py:976
  477.1 22.8 %multiply_convert_fusion = (bf16[2048,800]{1,0:T(8,128)(2,1)}, bf16[2048,800]{1,0:T(8,128)(2,1)}, bf16[2048,800]{1,0:T(8,128)(2,1)}) fusion(f32[2048,800]{1,0:T(8,128)} %get-tuple-element.90, f32[2048,800]{1,0:T(8,128)} %get-tuple-element.91, bf16[2048,2560]{1,0:T(8,128)(2,1)} %get-tuple-element.92, bf16[800,2560]{1,0:T(8,128)(2,1)} %bitcast.277), kind=kOutput, calls=%fused_computation | convolution fusion | flops 8413184000 | bytes 37519360 | tf_op jit(solution)/shard_map/dot_general | solution.py:36
  499.9 14.3 %convolution_convert_fusion = bf16[800,2560]{1,0:T(8,128)(2,1)} fusion(bf16[2048,800]{1,0:T(8,128)(2,1)} %get-tuple-element.165.refs_2_, bf16[2048,2560]{1,0:T(8,128)(2,1)} %get-tuple-element.92), kind=kOutput, calls=%fused_computation.5 | convolution fusion | flops 8390656000 | bytes 17858560 | tf_op jit(solution)/shard_map/dot_general | solution.py:42
  514.3 74.6 %shard_map.514 = (f32[256,2560]{1,0:T(8,128)}, bf16[3,200,2560]{2,1,0:T(8,128)(2,1)}, bf16[2560,800]{1,0:T(8,128)(2,1)}, bf16[2560,800]{1,0:T(8,128)(2,1)}) custom-call(bf16[4,200,2560]{2,1,0:T(8,128)(2,1)} %bitcast.272, bf16[2048,2560]{1,0:T(8,128)(2,1)} %get-tuple-element.93.refs_1_, bf16[2048,800]{1,0:T(8,128)(2,1)} %get-tuple-element.164.refs_2_, ...), custom_call_target="tpu_custom_call" | custom-call | bytes 268435456 | tf_op jit(solution)/shard_map/pallas_call | solution.py:976
  588.9 6.7 multiply_subtract_fusion
  599.0 78.2 %shard_map.515 = (bf16[2048,2560]{1,0:T(8,128)(2,1)}, bf16[3,4,160,800]{3,2,1,0:T(8,128)(2,1)}, bf16[2048,2560]{1,0:T(8,128)(2,1)}) custom-call(bf16[256,2560]{1,0:T(8,128)(2,1)} %multiply_convert_fusion.3.refs_0_, bf16[4,4,160,800]{3,2,1,0:T(8,128)(2,1)} %bitcast.270, bf16[2048,800]{1,0:T(8,128)(2,1)} %get-tuple-element.165.refs_2_, bf16[800,2560]{1,0:T(8,128)(2,1)} %bitcast.278), custom_call_target="tpu_custom_call" | custom-call | bytes 268435456 | tf_op jit(solution)/shard_map/pallas_call | solution.py:976
  677.3 9.5 convolution_convert_fusion.1.refs_6_
  686.7 2.9 fusion.29.refs_2_
  689.7 90.8 %shard_map.516 = (f32[256,2560]{1,0:T(8,128)}, bf16[3,4,160,800]{3,2,1,0:T(8,128)(2,1)}, bf16[4,160,800]{2,1,0:T(8,128)(2,1)}, bf16[2048,640]{1,0:T(8,128)(2,1)}...) custom-call(bf16[2048,2560]{1,0:T(8,128)(2,1)} %get-tuple-element.97.refs_0_, bf16[4,4,160,800]{3,2,1,0:T(8,128)(2,1)} %bitcast.268, ...), custom_call_target="tpu_custom_call" | custom-call | bytes 268435456 | tf_op jit(solution)/shard_map/pallas_call | solution.py:976
  780.5 4.1 fusion.30.refs_2_
  784.6 7.6 fusion.121
  793.5 38.3 %shard_map.517 = (f32[256,1152]{1,0:T(8,128)}, bf16[3,80,2560]{2,1,0:T(8,128)(2,1)}, bf16[4,160,800]{2,1,0:T(8,128)(2,1)}, bf16[160,3200]{1,0:T(8,128)(2,1)}) custom-call(bf16[2048,1152]{1,0:T(8,128)(2,1)} %get-tuple-element.105.refs_0_, bf16[4,80,2560]{2,1,0:T(8,128)(2,1)} %bitcast.266, bf16[4,160,800]{2,1,0:T(8,128)(2,1)} %fusion.30.refs_2_, ...), custom_call_target="tpu_custom_call" | custom-call | bytes 268435456 | tf_op jit(solution)/shard_map/pallas_call | solution.py:976
  838.3 7.1 fusion.15
  848.9 3.1 convolution_convert_fusion.2
  852.0 5.5 fusion.25
  860.4 3.1 fusion.18
  863.5 5.5 copy.149
  869.0 4.7 reshape.386.refs_3_
  873.6 59.8 %shard_map.518 = (f32[384,1056]{1,0:T(8,128)}, bf16[3,4,48,640]{3,2,1,0:T(8,128)(2,1)}, bf16[3,4,16,640]{3,2,1,0:T(8,128)(2,1)}, bf16[80,2560]{1,0:T(8,128)(2,1)}, bf16[160,3200]{1,0:T(8,128)(2,1)}) custom-call(bf16[4,4,48,640]{3,2,1,0:T(8,128)(2,1)} %bitcast.284, bf16[4,4,16,640]{3,2,1,0:T(8,128)(2,1)} %bitcast.290, bf16[80,2560]{1,0:T(8,128)(2,1)} %fusion.37.refs_2_, ...), custom_call_target="tpu_custom_call" | custom-call | bytes 268435456 | tf_op jit(solution)/shard_map/pallas_call | solution.py:976
  933.5 5.7 multiply_subtract_fusion.1
  943.6 23.5 %shard_map.519 = (bf16[3,96,1056]{2,1,0:T(8,128)(2,1)}, bf16[4,48,640]{2,1,0:T(8,128)(2,1)}, bf16[4,16,640]{2,1,0:T(8,128)(2,1)}) custom-call(bf16[4,96,1056]{2,1,0:T(8,128)(2,1)} %bitcast.275, bf16[4,48,640]{2,1,0:T(8,128)(2,1)} %fusion.43.refs_1_, bf16[4,16,640]{2,1,0:T(8,128)(2,1)} %fusion.95.refs_2_), custom_call_target="tpu_custom_call" | custom-call | bytes 268435456 | tf_op jit(solution)/shard_map/pallas_call | solution.py:976
  972.7 2.5 multiply_subtract_fusion.4
  983.3 3.0 multiply_subtract_fusion.3
  986.4 2.9 fusion.14
  990.3 3.7 multiply_subtract_fusion.2
  (255 shorter events, 114.9 us)
Async XLA Ops:
  0.8 4.1 copy-start.33
  136.1 702.3 %copy-start.43 = (f32[256]{0:T(256)}, f32[256]{0:T(256)S(1)}, u32[]{:S(2)}) copy-start(f32[256]{0:T(256)S(1)} %add_rsqrt_fusion.3) | copy-start | bytes 3076
  136.4 5.0 copy-start.13
  141.5 47.0 %copy-start.5 = (f32[256,1056]{1,0:T(8,128)}, f32[256,1056]{1,0:T(8,128)S(1)}, u32[]{:S(2)}) copy-start(f32[256,1056]{1,0:T(8,128)S(1)} %fusion.120) | copy-start | bytes 3244036
  202.3 115.2 %copy-start.24 = (bf16[4,80,2560]{2,1,0:T(8,128)(2,1)S(1)}, bf16[4,80,2560]{2,1,0:T(8,128)(2,1)}, u32[]{:S(2)}) copy-start(bf16[4,80,2560]{2,1,0:T(8,128)(2,1)} %get-tuple-element.86) | copy-start | bytes 4915204
  318.8 78.5 %copy-start.3 = (bf16[256,2560]{1,0:T(8,128)(2,1)S(1)}, bf16[256,2560]{1,0:T(8,128)(2,1)}, u32[]{:S(2)}) copy-start(bf16[256,2560]{1,0:T(8,128)(2,1)} %param.30) | copy-start | bytes 3932164
  399.6 196.8 %copy-start.40 = (f32[256]{0:T(256)}, f32[256]{0:T(256)S(1)}, u32[]{:S(2)}) copy-start(f32[256]{0:T(256)S(1)} %add_rsqrt_fusion) | copy-start | bytes 3076
  588.9 6.8 copy-start
  599.0 78.3 %copy-start.25 = (bf16[4,80,2560]{2,1,0:T(8,128)(2,1)S(1)}, bf16[4,80,2560]{2,1,0:T(8,128)(2,1)}, u32[]{:S(2)}) copy-start(bf16[4,80,2560]{2,1,0:T(8,128)(2,1)} %get-tuple-element.86) | copy-start | bytes 4915204
  677.3 9.5 copy-start.15
  780.5 4.1 copy-start.26
  793.5 38.4 %copy-start.6 = (f32[256,1056]{1,0:T(8,128)S(1)}, f32[256,1056]{1,0:T(8,128)}, u32[]{:S(2)}) copy-start(f32[256,1056]{1,0:T(8,128)} %copy-done.5) | copy-start | bytes 3244036
  831.8 3.8 copy-start.14
  873.6 59.9 %copy-start.11 = (f32[160,3200]{1,0:T(8,128)S(1)}, f32[160,3200]{1,0:T(8,128)}, u32[]{:S(2)}) copy-start(f32[160,3200]{1,0:T(8,128)} %refs_5_.1) | copy-start | bytes 6144004
  873.6 59.9 %copy-start.20 = (f32[160,3200]{1,0:T(8,128)S(1)}, f32[160,3200]{1,0:T(8,128)}, u32[]{:S(2)}) copy-start(f32[160,3200]{1,0:T(8,128)} %param.55) | copy-start | bytes 6144004
  933.5 5.7 copy-start.37
  933.5 7.3 copy-start.32
  933.5 9.1 copy-start.23
  972.3 8.6 copy-start.38
  972.7 4.1 copy-start.29
  972.7 6.2 copy-start.39
  972.7 6.2 copy-start.34
  972.7 13.6 %copy-start.19 = (f32[256,2560]{1,0:T(8,128)S(1)}, f32[256,2560]{1,0:T(8,128)}, u32[]{:S(2)}) copy-start(f32[256,2560]{1,0:T(8,128)} %get-tuple-element.218) | copy-start | bytes 7864324
  975.2 5.7 copy-start.36
  975.2 7.4 copy-start.48
  975.2 7.4 copy-start.49
  975.2 7.4 copy-start.50
  975.2 8.0 copy-start.17
  975.2 7.9 copy-start.30
  975.2 7.9 copy-start.31
  978.8 7.5 copy-start.18
  986.4 4.0 copy-start.27
  (22 other events, 61.3 us)
